TPU v7x, 256 devices: a whole 4x4x8 slice. The times are simulated.
256 devices in a mesh: tm: 64 (over y, z, x_hi), fsdp: 4 (over x_lo, core).
Axes of the slice: x: 4 (x_hi: 2, x_lo: 2; x = x_hi * 2 + x_lo), y: 4, z: 8, core: 2. Of those that a mesh axis runs over, the one named last changes fastest.
Arguments:
- frames_in: bfloat16 [8, 8192, 1536], P('fsdp', 'tm'), may hold values from -24 to 24
- lengths: int32 [8], replicated, may hold values from 2048 to 8192, as said below
- depth_kernel: float32 [32, 1536], replicated, may hold values from -1 to 1
- norm_gain: float32 [1536], replicated, may hold values from 0.1 to 1.9
- norm_bias: float32 [1536], replicated, may hold values from -3 to 3
- out_weight: bfloat16 [1536, 1536], P(None, 'fsdp'), may hold values from -0.15625 to 0.15625
- cotangent: bfloat16 [8, 8192, 1536], P('fsdp', 'tm'), may hold values from -16 to 16
Outputs:
- mixed: bfloat16 [8, 8192, 1536], P('fsdp', 'tm')
- frames_grad: bfloat16 [8, 8192, 1536], P('fsdp', 'tm')
- weight_grad: float32 [1536, 1536], P(None, 'fsdp')
- kernel_grad: float32 [32, 1536], replicated
- gain_grad: float32 [1536], replicated
- bias_grad: float32 [1536], replicated
Inputs may be any that keep to these rules, and one draw needn't show every extreme that they name: `lengths`: one utterance has exactly 8192 valid frames.
All inputs are finite; a program needn't handle non-finite values.
Results may differ from a plain program's by a relative error of at most 0.005.
Values may be sent and summed in bfloat16 or wider, within the bound.
No kernel may reach another device: no remote copies, remote signals or barrier semaphores. Data moves between devices by JAX's collectives and lax.ppermute only.
A program may use at most 128 MiB of HBM per device.

v0:
```python
import jax
import jax.numpy as jnp
from jax import lax
from jax.sharding import PartitionSpec as P

epsilon = 1e-05


def shifted(value, axis, steps):
    count = lax.axis_size(axis)
    leading, last = (max(0, -steps), min(count, count - steps))
    return lax.ppermute(value, axis, [(source, source + steps) for source in range(leading, last)])


def on_device(frames_in, lengths, depth_kernel, norm_gain, norm_bias, out_weight, cotangent):
    local_utts = frames_in.shape[0]
    own_rows = frames_in.shape[1]
    channels = frames_in.shape[2]
    halo_rows = depth_kernel.shape[0] - 1
    first_utt = lax.axis_index("fsdp") * local_utts
    own_lengths = lax.dynamic_slice_in_dim(lengths, first_utt, local_utts, 0)
    positions = lax.axis_index("tm") * own_rows + jnp.arange(own_rows, dtype=jnp.int32)
    valid_rows = (positions[None, :] < own_lengths[:, None]).astype(jnp.float32)[:, :, None]
    frames_valid = jnp.sum(lengths).astype(jnp.float32)
    masked = frames_in * valid_rows.astype(jnp.bfloat16)
    before = shifted(masked[:, own_rows - halo_rows :, :], "tm", 1)
    padded = jnp.concatenate([before, masked], 1)
    convolved = jnp.zeros(frames_in.shape, jnp.float32)
    for tap_index in range(halo_rows + 1):
        convolved = (
            convolved + depth_kernel[tap_index] * padded[:, tap_index : tap_index + own_rows, :]
        )
    channel_sum = lax.psum(jnp.sum(convolved * valid_rows, axis=(0, 1)), ("tm", "fsdp"))
    average = channel_sum / frames_valid
    centred = convolved - average
    square_sum = lax.psum(jnp.sum(centred * centred * valid_rows, axis=(0, 1)), ("tm", "fsdp"))
    variance = square_sum / frames_valid
    inv_spread = lax.rsqrt(variance + epsilon)
    normed = centred * inv_spread
    preact = normed * norm_gain + norm_bias
    active = jax.nn.silu(preact).astype(jnp.bfloat16)
    all_rows = local_utts * own_rows
    flat_active = active.reshape(all_rows, channels)
    flat_valid = valid_rows.reshape(all_rows, 1)
    masked_grad = (cotangent * valid_rows.astype(jnp.bfloat16)).reshape(all_rows, channels)
    whole_weight = lax.all_gather(out_weight, "fsdp", axis=1, tiled=True)
    projected = jnp.dot(flat_active, whole_weight, preferred_element_type=jnp.float32)
    act_grad = lax.dot_general(
        masked_grad, whole_weight, (((1,), (1,)), ((), ())), preferred_element_type=jnp.float32
    )
    mixed = (projected * flat_valid).astype(jnp.bfloat16).reshape(frames_in.shape)
    weight_term = lax.dot_general(
        flat_active, masked_grad, (((0,), (0,)), ((), ())), preferred_element_type=jnp.float32
    )
    tm_count = lax.axis_size("tm")
    fsdp_count = lax.axis_size("fsdp")
    block_cols = channels // (tm_count * fsdp_count)
    reordered = (
        weight_term.reshape(channels, fsdp_count, tm_count, block_cols)
        .transpose(0, 2, 1, 3)
        .reshape(channels, channels)
    )
    own_share = lax.psum_scatter(reordered, ("tm", "fsdp"), scatter_dimension=1, tiled=True)
    weight_grad = lax.all_gather(own_share, "tm", axis=1, tiled=True)
    sigmoid_pre = jax.nn.sigmoid(preact)
    pre_grad = (
        act_grad.reshape(frames_in.shape) * sigmoid_pre * (1.0 + preact * (1.0 - sigmoid_pre))
    )
    bias_grad, gain_grad = lax.psum(
        (
            jnp.sum(pre_grad * valid_rows, axis=(0, 1)),
            jnp.sum(pre_grad * normed * valid_rows, axis=(0, 1)),
        ),
        ("tm", "fsdp"),
    )
    conv_grad = (
        valid_rows
        * norm_gain
        * inv_spread
        * (pre_grad - bias_grad / frames_valid - normed * gain_grad / frames_valid)
    )
    after = shifted(conv_grad[:, :halo_rows, :].astype(jnp.bfloat16), "tm", -1).astype(jnp.float32)
    extended = jnp.concatenate([conv_grad, after], 1)
    backed = jnp.zeros(frames_in.shape, jnp.float32)
    for tap_index in range(halo_rows + 1):
        backed = (
            backed
            + depth_kernel[tap_index]
            * extended[:, halo_rows - tap_index : halo_rows - tap_index + own_rows, :]
        )
    frames_grad = (backed * valid_rows).astype(jnp.bfloat16)
    kernel_part = jnp.stack(
        [
            jnp.sum(padded[:, tap_index : tap_index + own_rows, :] * conv_grad, axis=(0, 1))
            for tap_index in range(halo_rows + 1)
        ]
    )
    kernel_grad = lax.psum(kernel_part, ("tm", "fsdp"))
    return (mixed, frames_grad, weight_grad, kernel_grad, gain_grad, bias_grad)


def solution(mesh):
    in_specs = (P("fsdp", "tm", None), P(), P(), P(), P(), P(None, "fsdp"), P("fsdp", "tm", None))
    out_specs = (P("fsdp", "tm", None), P("fsdp", "tm", None), P(None, "fsdp"), P(), P(), P())
    return jax.shard_map(
        on_device, mesh=mesh, in_specs=in_specs, out_specs=out_specs, check_vma=False
    )
```

profile of v0, /device:TPU:8, one launch (start us, length us, event | category | flops | bytes accessed | tf_op | source)
XLA Modules:
  0.0 1891.2 jit_solution(16103337805509789334)
XLA Ops:
  34.4 73.4 %psum.35 = f32[1536]{0:T(1024)S(1)} all-reduce(f32[1536]{0:T(1024)} %get-tuple-element.87), channel_id=1, replica_groups=mesh['tm'=64,'fsdp'=4] {'tm','fsdp'}, use_global_device_ids=true, to_apply=%region_1.0 | all-reduce | flops 1536 | bytes 12288 | tf_op jit(solution)/shard_map/psum | solution.py:33
  108.8 74.6 %psum.36 = f32[1536]{0:T(1024)S(1)} all-reduce(f32[1536]{0:T(1024)S(1)} %multiply_reduce_fusion.2), channel_id=1, replica_groups=mesh['tm'=64,'fsdp'=4] {'tm','fsdp'}, use_global_device_ids=true, to_apply=%region_4.0 | all-reduce | flops 1536 | bytes 12288 | tf_op jit(solution)/shard_map/psum | solution.py:36
  213.9 632.3 %fusion = f32[1536,8]{0,1:T(8,128)S(1)} fusion(f32[1536,1536]{0,1:T(8,128)} %reshape.147), kind=kCustom, calls=%all-reduce-scatter | all-reduce-scatter fusion | flops 3145729 | bytes 9486336
  850.1 65.6 %collective-permute-start.62 = (f32[1536,8]{0,1:T(8,128)S(1)}, f32[1536,8]{0,1:T(8,128)S(1)}, u32[]{:S(2)}, u32[]{:S(2)}) collective-permute-start(f32[1536,8]{0,1:T(8,128)S(1)} %fusion), channel_id=1, source_target_pairs={{0,61},{1,62},{2,63},{3,64},{4,65},{5,66},{6,67},{7,68},{8,69},{9,... | collective-permute-start | bytes 147464
  1005.7 16.8 collective-permute-start.34
  1036.6 13.1 collective-permute-start.30
  1049.8 13.1 collective-permute-start.29
  1062.9 13.1 collective-permute-start.28
  1076.1 13.1 collective-permute-start.27
  1089.2 13.1 collective-permute-start.26
  1102.3 13.1 collective-permute-start.25
  1115.5 13.1 collective-permute-start.24
  1128.6 13.1 collective-permute-start.23
  1141.8 13.1 collective-permute-start.22
  1154.9 13.1 collective-permute-start.21
  1168.0 13.1 collective-permute-start.20
  1181.2 13.1 collective-permute-start.19
  1194.3 13.1 collective-permute-start.18
  1207.5 13.1 collective-permute-start.17
  1220.6 13.1 collective-permute-start.16
  1233.7 13.1 collective-permute-start.15
  1246.9 13.1 collective-permute-start.14
  1260.0 13.1 collective-permute-start.13
  1273.2 13.1 collective-permute-start.12
  1286.3 13.1 collective-permute-start.11
  1299.4 13.1 collective-permute-start.10
  1352.0 13.1 collective-permute-start.6
  1381.7 13.1 collective-permute-start.3
  1394.9 13.1 collective-permute-start.2
  1416.2 96.9 %concatenate.8 = f32[1536,518]{0,1:T(8,128)} concatenate(f32[1536,6]{0,1:T(8,128)S(1)} %collective-permute-done.65, f32[1536,8]{0,1:T(8,128)S(1)} %collective-permute-done.64, f32[1536,8]{0,1:T(8,128)S(1)} %collective-permute-done.63, f32[1536,8]{0,1:T(8,128)S(1)} %collective-permute-done.62, f32[1536,8]{0,1:T(8,128)S(1)} %collective-permute-done.61, ...), dimensions={1} | concatenate | bytes 6365184
  1514.7 72.5 %all-reduce.2 = (f32[1536]{0:T(1024)S(1)}, f32[1536]{0:T(1024)S(1)}) all-reduce(f32[1536]{0:T(1024)} %get-tuple-element.51, f32[1536]{0:T(1024)S(1)} %get-tuple-element.50), channel_id=1, replica_groups=mesh['tm'=64,'fsdp'=4] {'tm','fsdp'}, use_global_device_ids=true, to_apply=%region_8.9 | all-reduce | flops 3072 | bytes 24576 | tf_op jit(solution)/shard_map/psum | solution.py:69
  1639.1 244.0 %all-reduce.5.cloned.1.call-done = f32[32,1536]{1,0:T(8,128)} async-done(((f32[32,1536]{1,0:T(8,128)}), f32[32,1536]{1,0:T(8,128)}) %all-reduce.5.cloned.1.call-update) | async-done | bytes 196624 | tf_op jit(solution)/shard_map/psum | solution.py:98
  (347 shorter events, 283.3 us)
Async XLA Ops:
  7.2 176.2 %all-gather.4.cloned.1.call-start = ((), (), s32[]{:S(2)}) async-start(), calls=%async_computation | async-start | bytes 5898240 | tf_op jit(solution)/shard_map/all_gather | solution.py:46
  7.9 1626.6 %all-gather.6.cloned.1.call-start = ((), (), s32[]{:S(2)}) async-start(), calls=%async_computation.2 | async-start | bytes 3194880 | tf_op jit(solution)/shard_map/all_gather | solution.py:64
  846.2 88.3 %collective-permute-start.64 = (f32[1536,8]{0,1:T(8,128)S(1)}, f32[1536,8]{0,1:T(8,128)S(1)}, u32[]{:S(2)}, u32[]{:S(2)}) collective-permute-start(f32[1536,8]{0,1:T(8,128)S(1)} %fusion), channel_id=1, source_target_pairs={{0,63},{1,64},{2,65},{3,66},{4,67},{5,68},{6,69},{7,70},{8,71},{9,... | collective-permute-start | bytes 147464
  848.1 88.4 %collective-permute-start.63 = (f32[1536,8]{0,1:T(8,128)S(1)}, f32[1536,8]{0,1:T(8,128)S(1)}, u32[]{:S(2)}, u32[]{:S(2)}) collective-permute-start(f32[1536,8]{0,1:T(8,128)S(1)} %fusion), channel_id=1, source_target_pairs={{0,62},{1,63},{2,64},{3,65},{4,66},{5,67},{6,68},{7,69},{8,70},{9,... | collective-permute-start | bytes 147464
  850.1 88.4 %collective-permute-start.62 = (f32[1536,8]{0,1:T(8,128)S(1)}, f32[1536,8]{0,1:T(8,128)S(1)}, u32[]{:S(2)}, u32[]{:S(2)}) collective-permute-start(f32[1536,8]{0,1:T(8,128)S(1)} %fusion), channel_id=1, source_target_pairs={{0,61},{1,62},{2,63},{3,64},{4,65},{5,66},{6,67},{7,68},{8,69},{9,... | collective-permute-start | bytes 147464
  1026.4 62.8 %collective-permute-start.31 = (f32[1536,8]{0,1:T(8,128)S(1)}, f32[1536,8]{0,1:T(8,128)S(1)}, u32[]{:S(2)}, u32[]{:S(2)}) collective-permute-start(f32[1536,8]{0,1:T(8,128)S(1)} %fusion), channel_id=1, source_target_pairs={{0,30},{1,31},{2,32},{3,33},{4,34},{5,35},{6,36},{7,37},{8,38},{9,... | collective-permute-start | bytes 147464
  1036.6 65.7 %collective-permute-start.30 = (f32[1536,8]{0,1:T(8,128)S(1)}, f32[1536,8]{0,1:T(8,128)S(1)}, u32[]{:S(2)}, u32[]{:S(2)}) collective-permute-start(f32[1536,8]{0,1:T(8,128)S(1)} %fusion), channel_id=1, source_target_pairs={{0,29},{1,30},{2,31},{3,32},{4,33},{5,34},{6,35},{7,36},{8,37},{9,... | collective-permute-start | bytes 147464
  1049.8 65.7 %collective-permute-start.29 = (f32[1536,8]{0,1:T(8,128)S(1)}, f32[1536,8]{0,1:T(8,128)S(1)}, u32[]{:S(2)}, u32[]{:S(2)}) collective-permute-start(f32[1536,8]{0,1:T(8,128)S(1)} %fusion), channel_id=1, source_target_pairs={{0,28},{1,29},{2,30},{3,31},{4,32},{5,33},{6,34},{7,35},{8,36},{9,... | collective-permute-start | bytes 147464
  1062.9 65.7 %collective-permute-start.28 = (f32[1536,8]{0,1:T(8,128)S(1)}, f32[1536,8]{0,1:T(8,128)S(1)}, u32[]{:S(2)}, u32[]{:S(2)}) collective-permute-start(f32[1536,8]{0,1:T(8,128)S(1)} %fusion), channel_id=1, source_target_pairs={{0,27},{1,28},{2,29},{3,30},{4,31},{5,32},{6,33},{7,34},{8,35},{9,... | collective-permute-start | bytes 147464
  1076.1 65.7 %collective-permute-start.27 = (f32[1536,8]{0,1:T(8,128)S(1)}, f32[1536,8]{0,1:T(8,128)S(1)}, u32[]{:S(2)}, u32[]{:S(2)}) collective-permute-start(f32[1536,8]{0,1:T(8,128)S(1)} %fusion), channel_id=1, source_target_pairs={{0,26},{1,27},{2,28},{3,29},{4,30},{5,31},{6,32},{7,33},{8,34},{9,... | collective-permute-start | bytes 147464
  1089.2 65.7 %collective-permute-start.26 = (f32[1536,8]{0,1:T(8,128)S(1)}, f32[1536,8]{0,1:T(8,128)S(1)}, u32[]{:S(2)}, u32[]{:S(2)}) collective-permute-start(f32[1536,8]{0,1:T(8,128)S(1)} %fusion), channel_id=1, source_target_pairs={{0,25},{1,26},{2,27},{3,28},{4,29},{5,30},{6,31},{7,32},{8,33},{9,... | collective-permute-start | bytes 147464
  1102.3 65.7 %collective-permute-start.25 = (f32[1536,8]{0,1:T(8,128)S(1)}, f32[1536,8]{0,1:T(8,128)S(1)}, u32[]{:S(2)}, u32[]{:S(2)}) collective-permute-start(f32[1536,8]{0,1:T(8,128)S(1)} %fusion), channel_id=1, source_target_pairs={{0,24},{1,25},{2,26},{3,27},{4,28},{5,29},{6,30},{7,31},{8,32},{9,... | collective-permute-start | bytes 147464
  1115.5 65.7 %collective-permute-start.24 = (f32[1536,8]{0,1:T(8,128)S(1)}, f32[1536,8]{0,1:T(8,128)S(1)}, u32[]{:S(2)}, u32[]{:S(2)}) collective-permute-start(f32[1536,8]{0,1:T(8,128)S(1)} %fusion), channel_id=1, source_target_pairs={{0,23},{1,24},{2,25},{3,26},{4,27},{5,28},{6,29},{7,30},{8,31},{9,... | collective-permute-start | bytes 147464
  1128.6 65.7 %collective-permute-start.23 = (f32[1536,8]{0,1:T(8,128)S(1)}, f32[1536,8]{0,1:T(8,128)S(1)}, u32[]{:S(2)}, u32[]{:S(2)}) collective-permute-start(f32[1536,8]{0,1:T(8,128)S(1)} %fusion), channel_id=1, source_target_pairs={{0,22},{1,23},{2,24},{3,25},{4,26},{5,27},{6,28},{7,29},{8,30},{9,... | collective-permute-start | bytes 147464
  1141.8 65.7 %collective-permute-start.22 = (f32[1536,8]{0,1:T(8,128)S(1)}, f32[1536,8]{0,1:T(8,128)S(1)}, u32[]{:S(2)}, u32[]{:S(2)}) collective-permute-start(f32[1536,8]{0,1:T(8,128)S(1)} %fusion), channel_id=1, source_target_pairs={{0,21},{1,22},{2,23},{3,24},{4,25},{5,26},{6,27},{7,28},{8,29},{9,... | collective-permute-start | bytes 147464
  1154.9 65.7 %collective-permute-start.21 = (f32[1536,8]{0,1:T(8,128)S(1)}, f32[1536,8]{0,1:T(8,128)S(1)}, u32[]{:S(2)}, u32[]{:S(2)}) collective-permute-start(f32[1536,8]{0,1:T(8,128)S(1)} %fusion), channel_id=1, source_target_pairs={{0,20},{1,21},{2,22},{3,23},{4,24},{5,25},{6,26},{7,27},{8,28},{9,... | collective-permute-start | bytes 147464
  1168.0 65.7 %collective-permute-start.20 = (f32[1536,8]{0,1:T(8,128)S(1)}, f32[1536,8]{0,1:T(8,128)S(1)}, u32[]{:S(2)}, u32[]{:S(2)}) collective-permute-start(f32[1536,8]{0,1:T(8,128)S(1)} %fusion), channel_id=1, source_target_pairs={{0,19},{1,20},{2,21},{3,22},{4,23},{5,24},{6,25},{7,26},{8,27},{9,... | collective-permute-start | bytes 147464
  1181.2 65.7 %collective-permute-start.19 = (f32[1536,8]{0,1:T(8,128)S(1)}, f32[1536,8]{0,1:T(8,128)S(1)}, u32[]{:S(2)}, u32[]{:S(2)}) collective-permute-start(f32[1536,8]{0,1:T(8,128)S(1)} %fusion), channel_id=1, source_target_pairs={{0,18},{1,19},{2,20},{3,21},{4,22},{5,23},{6,24},{7,25},{8,26},{9,... | collective-permute-start | bytes 147464
  1194.3 65.7 %collective-permute-start.18 = (f32[1536,8]{0,1:T(8,128)S(1)}, f32[1536,8]{0,1:T(8,128)S(1)}, u32[]{:S(2)}, u32[]{:S(2)}) collective-permute-start(f32[1536,8]{0,1:T(8,128)S(1)} %fusion), channel_id=1, source_target_pairs={{0,17},{1,18},{2,19},{3,20},{4,21},{5,22},{6,23},{7,24},{8,25},{9,... | collective-permute-start | bytes 147464
  1207.5 65.7 %collective-permute-start.17 = (f32[1536,8]{0,1:T(8,128)S(1)}, f32[1536,8]{0,1:T(8,128)S(1)}, u32[]{:S(2)}, u32[]{:S(2)}) collective-permute-start(f32[1536,8]{0,1:T(8,128)S(1)} %fusion), channel_id=1, source_target_pairs={{0,16},{1,17},{2,18},{3,19},{4,20},{5,21},{6,22},{7,23},{8,24},{9,... | collective-permute-start | bytes 147464
  1220.6 65.7 %collective-permute-start.16 = (f32[1536,8]{0,1:T(8,128)S(1)}, f32[1536,8]{0,1:T(8,128)S(1)}, u32[]{:S(2)}, u32[]{:S(2)}) collective-permute-start(f32[1536,8]{0,1:T(8,128)S(1)} %fusion), channel_id=1, source_target_pairs={{0,15},{1,16},{2,17},{3,18},{4,19},{5,20},{6,21},{7,22},{8,23},{9,... | collective-permute-start | bytes 147464
  1233.7 65.7 %collective-permute-start.15 = (f32[1536,8]{0,1:T(8,128)S(1)}, f32[1536,8]{0,1:T(8,128)S(1)}, u32[]{:S(2)}, u32[]{:S(2)}) collective-permute-start(f32[1536,8]{0,1:T(8,128)S(1)} %fusion), channel_id=1, source_target_pairs={{0,14},{1,15},{2,16},{3,17},{4,18},{5,19},{6,20},{7,21},{8,22},{9,... | collective-permute-start | bytes 147464
  1246.9 65.7 %collective-permute-start.14 = (f32[1536,8]{0,1:T(8,128)S(1)}, f32[1536,8]{0,1:T(8,128)S(1)}, u32[]{:S(2)}, u32[]{:S(2)}) collective-permute-start(f32[1536,8]{0,1:T(8,128)S(1)} %fusion), channel_id=1, source_target_pairs={{0,13},{1,14},{2,15},{3,16},{4,17},{5,18},{6,19},{7,20},{8,21},{9,... | collective-permute-start | bytes 147464
  1260.0 65.7 %collective-permute-start.13 = (f32[1536,8]{0,1:T(8,128)S(1)}, f32[1536,8]{0,1:T(8,128)S(1)}, u32[]{:S(2)}, u32[]{:S(2)}) collective-permute-start(f32[1536,8]{0,1:T(8,128)S(1)} %fusion), channel_id=1, source_target_pairs={{0,12},{1,13},{2,14},{3,15},{4,16},{5,17},{6,18},{7,19},{8,20},{9,... | collective-permute-start | bytes 147464
  1273.2 65.7 %collective-permute-start.12 = (f32[1536,8]{0,1:T(8,128)S(1)}, f32[1536,8]{0,1:T(8,128)S(1)}, u32[]{:S(2)}, u32[]{:S(2)}) collective-permute-start(f32[1536,8]{0,1:T(8,128)S(1)} %fusion), channel_id=1, source_target_pairs={{0,11},{1,12},{2,13},{3,14},{4,15},{5,16},{6,17},{7,18},{8,19},{9,... | collective-permute-start | bytes 147464
  1286.3 65.7 %collective-permute-start.11 = (f32[1536,8]{0,1:T(8,128)S(1)}, f32[1536,8]{0,1:T(8,128)S(1)}, u32[]{:S(2)}, u32[]{:S(2)}) collective-permute-start(f32[1536,8]{0,1:T(8,128)S(1)} %fusion), channel_id=1, source_target_pairs={{0,10},{1,11},{2,12},{3,13},{4,14},{5,15},{6,16},{7,17},{8,18},{9,... | collective-permute-start | bytes 147464
  1299.4 65.7 %collective-permute-start.10 = (f32[1536,8]{0,1:T(8,128)S(1)}, f32[1536,8]{0,1:T(8,128)S(1)}, u32[]{:S(2)}, u32[]{:S(2)}) collective-permute-start(f32[1536,8]{0,1:T(8,128)S(1)} %fusion), channel_id=1, source_target_pairs={{0,9},{1,10},{2,11},{3,12},{4,13},{5,14},{6,15},{7,16},{8,17},{9,1... | collective-permute-start | bytes 147464
  1312.6 57.5 %collective-permute-start.9 = (f32[1536,8]{0,1:T(8,128)S(1)}, f32[1536,8]{0,1:T(8,128)S(1)}, u32[]{:S(2)}, u32[]{:S(2)}) collective-permute-start(f32[1536,8]{0,1:T(8,128)S(1)} %fusion), channel_id=1, source_target_pairs={{0,8},{1,9},{2,10},{3,11},{4,12},{5,13},{6,14},{7,15},{8,16},{9,17... | collective-permute-start | bytes 147464
  1325.7 55.9 %collective-permute-start.8 = (f32[1536,8]{0,1:T(8,128)S(1)}, f32[1536,8]{0,1:T(8,128)S(1)}, u32[]{:S(2)}, u32[]{:S(2)}) collective-permute-start(f32[1536,8]{0,1:T(8,128)S(1)} %fusion), channel_id=1, source_target_pairs={{0,7},{1,8},{2,9},{3,10},{4,11},{5,12},{6,13},{7,14},{8,15},{9,16}... | collective-permute-start | bytes 147464
  1338.9 55.9 %collective-permute-start.7 = (f32[1536,8]{0,1:T(8,128)S(1)}, f32[1536,8]{0,1:T(8,128)S(1)}, u32[]{:S(2)}, u32[]{:S(2)}) collective-permute-start(f32[1536,8]{0,1:T(8,128)S(1)} %fusion), channel_id=1, source_target_pairs={{0,6},{1,7},{2,8},{3,9},{4,10},{5,11},{6,12},{7,13},{8,14},{9,15},... | collective-permute-start | bytes 147464
  1352.0 56.1 %collective-permute-start.6 = (f32[1536,8]{0,1:T(8,128)S(1)}, f32[1536,8]{0,1:T(8,128)}, u32[]{:S(2)}, u32[]{:S(2)}) collective-permute-start(f32[1536,8]{0,1:T(8,128)S(1)} %fusion), channel_id=1, source_target_pairs={{0,5},{1,6},{2,7},{3,8},{4,9},{5,10},{6,11},{7,12},{8,13},{9,14},{... | collective-permute-start | bytes 147464
  1514.6 368.4 %all-reduce.5.cloned.1.call-start = ((), (), s32[]{:S(2)}) async-start(), calls=%async_computation.1 | async-start | bytes 393216 | tf_op jit(solution)/shard_map/psum | solution.py:98
  (121 other events, 3805.6 us)
Sparse Core Ops, SparseCore 0:
  9.8 56.3 all-gather.3
  1514.7 119.6 all-gather.5
  1640.6 242.4 all-reduce.4
where the time goes:
time: 1900 us; the launch traced here: 1890 us
  blocking collectives  853 us (45%)
  starting transfers between devices  568 us (30%)
  waiting for transfers between devices  265 us (14%)
  local copies, waits for them, and re-layouts  145 us (8%)
  other arithmetic  30.5 us (2%)
    unnamed x1, blocking collectives  632 us
    unnamed x64, starting transfers between devices  555 us
    psum x1, waiting for transfers between devices, on_device(): kernel_grad = lax.psum(kernel_part, ('tm', 'fsdp'))  244 us
    unnamed x174, local copies, waits for them, and re-layouts  106 us
    psum x1, blocking collectives, on_device(): lax.psum(jnp.sum(centred * centred * valid_rows, axis=(0, 1)), ('tm', 'fs...  74.6 us
    psum x1, blocking collectives, on_device(): lax.psum(jnp.sum(convolved * valid_rows, axis=(0, 1)), ('tm', 'fsdp'))  73.4 us
    psum x1, blocking collectives, on_device(): lax.psum((jnp.sum(pre_grad * valid_rows, axis=(0, 1)), jnp.sum(pre_grad *...  72.5 us
  transfers between devices with their start and end apart: 69, of which 8 were waited for; matrix products, arithmetic and copies ran while one was open for 3% of the time, Pallas kernels for 0%

commit v1 on v0

v1 whole, which is shorter than its diff:
```python
import functools
import jax
import jax.numpy as jnp
from jax import lax
from jax.experimental import pallas as pl
from jax.experimental.pallas import tpu as pltpu
from jax.sharding import PartitionSpec as P

epsilon = 1e-05
LANES = 128
HALO = 32
f32, bf16 = jnp.float32, jnp.bfloat16


def masked_rows(value, first, limit):
    rows = first + lax.broadcasted_iota(jnp.int32, value.shape, 0)
    return jnp.where(rows < limit, value.astype(f32), 0.0)


def conv_kernel(limits, taps, before, own, convolved, stats, padded):
    utts, rows = own.shape[0], own.shape[1]
    total = jnp.zeros((1, LANES), f32)
    valid_count = 0.0
    for utt in range(utts):
        limit = limits[utt]
        padded[utt, 0:HALO, :] = masked_rows(before[utt], -HALO, limit)
        padded[utt, HALO : HALO + rows, :] = masked_rows(own[utt], 0, limit)
        for start in range(0, rows, 64):
            result = jnp.zeros((64, LANES), f32)
            for tap in range(HALO):
                result = result + taps[tap : tap + 1, :] * padded[utt, start + tap + 1 : start + tap + 65, :]
            convolved[utt, start : start + 64, :] = result
            total = total + jnp.sum(masked_rows(result, start, limit), axis=0, keepdims=True)
        valid_count = valid_count + jnp.clip(limit, 0, rows).astype(f32)
    mean = total / jnp.maximum(valid_count, 1.0)
    squares = jnp.zeros((1, LANES), f32)
    for utt in range(utts):
        centred = masked_rows(convolved[utt] - mean, 0, limits[utt])
        squares = squares + jnp.sum(centred * centred, axis=0, keepdims=True)
    stats[0:1, :] = total
    stats[1:2, :] = squares


def depthwise(limits, taps, before, own):
    utts, rows, channels = own.shape
    tiles = channels // LANES
    return pl.pallas_call(
        conv_kernel,
        grid_spec=pltpu.PrefetchScalarGridSpec(
            num_scalar_prefetch=1,
            grid=(tiles,),
            in_specs=[
                pl.BlockSpec((HALO, LANES), lambda j, s: (0, j)),
                pl.BlockSpec((utts, HALO, LANES), lambda j, s: (0, 0, j)),
                pl.BlockSpec((utts, rows, LANES), lambda j, s: (0, 0, j)),
            ],
            out_specs=[
                pl.BlockSpec((utts, rows, LANES), lambda j, s: (0, 0, j)),
                pl.BlockSpec((2, LANES), lambda j, s: (0, j)),
            ],
            scratch_shapes=[pltpu.VMEM((utts, HALO + rows, LANES), f32)],
        ),
        out_shape=[
            jax.ShapeDtypeStruct(own.shape, f32),
            jax.ShapeDtypeStruct((2, channels), f32),
        ],
        compiler_params=pltpu.CompilerParams(vmem_limit_bytes=24 << 20),
        cost_estimate=pl.CostEstimate(flops=30_000_000, bytes_accessed=3_000_000, transcendentals=0),
    )(limits, taps, before, own)


def project_kernel(scalars, convolved, params, cotangent, active_out, grad_out, send, keep, active):
    utts, rows, channels = convolved.shape
    step = pl.program_id(0)

    @pl.when(step == 0)
    def _():
        for utt in range(utts):
            for start in range(0, rows, 32):
                normed = (convolved[utt, start : start + 32, :] - params[0:1, :]) * params[1:2, :]
                preact = normed * params[2:3, :] + params[3:4, :]
                value = jax.nn.silu(preact).astype(bf16)
                at = utt * rows + start
                active[at : at + 32, :] = value
                active_out[at : at + 32, :] = value

    block = cotangent.shape[2]
    parts = []
    for utt in range(utts):
        parts.append(masked_rows(cotangent[utt], 0, scalars[utt]).astype(bf16))
    masked = jnp.concatenate(parts, 0)
    grad_out[...] = masked
    for start in range(0, channels, 384):
        term = lax.dot_general(
            active[:, start : start + 384], masked, (((0,), (0,)), ((), ())), preferred_element_type=f32
        )

        @pl.when(step < 2)
        def _():
            send[0, start : start + 384, :] = term.astype(bf16)

        @pl.when(step >= 2)
        def _():
            keep[0, start : start + 384, :] = term


def project(scalars, convolved, params, cotangent):
    utts, rows, channels = convolved.shape
    block = channels // 4
    whole = utts * rows
    return pl.pallas_call(
        project_kernel,
        grid_spec=pltpu.PrefetchScalarGridSpec(
            num_scalar_prefetch=1,
            grid=(4,),
            in_specs=[
                pl.BlockSpec((utts, rows, channels), lambda j, s: (0, 0, 0)),
                pl.BlockSpec((4, channels), lambda j, s: (0, 0)),
                pl.BlockSpec((utts, rows, block), lambda j, s: (0, 0, s[2 + j])),
            ],
            out_specs=[
                pl.BlockSpec((whole, channels), lambda j, s: (0, 0)),
                pl.BlockSpec((whole, block), lambda j, s: (0, s[2 + j])),
                pl.BlockSpec((1, channels, block), lambda j, s: (jnp.minimum(j, 1), 0, 0)),
                pl.BlockSpec((1, channels, block), lambda j, s: (jnp.maximum(j - 2, 0), 0, 0)),
            ],
            scratch_shapes=[pltpu.VMEM((whole, channels), bf16)],
        ),
        out_shape=[
            jax.ShapeDtypeStruct((whole, channels), bf16),
            jax.ShapeDtypeStruct((whole, channels), bf16),
            jax.ShapeDtypeStruct((2, channels, block), bf16),
            jax.ShapeDtypeStruct((2, channels, block), f32),
        ],
        compiler_params=pltpu.CompilerParams(vmem_limit_bytes=32 << 20),
        cost_estimate=pl.CostEstimate(
            flops=2 * whole * channels * channels, bytes_accessed=12_000_000, transcendentals=whole * channels
        ),
    )(scalars, convolved, params, cotangent)


def sums_kernel(
    scalars, taps, params, before, own, after, convolved, act_grad, sums, pre_out, normed_out, padded, pre, norm
):
    utts, rows = own.shape[0], own.shape[1]
    reach = rows + HALO
    mean, inverse, gain, shift = (params[i : i + 1, :] for i in range(4))
    bias_sum = jnp.zeros((1, LANES), f32)
    gain_sum = jnp.zeros((1, LANES), f32)
    ones = jnp.zeros((HALO, LANES), f32)
    for utt in range(utts):
        limit = scalars[utt]
        padded[utt, 0:HALO, :] = masked_rows(before[utt], -HALO, limit)
        padded[utt, HALO : HALO + rows, :] = masked_rows(own[utt], 0, limit)
        padded[utt, HALO + rows :, :] = masked_rows(after[utt], rows, limit)
        beyond = jnp.zeros((HALO, LANES), f32)
        for tap in range(HALO):
            beyond = beyond + taps[tap : tap + 1, :] * padded[utt, rows + tap + 1 : rows + tap + 1 + HALO, :]
        for start in range(0, reach, 32):
            value = convolved[utt, start : start + 32, :] if start < rows else beyond
            normed = (value - mean) * inverse
            preact = normed * gain + shift
            sigmoid = jax.nn.sigmoid(preact)
            grad = act_grad[utt, start : start + 32, :] * sigmoid * (1.0 + preact * (1.0 - sigmoid))
            grad = masked_rows(grad, start, limit)
            normed = masked_rows(normed, start, limit)
            pre[utt, start : start + 32, :] = grad
            norm[utt, start : start + 32, :] = normed
            pre_out[utt, start : start + 32, :] = grad
            normed_out[utt, start : start + 32, :] = normed
            if start < rows:
                bias_sum = bias_sum + jnp.sum(grad, axis=0, keepdims=True)
                gain_sum = gain_sum + jnp.sum(grad * normed, axis=0, keepdims=True)
        lag = (
            lax.broadcasted_iota(jnp.int32, (HALO, reach), 1)
            - lax.broadcasted_iota(jnp.int32, (HALO, reach), 0)
            - 1
        )
        band = jnp.where((lag >= 0) & (lag < jnp.minimum(limit, rows)), 1.0, 0.0).astype(bf16)
        ones = ones + jnp.dot(band, padded[utt, 0:reach, :].astype(bf16), preferred_element_type=f32)
    for first in range(0, HALO, 8):
        by_pre = [jnp.zeros((8, LANES), f32) for _ in range(8)]
        by_norm = [jnp.zeros((8, LANES), f32) for _ in range(8)]
        for utt in range(utts):
            for row in range(0, rows, 8):
                grad = pre[utt, row : row + 8, :]
                normed = norm[utt, row : row + 8, :]
                for tap in range(8):
                    at = row + first + tap + 1
                    window = padded[utt, at : at + 8, :]
                    by_pre[tap] = by_pre[tap] + window * grad
                    by_norm[tap] = by_norm[tap] + window * normed
        for tap in range(8):
            sums[0, first + tap : first + tap + 1, :] = jnp.sum(by_pre[tap], axis=0, keepdims=True)
            sums[0, 64 + first + tap : 65 + first + tap, :] = jnp.sum(by_norm[tap], axis=0, keepdims=True)
    sums[0, 32:64, :] = ones
    sums[0, 96:128, :] = jnp.zeros((32, LANES), f32)
    sums[0, 96:97, :] = bias_sum
    sums[0, 97:98, :] = gain_sum


def channel_sums(scalars, taps, params, before, own, after, convolved, act_grad):
    utts, rows, channels = own.shape
    reach = rows + HALO
    block_tiles = channels // 4 // LANES

    def slot(j, s):
        place = s[6 + j // block_tiles]
        return (place, 0, j % block_tiles)

    by_tile = lambda j, s: (0, 0, j)
    return pl.pallas_call(
        sums_kernel,
        grid_spec=pltpu.PrefetchScalarGridSpec(
            num_scalar_prefetch=1,
            grid=(channels // LANES,),
            in_specs=[
                pl.BlockSpec((HALO, LANES), lambda j, s: (0, j)),
                pl.BlockSpec((4, LANES), lambda j, s: (0, j)),
                pl.BlockSpec((utts, HALO, LANES), by_tile),
                pl.BlockSpec((utts, rows, LANES), by_tile),
                pl.BlockSpec((utts, HALO, LANES), by_tile),
                pl.BlockSpec((utts, rows, LANES), by_tile),
                pl.BlockSpec((utts, reach, LANES), by_tile),
            ],
            out_specs=[
                pl.BlockSpec((1, 128, LANES), slot),
                pl.BlockSpec((utts, reach, LANES), by_tile),
                pl.BlockSpec((utts, reach, LANES), by_tile),
            ],
            scratch_shapes=[
                pltpu.VMEM((utts, HALO + reach, LANES), f32),
                pltpu.VMEM((utts, reach, LANES), f32),
                pltpu.VMEM((utts, reach, LANES), f32),
            ],
        ),
        out_shape=[
            jax.ShapeDtypeStruct((4, 128, channels // 4), f32),
            jax.ShapeDtypeStruct((utts, reach, channels), f32),
            jax.ShapeDtypeStruct((utts, reach, channels), f32),
        ],
        compiler_params=pltpu.CompilerParams(vmem_limit_bytes=24 << 20),
        cost_estimate=pl.CostEstimate(flops=80_000_000, bytes_accessed=12_000_000, transcendentals=500_000),
    )(scalars, taps, params, before, own, after, convolved, act_grad)


def back_kernel(limits, taps, params, pre, normed, out, grad):
    utts, rows = out.shape[0], out.shape[1]
    scale, bias_mean, gain_mean = (params[i : i + 1, :] for i in range(3))
    for utt in range(utts):
        limit = limits[utt]
        value = pre[utt] - bias_mean - normed[utt] * gain_mean
        grad[utt] = masked_rows(value * scale, 0, limit)
        for start in range(0, rows, 64):
            result = jnp.zeros((64, LANES), f32)
            for ahead in range(HALO):
                tap = HALO - 1 - ahead
                result = result + taps[tap : tap + 1, :] * grad[utt, start + ahead : start + ahead + 64, :]
            out[utt, start : start + 64, :] = masked_rows(result, start, limit).astype(bf16)


def frames_back(limits, taps, params, pre, normed, rows):
    utts, reach, channels = pre.shape
    by_tile = lambda j, s: (0, 0, j)
    return pl.pallas_call(
        back_kernel,
        grid_spec=pltpu.PrefetchScalarGridSpec(
            num_scalar_prefetch=1,
            grid=(channels // LANES,),
            in_specs=[
                pl.BlockSpec((HALO, LANES), lambda j, s: (0, j)),
                pl.BlockSpec((3, LANES), lambda j, s: (0, j)),
                pl.BlockSpec((utts, reach, LANES), by_tile),
                pl.BlockSpec((utts, reach, LANES), by_tile),
            ],
            out_specs=pl.BlockSpec((utts, rows, LANES), by_tile),
            scratch_shapes=[pltpu.VMEM((utts, reach, LANES), f32)],
        ),
        out_shape=jax.ShapeDtypeStruct((utts, rows, channels), bf16),
        compiler_params=pltpu.CompilerParams(vmem_limit_bytes=24 << 20),
        cost_estimate=pl.CostEstimate(flops=30_000_000, bytes_accessed=5_000_000, transcendentals=0),
    )(limits, taps, params, pre, normed)


def moved(value, steps):
    count = lax.axis_size("tm")
    return lax.ppermute(value, "tm", [(i, i + steps) for i in range(count) if 0 <= i + steps < count])


def other_core(value):
    return lax.ppermute(value, "fsdp", [(0, 1), (1, 0), (2, 3), (3, 2)])


def other_chip(value):
    return lax.ppermute(value, "fsdp", [(0, 2), (2, 0), (1, 3), (3, 1)])


def merged(total, squares, counts):
    count = jnp.sum(counts, axis=0)
    sum_all = jnp.sum(total, axis=0)
    mean = sum_all / jnp.maximum(count, 1.0)
    apart = total / jnp.maximum(counts, 1.0) - mean
    return sum_all, mean, jnp.sum(squares + counts * apart * apart, axis=0), count


def in_three(value):
    first = lax.reduce_precision(value, 8, 7)
    second = lax.reduce_precision(value - first, 8, 7)
    third = value - first - second
    return first.astype(bf16), second.astype(bf16), third.astype(bf16)


def on_device(frames_in, lengths, depth_kernel, norm_gain, norm_bias, out_weight, cotangent):
    utts, rows, channels = frames_in.shape
    tm, fsdp = lax.axis_index("tm"), lax.axis_index("fsdp")
    tm_count, fsdp_count = lax.axis_size("tm"), lax.axis_size("fsdp")
    block = channels // fsdp_count
    chip, core = fsdp // 2, fsdp % 2
    frames_valid = jnp.sum(lengths).astype(f32)
    own_lengths = lax.dynamic_slice_in_dim(lengths, fsdp * utts, utts, 0)
    limits = own_lengths - tm * rows
    near, far = chip * 2, (1 - chip) * 2
    order = jnp.stack([near + 1 - core, far + 1 - core, near + core, far + core])
    index = jnp.arange(4, dtype=jnp.int32)
    place = jnp.where(index % 2 == core, 0, 2) + jnp.where(index // 2 == chip, 0, 1)
    scalars = jnp.concatenate([limits, order, place]).astype(jnp.int32)

    whole_weight = lax.all_gather(out_weight, "fsdp", axis=1, tiled=True)
    before = moved(frames_in[:, rows - HALO :, :], 1)
    before, ahead_frames, ahead_grads = lax.optimization_barrier(
        (before, frames_in[:, :HALO, :], cotangent[:, :HALO, :])
    )
    ahead = moved(jnp.concatenate([ahead_frames, ahead_grads], 0), -1)
    after, after_grad = ahead[:utts], ahead[utts:]

    convolved, stats = depthwise(scalars, depth_kernel, before, frames_in)

    by_fsdp = lax.all_gather(stats, "fsdp")
    mine = lax.dynamic_slice_in_dim(by_fsdp, fsdp * block, block, 2)
    at_tm = jnp.clip(lengths[None, :] - rows * jnp.arange(tm_count, dtype=jnp.int32)[:, None], 0, rows)
    here = jnp.clip(lengths - tm * rows, 0, rows).reshape(fsdp_count, utts).sum(1).astype(f32)
    total, _, squares, _ = merged(mine[:, 0], mine[:, 1], here[:, None])
    third = block // LANES
    piece = jnp.concatenate(
        [total.reshape(third, LANES), squares.reshape(third, LANES), jnp.zeros((8 - 2 * third, LANES), f32)], 0
    )
    pieces = lax.all_to_all(jnp.broadcast_to(piece, (tm_count, 8, LANES)), "tm", 0, 0, tiled=True)
    counts = jnp.sum(at_tm, axis=1).astype(f32)[:, None, None]
    _, mean, squares, _ = merged(pieces[:, :third], pieces[:, third : 2 * third], counts)
    inverse = lax.rsqrt(squares / frames_valid + epsilon)
    norm_params = lax.all_gather(jnp.stack([mean.reshape(block), inverse.reshape(block)]), "fsdp")
    norm_params = norm_params.transpose(1, 0, 2).reshape(2, channels)
    params = jnp.concatenate([norm_params, norm_gain[None], norm_bias[None]], 0)

    active, masked_grad, send, keep = project(scalars, convolved, params, cotangent)
    arrived = other_core(send)
    far_sum = (keep[1] + arrived[1].astype(f32)).astype(bf16)
    far_arrived = other_chip(far_sum)

    ahead_valid = (rows + jnp.arange(HALO, dtype=jnp.int32))[None, :] < limits[:, None]
    after_grad = jnp.where(ahead_valid[:, :, None], after_grad, jnp.zeros((), bf16))
    reach_grad = jnp.concatenate([masked_grad.reshape(utts, rows, channels), after_grad], 1)
    act_grad = lax.dot_general(
        reach_grad.reshape(utts * (rows + HALO), channels),
        whole_weight,
        (((1,), (1,)), ((), ())),
        preferred_element_type=f32,
    ).reshape(utts, rows + HALO, channels)
    sums, pre, normed = channel_sums(
        scalars, depth_kernel, params, before, frames_in, after, convolved, act_grad
    )
    sums_near = sums[:2] + other_core(sums[2:])
    own_sums = sums_near[0] + other_chip(sums_near[1])

    valid_rows = jnp.arange(rows, dtype=jnp.int32)[None, :] < limits[:, None]
    projected = jnp.dot(active, whole_weight, preferred_element_type=f32).reshape(utts, rows, channels)
    mixed = jnp.where(valid_rows[:, :, None], projected, 0.0).astype(bf16)

    own_weight = keep[0] + arrived[0].astype(f32) + far_arrived.astype(f32)
    weight_rows = channels // tm_count
    sum_rows = own_sums.shape[0] // tm_count
    spare = jnp.zeros((tm_count, 8 - 3 * sum_rows, block), bf16)
    split = [part.reshape(tm_count, sum_rows, block) for part in in_three(own_sums)]
    outgoing = jnp.concatenate([own_weight.astype(bf16).reshape(tm_count, weight_rows, block), *split, spare], 1)
    incoming = lax.all_to_all(outgoing, "tm", 0, 0, tiled=True)
    summed = jnp.sum(incoming.astype(f32), axis=0)
    parts = summed[weight_rows : weight_rows + 3 * sum_rows].reshape(3, sum_rows, block)
    reduced = parts[0] + parts[1] + parts[2]
    piece = jnp.concatenate(
        [summed[:weight_rows].astype(bf16), *in_three(reduced), jnp.zeros((8 - 3 * sum_rows, block), bf16)], 0
    )
    gathered = lax.all_to_all(
        jnp.broadcast_to(piece, (tm_count, *piece.shape)), "tm", 0, 0, tiled=True
    )
    weight_grad = gathered[:, :weight_rows].astype(f32).reshape(channels, block)
    terms = gathered[:, weight_rows : weight_rows + 3 * sum_rows].astype(f32).reshape(tm_count, 3, sum_rows, block)
    all_sums = (terms[:, 0] + terms[:, 1] + terms[:, 2]).reshape(tm_count * sum_rows, block)
    bias_own, gain_own = all_sums[96], all_sums[97]
    inverse_own = inverse.reshape(block)
    gain_scale = lax.dynamic_slice_in_dim(norm_gain, fsdp * block, block, 0) * inverse_own
    kernel_own = gain_scale * (
        all_sums[0:32] - bias_own / frames_valid * all_sums[32:64] - gain_own / frames_valid * all_sums[64:96]
    )
    final = jnp.concatenate([kernel_own, all_sums[96:98], jnp.zeros((6, block), f32)], 0)
    final = lax.all_gather(final, "fsdp", axis=1, tiled=True)
    kernel_grad, bias_grad, gain_grad = final[:32], final[32], final[33]
    back_params = jnp.stack([norm_gain * params[1], bias_grad / frames_valid, gain_grad / frames_valid])
    frames_grad = frames_back(scalars, depth_kernel, back_params, pre, normed, rows)
    return (mixed, frames_grad, weight_grad, kernel_grad, gain_grad, bias_grad)


def solution(mesh):
    in_specs = (P("fsdp", "tm", None), P(), P(), P(), P(), P(None, "fsdp"), P("fsdp", "tm", None))
    out_specs = (P("fsdp", "tm", None), P("fsdp", "tm", None), P(None, "fsdp"), P(), P(), P())
    return jax.shard_map(
        on_device, mesh=mesh, in_specs=in_specs, out_specs=out_specs, check_vma=False
    )
```

time: 1900 us -> 256 us (0.13)
  blocking collectives: 853 us -> 64.5 us
  starting transfers between devices: 568 us -> 28 us
  waiting for transfers between devices: 265 us -> 74.2 us
  local copies, waits for them, and re-layouts: 145 us -> 18.7 us
  Pallas kernels: 0 us -> 30.9 us
    unnamed x1 -> x0, blocking collectives: 632 us -> none
    unnamed x64 -> x0, starting transfers between devices: 555 us -> none
    psum x1 -> x0, waiting for transfers between devices: 244 us -> none  [on_device(): kernel_grad = lax.psum(kernel_part, ('tm', 'fsdp'))]
    psum x3 -> x0, blocking collectives: 221 us -> none  [the longest x1 74.6 us: on_device(): lax.psum(jnp.sum(centred * centred * valid_rows, axis=(0, 1)), ('tm', 'fs...]
    unnamed x174 -> x39, local copies, waits for them, and re-layouts: 106 us -> 3.21 us
    all_to_all x0 -> x1, blocking collectives: none -> 48.1 us  [on_device(): incoming = lax.all_to_all(outgoing, 'tm', 0, 0, tiled=True)]
    all_to_all x0 -> x2, waiting for transfers between devices: none -> 45.5 us  [the longest x1 34.1 us: on_device(): lax.all_to_all(jnp.broadcast_to(piece, (tm_count, *piece.shape)), 'tm', 0...]
    pallas_call x0 -> x4, Pallas kernels: none -> 30.9 us  [the longest x1 12.3 us: channel_sums(): pl.pallas_call(sums_kernel, grid_spec=pltpu.PrefetchScalarGridSpec(num_sc...]
  transfers between devices with their start and end apart: 69 -> 9, of which waited for: 8 -> 6; matrix products, arithmetic and copies ran while one was open for 3% -> 8% of each run, Pallas kernels for 0% -> 9%
where the time goes in v1:
time: 256 us; the launch traced here: 253 us
  waiting for transfers between devices  74.2 us (29%)
  blocking collectives  64.5 us (25%)
  Pallas kernels  30.9 us (12%)
  starting transfers between devices  28 us (11%)
  local copies, waits for them, and re-layouts  18.7 us (7%)
  between operations  16.5 us (6%)
  other arithmetic  12.2 us (5%)
  matrix products  8.17 us (3%)
    all_to_all x1, blocking collectives, on_device(): incoming = lax.all_to_all(outgoing, 'tm', 0, 0, tiled=True)  48.1 us
    all_to_all x1, waiting for transfers between devices, on_device(): lax.all_to_all(jnp.broadcast_to(piece, (tm_count, *piece.shape)), 'tm', 0...  34.1 us
    ppermute x2, waiting for transfers between devices, moved(): lax.ppermute(value, 'tm', [(i, i + steps) for i in range(count) if 0 <= i...  17.9 us
    pallas_call x1, Pallas kernels, channel_sums(): pl.pallas_call(sums_kernel, grid_spec=pltpu.PrefetchScalarGridSpec(num_sc...  12.3 us
    all_to_all x1, waiting for transfers between devices, on_device(): lax.all_to_all(jnp.broadcast_to(piece, (tm_count, 8, LANES)), 'tm', 0, 0,...  11.3 us
    all_to_all x1, starting transfers between devices, on_device(): lax.all_to_all(jnp.broadcast_to(piece, (tm_count, 8, LANES)), 'tm', 0, 0,...  9.59 us
    ppermute x2, starting transfers between devices, moved(): lax.ppermute(value, 'tm', [(i, i + steps) for i in range(count) if 0 <= i...  8.64 us
    ppermute x2, waiting for transfers between devices, other_chip(): return lax.ppermute(value, 'fsdp', [(0, 2), (2, 0), (1, 3), (3, 1)])  8.4 us
  transfers between devices with their start and end apart: 9, of which 6 were waited for; matrix products, arithmetic and copies ran while one was open for 8% of the time, Pallas kernels for 9%

profile of v1, /device:TPU:8, one launch (start us, length us, event | category | flops | bytes accessed | tf_op | source)
XLA Modules:
  0.0 253.1 jit_solution(18325478061054708397)
XLA Ops:
  8.0 1.7 fusion.20
  9.7 4.9 %collective-permute-start = (bf16[2,32,1536]{2,1,0:T(8,128)(2,1)S(1)}, bf16[2,32,1536]{2,1,0:T(8,128)(2,1)S(1)}, u32[]{:S(2)}, u32[]{:S(2)}) collective-permute-start(bf16[2,32,1536]{2,1,0:T(8,128)(2,1)S(1)} %get-tuple-element.39), channel_id=1, source_target_pairs={{0,4},{4,8},{8,12},{12,16},{16,20},{20,24},{24,28},{28,32},{32,36}... | collective-permute-start | bytes 589832 | tf_op jit(solution)/shard_map/ppermute | solution.py:287
  14.6 1.3 fusion.23
  17.5 7.1 %collective-permute-done.before = bf16[2,32,1536]{2,1,0:T(8,128)(2,1)S(1)} collective-permute-done((bf16[2,32,1536]{2,1,0:T(8,128)(2,1)S(1)}, bf16[2,32,1536]{2,1,0:T(8,128)(2,1)S(1)}, u32[]{:S(2)}, u32[]{:S(2)}) %collective-permute-start) | collective-permute-done | bytes 196640 | tf_op jit(solution)/shard_map/ppermute | solution.py:287
  24.7 5.2 %shard_map.118 = (f32[2,128,1536]{2,1,0:T(8,128)S(1)}, f32[2,1536]{1,0:T(2,128)S(1)}) custom-call(s32[10]{0:T(128)S(1)} %concatenate.24.limits.scalars, f32[32,1536]{1,0:T(8,128)S(1)} %copy-done.4, bf16[2,32,1536]{2,1,0:T(8,128)(2,1)S(1)} %collective-permute-done.before, bf16[2,128,1536]{2,1,0:T(8,128)(2,1)S(1)} %copy-done), custom_call_target="tpu_custom_call" | custom-call | flops 30000000 | bytes 3000000 | tf_op jit(solution)/shard_map/pallas_call | solution.py:47
  29.9 5.4 %all-gather.2 = f32[4,2,1536]{2,1,0:T(2,128)S(1)} all-gather(f32[1,2,1536]{2,1,0:T(2,128)S(1)} %bitcast.69), channel_id=2, replica_groups=mesh['tm'=64,'fsdp'=4] {'fsdp'}, dimensions={0}, use_global_device_ids=true | all-gather | bytes 61440 | tf_op jit(solution)/shard_map/all_gather | solution.py:338
  36.4 9.6 %all-to-all-start = ((f32[64,8,128]{2,1,0:T(8,128)}), f32[64,8,128]{2,1,0:T(8,128)S(1)}, u32[]{:S(2)}, u32[]{:S(2)}) async-start(f32[64,8,128]{2,1,0:T(8,128)} %broadcast_in_dim.71), calls=%async_computation | async-start | bytes 524288 | tf_op jit(solution)/shard_map/all_to_all | solution.py:347
  48.0 11.3 %all-to-all-done = f32[64,8,128]{2,1,0:T(8,128)S(1)} async-done(((f32[64,8,128]{2,1,0:T(8,128)}), f32[64,8,128]{2,1,0:T(8,128)S(1)}, u32[]{:S(2)}, u32[]{:S(2)}) %all-to-all-start) | async-done | bytes 262176 | tf_op jit(solution)/shard_map/all_to_all | solution.py:347
  59.6 5.2 %all-gather.3 = f32[4,2,384]{2,1,0:T(2,128)S(1)} all-gather(f32[1,2,384]{2,1,0:T(2,128)S(1)} %maximum_bitcast_fusion), channel_id=3, replica_groups=mesh['tm'=64,'fsdp'=4] {'fsdp'}, dimensions={0}, use_global_device_ids=true | all-gather | bytes 15360 | tf_op jit(solution)/shard_map/all_gather | solution.py:351
  64.9 1.1 copy-done.7
  66.0 6.4 %shard_map.119 = (bf16[256,1536]{1,0:T(8,128)(2,1)S(1)}, bf16[256,1536]{1,0:T(8,128)(2,1)S(1)}, bf16[2,1536,384]{2,1,0:T(8,128)(2,1)S(1)}, f32[2,1536,384]{2,1,0:T(8,128)S(1)}) custom-call(s32[10]{0:T(128)S(1)} %concatenate.24.limits.scalars, f32[2,128,1536]{2,1,0:T(8,128)S(1)} %get-tuple-element.19.convolved, f32[4,1536]{1,0:T(4,128)S(1)} %pad_maximum_fusion.1.params, ...), custom_call_target="tpu_custom_call" | custom-call | flops 1207959552 | bytes 12000000 | tf_op jit(solution)/shard_map/pallas_call | solution.py:111
  72.8 3.7 %collective-permute-start.3 = (bf16[4,32,1536]{2,1,0:T(8,128)(2,1)S(1)}, bf16[4,32,1536]{2,1,0:T(8,128)(2,1)S(1)}, u32[]{:S(2)}, u32[]{:S(2)}) collective-permute-start(bf16[4,32,1536]{2,1,0:T(8,128)(2,1)S(1)} %pad_maximum_fusion), channel_id=1, source_target_pairs={{4,0},{8,4},{12,8},{16,12},{20,16},{24,20},{28,24},{32,28},{36,32}... | collective-permute-start | bytes 1179656 | tf_op jit(solution)/shard_map/ppermute | solution.py:287
  76.7 10.8 %collective-permute-done.3 = bf16[4,32,1536]{2,1,0:T(8,128)(2,1)S(1)} collective-permute-done((bf16[4,32,1536]{2,1,0:T(8,128)(2,1)S(1)}, bf16[4,32,1536]{2,1,0:T(8,128)(2,1)S(1)}, u32[]{:S(2)}, u32[]{:S(2)}) %collective-permute-start.3) | collective-permute-done | bytes 393248 | tf_op jit(solution)/shard_map/ppermute | solution.py:287
  87.6 1.4 copy-done.11
  89.0 1.4 fusion.3
  90.4 1.2 collective-permute-start.2
  91.6 4.5 %fusion.act_grad = f32[2,160,1536]{2,1,0:T(8,128)S(1)} fusion(bf16[1536,1536]{1,0:T(8,128)(2,1)} %all-gather.6.cloned.1.call-done, bf16[2,32,1536]{2,1,0:T(8,128)(2,1)S(1)} %get-tuple-element.43, bf16[2,128,1536]{2,1,0:T(8,128)(2,1)} %bitcast.70), kind=kOutput, calls=%fused_computation | convolution fusion | flops 1511915520 | bytes 7667712 | tf_op jit(solution)/shard_map/dot_general | solution.py:363
  96.1 12.3 %shard_map.120 = (f32[4,128,384]{2,1,0:T(8,128)S(1)}, f32[2,160,1536]{2,1,0:T(8,128)S(1)}, f32[2,160,1536]{2,1,0:T(8,128)S(1)}) custom-call(s32[10]{0:T(128)S(1)} %concatenate.24.limits.scalars, f32[32,1536]{1,0:T(8,128)S(1)} %copy-done.4, f32[4,1536]{1,0:T(4,128)S(1)} %pad_maximum_fusion.1.params, bf16[2,32,1536]{2,1,0:T(8,128)(2,1)S(1)} %collective-permute-done.before, ...), custom_call_target="tpu_custom_call" | custom-call | flops 80000000 | bytes 12000000 | tf_op jit(solution)/shard_map/pallas_call | solution.py:212
  108.5 1.7 collective-permute-done.4
  111.3 8.4 %collective-permute-done.2 = bf16[1536,384]{1,0:T(8,128)(2,1)} collective-permute-done((bf16[1536,384]{1,0:T(8,128)(2,1)}, bf16[1536,384]{1,0:T(8,128)(2,1)}, u32[]{:S(2)}, u32[]{:S(2)}) %collective-permute-start.2) | collective-permute-done | bytes 1179680 | tf_op jit(solution)/shard_map/ppermute | solution.py:295
  119.7 2.9 %fusion.2 = bf16[1536,384]{1,0:T(8,128)(2,1)} fusion(bf16[1536,384]{1,0:T(8,128)(2,1)} %collective-permute-done.2, f32[2,1536,384]{2,1,0:T(8,128)S(1)} %bitcast.68, bf16[2,1536,384]{2,1,0:T(8,128)(2,1)S(1)} %copy-done.12), kind=kLoop, calls=%fused_computation.4 | loop fusion | flops 2949120 | bytes 5898240 | tf_op jit(solution)/shard_map/convert_element_type | solution.py:384
  122.8 7.6 %concatenate.29 = bf16[64,32,384]{2,1,0:T(8,128)(2,1)} concatenate(bf16[64,24,384]{2,1,0:T(8,128)(2,1)} %bitcast.71, bf16[64,2,384]{2,1,0:T(2,128)(2,1)S(1)} %reshape.225, bf16[64,2,384]{2,1,0:T(2,128)(2,1)S(1)} %reshape.226, bf16[64,2,384]{2,1,0:T(2,128)(2,1)S(1)} %reshape.227, bf16[64,2,384]{2,1,0:T(2,128)(2,1)S(1)} %broadcast_in_dim.77), dimensions={1} | concatenate | bytes 3145728 | tf_op jit(solution)/shard_map/concatenate | solution.py:384
  130.5 48.1 %all_to_all.15 = bf16[64,32,384]{2,1,0:T(8,128)(2,1)S(1)} all-to-all(bf16[64,32,384]{2,1,0:T(8,128)(2,1)} %concatenate.29), channel_id=1, replica_groups=mesh['tm'=64,'fsdp'=4] {'tm'}, dimensions={0} | all-to-all | bytes 3145728 | tf_op jit(solution)/shard_map/all_to_all | solution.py:385
  178.9 1.3 broadcast_in_dim.79
  180.2 7.1 %all-to-all-start.2 = ((bf16[64,32,384]{2,1,0:T(8,128)(2,1)}), bf16[64,32,384]{2,1,0:T(8,128)(2,1)}, u32[]{:S(2)}, u32[]{:S(2)}) async-start(bf16[64,32,384]{2,1,0:T(8,128)(2,1)} %broadcast_in_dim.79), calls=%async_computation.2 | async-start | bytes 3145728 | tf_op jit(solution)/shard_map/all_to_all | solution.py:392
  187.6 3.7 %fusion.24 = bf16[256,1536]{1,0:T(8,128)(2,1)S(1)} fusion(bf16[256,1536]{1,0:T(8,128)(2,1)S(1)} %copy-done.10, bf16[1536,1536]{1,0:T(8,128)(2,1)} %all-gather.6.cloned.1.call-done), kind=kOutput, calls=%fused_computation.92 | convolution fusion | flops 1207959552 | bytes 6291456 | tf_op jit(solution)/shard_map/dot_general | solution.py:376
  191.3 1.1 select_convert_fusion
  192.4 34.1 %all-to-all-done.2 = bf16[64,32,384]{2,1,0:T(8,128)(2,1)} async-done(((bf16[64,32,384]{2,1,0:T(8,128)(2,1)}), bf16[64,32,384]{2,1,0:T(8,128)(2,1)}, u32[]{:S(2)}, u32[]{:S(2)}) %all-to-all-start.2) | async-done | bytes 1572896 | tf_op jit(solution)/shard_map/all_to_all | solution.py:392
  228.5 5.7 %all_gather.23 = f32[40,1536]{1,0:T(8,128)S(1)} all-gather(f32[40,384]{1,0:T(8,128)S(1)} %maximum_maximum_fusion), channel_id=1, replica_groups=mesh['tm'=64,'fsdp'=4] {'fsdp'}, dimensions={1}, use_global_device_ids=true | all-gather | bytes 307200 | tf_op jit(solution)/shard_map/all_gather | solution.py:405
  235.5 1.4 slice.198
  236.9 1.7 bitcast_convert_fusion
  239.2 7.0 %shard_map.121 = bf16[2,128,1536]{2,1,0:T(8,128)(2,1)} custom-call(s32[10]{0:T(128)S(1)} %concatenate.24.limits.scalars, f32[32,1536]{1,0:T(8,128)S(1)} %copy-done.4, f32[3,1536]{1,0:T(4,128)S(1)} %pad_maximum_fusion.2.params, f32[2,160,1536]{2,1,0:T(8,128)S(1)} %get-tuple-element.28.pre, f32[2,160,1536]{2,1,0:T(8,128)S(1)} %copy-done.3), custom_call_target="tpu_custom_call" | custom-call | flops 30000000 | bytes 5000000 | tf_op jit(solution)/shard_map/pallas_call | solution.py:265
  (117 shorter events, 10.2 us)
Async XLA Ops:
  7.2 17.5 %copy-start = (bf16[2,128,1536]{2,1,0:T(8,128)(2,1)S(1)}, bf16[2,128,1536]{2,1,0:T(8,128)(2,1)}, u32[]{:S(2)}) copy-start(bf16[2,128,1536]{2,1,0:T(8,128)(2,1)} %own.3) | copy-start | bytes 2359300
  7.2 10.2 %copy-start.16 = (s32[8]{0:T(128)S(1)}, s32[8]{0:T(128)}, u32[]{:S(2)}) copy-start(s32[8]{0:T(128)} %param.8) | copy-start | bytes 100
  7.2 17.5 %copy-start.4 = (f32[32,1536]{1,0:T(8,128)S(1)}, f32[32,1536]{1,0:T(8,128)}, u32[]{:S(2)}) copy-start(f32[32,1536]{1,0:T(8,128)} %taps.5) | copy-start | bytes 589828
  7.2 40.8 %copy-start.15 = (f32[1536]{0:T(1024)S(1)}, f32[1536]{0:T(1024)}, u32[]{:S(2)}) copy-start(f32[1536]{0:T(1024)} %param.11) | copy-start | bytes 18436
  7.2 40.8 %copy-start.14 = (f32[1536]{0:T(1024)S(1)}, f32[1536]{0:T(1024)}, u32[]{:S(2)}) copy-start(f32[1536]{0:T(1024)} %param.10) | copy-start | bytes 18436
  7.2 84.4 %all-gather.6.cloned.1.call-start = ((), (), s32[]{:S(2)}) async-start(), calls=%async_computation.3 | async-start | bytes 5898240 | tf_op jit(solution)/shard_map/all_gather | solution.py:328
  9.7 15.0 %collective-permute-start = (bf16[2,32,1536]{2,1,0:T(8,128)(2,1)S(1)}, bf16[2,32,1536]{2,1,0:T(8,128)(2,1)S(1)}, u32[]{:S(2)}, u32[]{:S(2)}) collective-permute-start(bf16[2,32,1536]{2,1,0:T(8,128)(2,1)S(1)} %get-tuple-element.39), channel_id=1, source_target_pairs={{0,4},{4,8},{8,12},{12,16},{16,20},{20,24},{24,28},{28,32},{32,36}... | collective-permute-start | bytes 589832 | tf_op jit(solution)/shard_map/ppermute | solution.py:287
  29.9 42.5 %copy-start.5 = (f32[2,128,1536]{2,1,0:T(8,128)}, f32[2,128,1536]{2,1,0:T(8,128)S(1)}, u32[]{:S(2)}) copy-start(f32[2,128,1536]{2,1,0:T(8,128)S(1)} %get-tuple-element.19.convolved) | copy-start | bytes 4718596
  36.4 23.0 %all-to-all-start = ((f32[64,8,128]{2,1,0:T(8,128)}), f32[64,8,128]{2,1,0:T(8,128)S(1)}, u32[]{:S(2)}, u32[]{:S(2)}) async-start(f32[64,8,128]{2,1,0:T(8,128)} %broadcast_in_dim.71), calls=%async_computation | async-start | bytes 524288 | tf_op jit(solution)/shard_map/all_to_all | solution.py:347
  59.3 13.5 %copy-start.13 = (bf16[2,32,1536]{2,1,0:T(8,128)(2,1)S(1)}, bf16[2,32,1536]{2,1,0:T(8,128)(2,1)}, u32[]{:S(2)}) copy-start(bf16[2,32,1536]{2,1,0:T(8,128)(2,1)} %get-tuple-element.24) | copy-start | bytes 589828
  59.4 13.4 %slice-start.2 = ((bf16[2,128,1536]{2,1,0:T(8,128)(2,1)}), bf16[2,32,1536]{2,1,0:T(8,128)(2,1)S(1)}, s32[]{:S(2)}) async-start(bf16[2,128,1536]{2,1,0:T(8,128)(2,1)} %cotangent.1), calls=%async_computation.6 | async-start | bytes 393216 | tf_op jit(solution)/shard_map/slice | solution.py:331
  64.9 1.1 copy-start.7
  72.4 18.0 %copy-start.1 = (f32[2,1536,384]{2,1,0:T(8,128)}, f32[2,1536,384]{2,1,0:T(8,128)S(1)}, u32[]{:S(2)}) copy-start(f32[2,1536,384]{2,1,0:T(8,128)S(1)} %get-tuple-element.22) | copy-start | bytes 14155780
  72.4 18.0 %copy-start.8 = (bf16[256,1536]{1,0:T(8,128)(2,1)}, bf16[256,1536]{1,0:T(8,128)(2,1)S(1)}, u32[]{:S(2)}) copy-start(bf16[256,1536]{1,0:T(8,128)(2,1)S(1)} %get-tuple-element.26) | copy-start | bytes 2359300
  72.4 18.0 %copy-start.9 = (bf16[256,1536]{1,0:T(8,128)(2,1)}, bf16[256,1536]{1,0:T(8,128)(2,1)S(1)}, u32[]{:S(2)}) copy-start(bf16[256,1536]{1,0:T(8,128)(2,1)S(1)} %get-tuple-element.21) | copy-start | bytes 2359300
  72.4 15.2 %collective-permute-start.1 = (bf16[2,1536,384]{2,1,0:T(8,128)(2,1)S(1)}, bf16[2,1536,384]{2,1,0:T(8,128)(2,1)S(1)}, u32[]{:S(2)}, u32[]{:S(2)}) collective-permute-start(bf16[2,1536,384]{2,1,0:T(8,128)(2,1)S(1)} %get-tuple-element.23), channel_id=1, source_target_pairs={{0,1},{1,0},{2,3},{3,2},{4,5},{5,4},{6,7},{7,6},{8,9},{9,8},{10,11... | collective-permute-start | bytes 7077896 | tf_op jit(solution)/shard_map/ppermute | solution.py:291
  72.8 14.6 %collective-permute-start.3 = (bf16[4,32,1536]{2,1,0:T(8,128)(2,1)S(1)}, bf16[4,32,1536]{2,1,0:T(8,128)(2,1)S(1)}, u32[]{:S(2)}, u32[]{:S(2)}) collective-permute-start(bf16[4,32,1536]{2,1,0:T(8,128)(2,1)S(1)} %pad_maximum_fusion), channel_id=1, source_target_pairs={{4,0},{8,4},{12,8},{16,12},{20,16},{24,20},{28,24},{32,28},{36,32}... | collective-permute-start | bytes 1179656 | tf_op jit(solution)/shard_map/ppermute | solution.py:287
  87.6 1.4 copy-start.11
  90.4 29.3 %collective-permute-start.2 = (bf16[1536,384]{1,0:T(8,128)(2,1)}, bf16[1536,384]{1,0:T(8,128)(2,1)}, u32[]{:S(2)}, u32[]{:S(2)}) collective-permute-start(bf16[1536,384]{1,0:T(8,128)(2,1)} %fusion.3), channel_id=1, source_target_pairs={{0,2},{2,0},{1,3},{3,1},{4,6},{6,4},{5,7},{7,5},{8,10},{10,8},{9,1... | collective-permute-start | bytes 3538952 | tf_op jit(solution)/shard_map/ppermute | solution.py:295
  91.6 28.1 %slice-start = ((s8[4718592]{0:T(1024)(128)(4,1)}), s8[4194304]{0:T(1024)(128)(4,1)S(1)}, s32[]{:S(2)}) async-start(s8[4718592]{0:T(1024)(128)(4,1)} %bitcast.67), calls=%async_computation.4 | async-start | bytes 8388608
  91.6 4.5 %copy-start.6 = (f32[2,128,1536]{2,1,0:T(8,128)S(1)}, f32[2,128,1536]{2,1,0:T(8,128)}, u32[]{:S(2)}) copy-start(f32[2,128,1536]{2,1,0:T(8,128)} %copy-done.5) | copy-start | bytes 4718596
  91.6 28.1 %slice-start.1 = ((s8[4718592]{0:T(1024)(128)(4,1)}), s8[524288]{0:T(1024)(128)(4,1)S(1)}, s32[]{:S(2)}) async-start(s8[4718592]{0:T(1024)(128)(4,1)} %bitcast.67), calls=%async_computation.5 | async-start | bytes 1048576
  108.4 14.2 %copy-start.2 = (f32[2,160,1536]{2,1,0:T(8,128)}, f32[2,160,1536]{2,1,0:T(8,128)S(1)}, u32[]{:S(2)}) copy-start(f32[2,160,1536]{2,1,0:T(8,128)S(1)} %get-tuple-element.29.normed) | copy-start | bytes 5898244
  108.4 11.3 %copy-start.12 = (bf16[2,1536,384]{2,1,0:T(8,128)(2,1)S(1)}, bf16[2,1536,384]{2,1,0:T(8,128)(2,1)}, u32[]{:S(2)}) copy-start(bf16[2,1536,384]{2,1,0:T(8,128)(2,1)} %copy-done.11) | copy-start | bytes 7077892
  108.4 1.8 collective-permute-start.4
  110.3 12.3 %collective-permute-start.5 = (f32[128,384]{1,0:T(8,128)S(1)}, f32[128,384]{1,0:T(8,128)S(1)}, u32[]{:S(2)}, u32[]{:S(2)}) collective-permute-start(f32[128,384]{1,0:T(8,128)S(1)} %slice_bitcast_fusion), channel_id=1, source_target_pairs={{0,2},{2,0},{1,3},{3,1},{4,6},{6,4},{5,7},{7,5},{8,10},{10,8},{9,1... | collective-permute-start | bytes 589832 | tf_op jit(solution)/shard_map/ppermute | solution.py:295
  178.9 8.7 %copy-start.10 = (bf16[256,1536]{1,0:T(8,128)(2,1)S(1)}, bf16[256,1536]{1,0:T(8,128)(2,1)}, u32[]{:S(2)}) copy-start(bf16[256,1536]{1,0:T(8,128)(2,1)} %copy-done.9) | copy-start | bytes 2359300
  180.2 46.3 %all-to-all-start.2 = ((bf16[64,32,384]{2,1,0:T(8,128)(2,1)}), bf16[64,32,384]{2,1,0:T(8,128)(2,1)}, u32[]{:S(2)}, u32[]{:S(2)}) async-start(bf16[64,32,384]{2,1,0:T(8,128)(2,1)} %broadcast_in_dim.79), calls=%async_computation.2 | async-start | bytes 3145728 | tf_op jit(solution)/shard_map/all_to_all | solution.py:392
  236.9 2.3 copy-start.3
Sparse Core Ops, SparseCore 0:
  9.9 58.8 all-gather.5

commit v2 on v1

v2 whole, which is shorter than its diff:
```python
import functools
import jax
import jax.numpy as jnp
from jax import lax
from jax.experimental import pallas as pl
from jax.experimental.pallas import tpu as pltpu
from jax.sharding import PartitionSpec as P

epsilon = 1e-05
LANES = 128
HALO = 32
f32, bf16 = jnp.float32, jnp.bfloat16


def masked_rows(value, first, limit):
    rows = first + lax.broadcasted_iota(jnp.int32, value.shape, 0)
    return jnp.where(rows < limit, value.astype(f32), 0.0)


def limit_of(place, utt, utts, rows):
    return place[place[9] * utts + utt] - place[8] * rows


def chip_of(place):
    return (place[8] & 1) * 2 + (place[9] >> 1)


def conv_kernel(place, taps, before, own, convolved, stats, padded):
    utts, rows = own.shape[0], own.shape[1]
    total = jnp.zeros((1, LANES), f32)
    valid_count = 0.0
    for utt in range(utts):
        limit = limit_of(place, utt, utts, rows)
        padded[utt, 0:HALO, :] = masked_rows(before[utt], -HALO, limit)
        padded[utt, HALO : HALO + rows, :] = masked_rows(own[utt], 0, limit)
        for start in range(0, rows, 64):
            result = jnp.zeros((64, LANES), f32)
            for tap in range(HALO):
                result = result + taps[tap : tap + 1, :] * padded[utt, start + tap + 1 : start + tap + 65, :]
            convolved[utt, start : start + 64, :] = result
            total = total + jnp.sum(masked_rows(result, start, limit), axis=0, keepdims=True)
        valid_count = valid_count + jnp.clip(limit, 0, rows).astype(f32)
    mean = total / jnp.maximum(valid_count, 1.0)
    squares = jnp.zeros((1, LANES), f32)
    for utt in range(utts):
        centred = masked_rows(convolved[utt] - mean, 0, limit_of(place, utt, utts, rows))
        squares = squares + jnp.sum(centred * centred, axis=0, keepdims=True)
    stats[0, 0:1, :] = total
    stats[0, 1:2, :] = squares
    stats[0, 2:3, :] = jnp.zeros((1, LANES), f32) + valid_count


def stats_place(tiles):
    def index(j, s):
        column = j // tiles
        return ((column ^ s[9]) & 1, 0, (column >> 1) * tiles + j % tiles)

    return index


def merge_rows(parts):
    count = sum(part[2:3, :] for part in parts)
    total = sum(part[0:1, :] for part in parts)
    mean = total / jnp.maximum(count, 1.0)
    squares = jnp.zeros_like(mean)
    for part in parts:
        apart = part[0:1, :] / jnp.maximum(part[2:3, :], 1.0) - mean
        squares = squares + part[1:2, :] + part[2:3, :] * apart * apart
    return total, squares, count


def pair_kernel(own, got, out):
    total, squares, count = merge_rows([own[0], got[...]])
    out[0:1, :] = total
    out[1:2, :] = squares
    out[2:3, :] = count


def ring_kernel(own, first, second, third, out):
    total, squares, count = merge_rows([own[...], first[...], second[...], third[...]])
    tiles = total.shape[1] // LANES
    rows = [value[:, i * LANES : (i + 1) * LANES] for value in (total, squares) for i in range(tiles)]
    rows += [count[:, 0:LANES]] * (out.shape[1] - 2 * tiles)
    out[...] = jnp.broadcast_to(jnp.concatenate(rows, 0)[None], out.shape)


def moments_kernel(lengths, pieces, out):
    tiles = out.shape[1] // LANES
    total, squares = pieces[:, 0:tiles, :], pieces[:, tiles : 2 * tiles, :]
    counts = pieces[:, 2 * tiles : 2 * tiles + 1, :]
    valid = lengths[0]
    for utt in range(1, lengths.shape[0]):
        valid = valid + lengths[utt]
    mean = jnp.sum(total, axis=0) / jnp.sum(counts, axis=0)
    apart = total / jnp.maximum(counts, 1.0) - mean[None]
    variance = jnp.sum(squares + counts * apart * apart, axis=0) / (jnp.zeros_like(mean) + valid.astype(f32))
    inverse = lax.rsqrt(variance + epsilon)
    for i in range(tiles):
        out[0:1, i * LANES : (i + 1) * LANES] = mean[i : i + 1, :]
        out[1:2, i * LANES : (i + 1) * LANES] = inverse[i : i + 1, :]


def params_kernel(place, mine, theirs, gain, shift, out):
    block = gain.shape[1] // 4
    core = place[9] & 1
    for chip in range(2):
        part = slice(chip * block, (chip + 1) * block)
        first = pl.multiple_of(chip * 2 * block + core * block, LANES)
        second = pl.multiple_of(chip * 2 * block + (1 - core) * block, LANES)
        out[0:2, pl.ds(first, block)] = mine[:, part]
        out[0:2, pl.ds(second, block)] = theirs[:, part]
    out[2:3, :] = gain[...]
    out[3:4, :] = shift[...]


def in_vmem(kernel, shape, *operands, scalars=0):
    smem, vmem = pl.BlockSpec(memory_space=pltpu.SMEM), pl.BlockSpec(memory_space=pltpu.VMEM)
    return pl.pallas_call(
        kernel,
        in_specs=[smem] * scalars + [vmem] * (len(operands) - scalars),
        out_specs=vmem,
        out_shape=jax.ShapeDtypeStruct(shape, f32),
        compiler_params=pltpu.CompilerParams(vmem_limit_bytes=16 << 20),
        cost_estimate=pl.CostEstimate(flops=100_000, bytes_accessed=50_000, transcendentals=0),
    )(*operands)


def depthwise(place, taps, before, own):
    utts, rows, channels = own.shape
    tiles = channels // LANES
    return pl.pallas_call(
        conv_kernel,
        grid_spec=pltpu.PrefetchScalarGridSpec(
            num_scalar_prefetch=1,
            grid=(tiles,),
            in_specs=[
                pl.BlockSpec((HALO, LANES), lambda j, s: (0, j)),
                pl.BlockSpec((utts, HALO, LANES), lambda j, s: (0, 0, j)),
                pl.BlockSpec((utts, rows, LANES), lambda j, s: (0, 0, j)),
            ],
            out_specs=[
                pl.BlockSpec((utts, rows, LANES), lambda j, s: (0, 0, j)),
                pl.BlockSpec((1, 3, LANES), stats_place(tiles // 4)),
            ],
            scratch_shapes=[pltpu.VMEM((utts, HALO + rows, LANES), f32)],
        ),
        out_shape=[
            jax.ShapeDtypeStruct(own.shape, f32),
            jax.ShapeDtypeStruct((2, 3, channels // 2), f32),
        ],
        compiler_params=pltpu.CompilerParams(vmem_limit_bytes=24 << 20),
        cost_estimate=pl.CostEstimate(flops=30_000_000, bytes_accessed=3_000_000, transcendentals=0),
    )(place, taps, before, own)


QUARTERS = ((2, 0), (1, 1), (2, 1), (3, 0), (1, 0), (3, 1), (0, 0), (0, 1))


def quarter_term(place, active, grads, quarter):
    size = active.shape[1] // 4
    side, row = place[10 + quarter], place[18 + quarter]
    first = pl.multiple_of(((chip_of(place) + side & 3) >> 1) * (2 * size) + row * size, LANES)
    masked = jnp.concatenate([grads[utt] for utt in range(grads.shape[0])], 0)
    return lax.dot_general(
        active[:, pl.ds(first, size)], masked, (((0,), (0,)), ((), ())), preferred_element_type=f32
    )


def send_kernel(place, convolved, params, grads_even, grads_odd, active_out, first, rest, active):
    utts, rows, channels = convolved.shape
    step = pl.program_id(0)

    @pl.when(step == 0)
    def _():
        for utt in range(utts):
            limit = limit_of(place, utt, utts, rows)
            for start in range(0, rows, 32):
                normed = (convolved[utt, start : start + 32, :] - params[0:1, :]) * params[1:2, :]
                preact = normed * params[2:3, :] + params[3:4, :]
                value = masked_rows(jax.nn.silu(preact), start, limit).astype(bf16)
                at = utt * rows + start
                active[at : at + 32, :] = value
                active_out[at : at + 32, :] = value

    even = quarter_term(place, active, grads_even, 2 * step).astype(bf16)
    odd = quarter_term(place, active, grads_odd, 2 * step + 1).astype(bf16)

    @pl.when(step < 2)
    def _():
        first[0] = even
        first[1] = odd

    @pl.when(step >= 2)
    def _():
        rest[0] = even
        rest[1] = odd


def keep_kernel(place, active, grads_even, grads_odd, first, rest):
    step = pl.program_id(0)
    even = quarter_term(place, active, grads_even, 2 * step)
    odd = quarter_term(place, active, grads_odd, 2 * step + 1)

    @pl.when(step < 2)
    def _():
        first[0] = even
        first[1] = odd

    @pl.when(step >= 2)
    def _():
        rest[0] = even
        rest[1] = odd


def weight_terms(place, convolved, params, reach_grad):
    utts, rows, channels = convolved.shape
    block = channels // 4
    whole = utts * rows

    def column(odd, other):
        return lambda i, s: (
            0,
            0,
            (chip_of(s) + s[10 + 2 * i + odd] & 1) * 2 + ((s[9] & 1) ^ other),
        )

    early = lambda i, s: (jnp.minimum(i, 1), 0, 0)
    late = lambda i, s: (jnp.maximum(i - 2, 0), 0, 0)
    active, send_first, send_rest = pl.pallas_call(
        send_kernel,
        grid_spec=pltpu.PrefetchScalarGridSpec(
            num_scalar_prefetch=1,
            grid=(4,),
            in_specs=[
                pl.BlockSpec((utts, rows, channels), lambda i, s: (0, 0, 0)),
                pl.BlockSpec((4, channels), lambda i, s: (0, 0)),
                pl.BlockSpec((utts, rows, block), column(0, 1)),
                pl.BlockSpec((utts, rows, block), column(1, 1)),
            ],
            out_specs=[
                pl.BlockSpec((whole, channels), lambda i, s: (0, 0)),
                pl.BlockSpec((2, block, block), early),
                pl.BlockSpec((2, block, block), late),
            ],
            scratch_shapes=[pltpu.VMEM((whole, channels), bf16)],
        ),
        out_shape=[
            jax.ShapeDtypeStruct((whole, channels), bf16),
            jax.ShapeDtypeStruct((4, block, block), bf16),
            jax.ShapeDtypeStruct((4, block, block), bf16),
        ],
        compiler_params=pltpu.CompilerParams(vmem_limit_bytes=24 << 20),
        cost_estimate=pl.CostEstimate(
            flops=whole * channels * channels, bytes_accessed=6_000_000, transcendentals=whole * channels
        ),
    )(place, convolved, params, reach_grad, reach_grad)
    keep_first, keep_rest = pl.pallas_call(
        keep_kernel,
        grid_spec=pltpu.PrefetchScalarGridSpec(
            num_scalar_prefetch=1,
            grid=(4,),
            in_specs=[
                pl.BlockSpec((whole, channels), lambda i, s: (0, 0)),
                pl.BlockSpec((utts, rows, block), column(0, 0)),
                pl.BlockSpec((utts, rows, block), column(1, 0)),
            ],
            out_specs=[
                pl.BlockSpec((2, block, block), early),
                pl.BlockSpec((2, block, block), late),
            ],
        ),
        out_shape=[jax.ShapeDtypeStruct((4, block, block), f32)] * 2,
        compiler_params=pltpu.CompilerParams(vmem_limit_bytes=24 << 20),
        cost_estimate=pl.CostEstimate(
            flops=whole * channels * channels, bytes_accessed=6_000_000, transcendentals=0
        ),
    )(place, active, reach_grad, reach_grad)
    return active, send_first, send_rest, keep_first, keep_rest


def pack_kernel(base, low, high, sums, out):
    groups, size = out.shape[0], out.shape[1] - 8
    first = pl.program_id(0) * groups
    total = base[...] + jnp.where(pl.program_id(0) < 2, low[...].astype(f32), high[...].astype(f32))
    filler = jnp.zeros((2, total.shape[1]), f32)
    for group in range(groups):
        row = first + group
        ride = jnp.concatenate([sums[pl.ds(row, 1), :], sums[pl.ds(32 + row, 1), :], sums[64:65, :]], 0)
        rounded = ride.astype(bf16).astype(f32)
        out[group] = jnp.concatenate(
            [total[group * size : (group + 1) * size], rounded, ride - rounded, filler], 0
        ).astype(bf16)


def packed(base, low, high, sums, count):
    half, block = base.shape
    size = half // count
    groups = count // 4
    by_rows = lambda i: (i, 0)
    return pl.pallas_call(
        pack_kernel,
        grid=(count // groups,),
        in_specs=[
            pl.BlockSpec((groups * size, block), by_rows),
            pl.BlockSpec((groups * size, block), lambda i: (jnp.minimum(i, 1), 0)),
            pl.BlockSpec((groups * size, block), lambda i: (jnp.maximum(i - 2, 0), 0)),
            pl.BlockSpec(sums.shape, lambda i: (0, 0)),
        ],
        out_specs=pl.BlockSpec((groups, size + 8, block), lambda i: (i, 0, 0)),
        out_shape=jax.ShapeDtypeStruct((count, size + 8, block), bf16),
        compiler_params=pltpu.CompilerParams(vmem_limit_bytes=16 << 20),
        cost_estimate=pl.CostEstimate(flops=2_000_000, bytes_accessed=4_000_000, transcendentals=0),
    )(base, low, high, sums)


def fill_padded(place, padded, before, own, after):
    utts, rows = own.shape[0], own.shape[1]
    for utt in range(utts):
        limit = limit_of(place, utt, utts, rows)
        padded[utt, 0:HALO, :] = masked_rows(before[utt], -HALO, limit)
        padded[utt, HALO : HALO + rows, :] = masked_rows(own[utt], 0, limit)
        if after is not None:
            padded[utt, HALO + rows :, :] = masked_rows(after[utt], rows, limit)


def correlate(padded, other, rows, store):
    for first in range(0, HALO, 8):
        running = [jnp.zeros((8, LANES), f32) for _ in range(8)]
        for utt in range(padded.shape[0]):
            for row in range(0, rows, 8):
                value = other[utt, row : row + 8, :]
                for tap in range(8):
                    at = row + first + tap + 1
                    running[tap] = running[tap] + padded[utt, at : at + 8, :] * value
        for tap in range(8):
            store(first + tap, jnp.sum(running[tap], axis=0, keepdims=True))


def early_kernel(place, before, own, convolved, stats, early, padded, centred):
    utts, rows = own.shape[0], own.shape[1]
    mean = stats[0, 0:1, :] / jnp.maximum(stats[0, 2:3, :], 1.0)
    fill_padded(place, padded, before, own, None)
    ones = jnp.zeros((HALO, LANES), f32)
    for utt in range(utts):
        limit = limit_of(place, utt, utts, rows)
        centred[utt] = masked_rows(convolved[utt] - mean, 0, limit)
        lag = (
            lax.broadcasted_iota(jnp.int32, (HALO, HALO + rows), 1)
            - lax.broadcasted_iota(jnp.int32, (HALO, HALO + rows), 0)
            - 1
        )
        band = jnp.where((lag >= 0) & (lag < jnp.minimum(limit, rows)), 1.0, 0.0).astype(bf16)
        ones = ones + jnp.dot(band, padded[utt].astype(bf16), preferred_element_type=f32)
    early[0:32, :] = ones

    def store(tap, value):
        early[32 + tap : 33 + tap, :] = value

    correlate(padded, centred, rows, store)


def early_sums(place, before, own, convolved, stats):
    utts, rows, channels = own.shape
    by_tile = lambda j, s: (0, 0, j)
    return pl.pallas_call(
        early_kernel,
        grid_spec=pltpu.PrefetchScalarGridSpec(
            num_scalar_prefetch=1,
            grid=(channels // LANES,),
            in_specs=[
                pl.BlockSpec((utts, HALO, LANES), by_tile),
                pl.BlockSpec((utts, rows, LANES), by_tile),
                pl.BlockSpec((utts, rows, LANES), by_tile),
                pl.BlockSpec((1, 3, LANES), stats_place(channels // 4 // LANES)),
            ],
            out_specs=pl.BlockSpec((64, LANES), lambda j, s: (0, j)),
            scratch_shapes=[
                pltpu.VMEM((utts, HALO + rows, LANES), f32),
                pltpu.VMEM((utts, rows, LANES), f32),
            ],
        ),
        out_shape=jax.ShapeDtypeStruct((64, channels), f32),
        compiler_params=pltpu.CompilerParams(vmem_limit_bytes=24 << 20),
        cost_estimate=pl.CostEstimate(flops=30_000_000, bytes_accessed=4_000_000, transcendentals=0),
    )(place, before, own, convolved, stats)


def late_kernel(
    place, params, before, own, convolved, act_grad, stats, early, sums, pre_out, normed_out, ends_out, padded, pre
):
    utts, rows = own.shape[0], own.shape[1]
    mean, inverse, gain, shift = (params[i : i + 1, :] for i in range(4))
    bias_sum = jnp.zeros((1, LANES), f32)
    gain_sum = jnp.zeros((1, LANES), f32)
    fill_padded(place, padded, before, own, None)
    for utt in range(utts):
        limit = limit_of(place, utt, utts, rows)
        for start in range(0, rows, 32):
            normed = (convolved[utt, start : start + 32, :] - mean) * inverse
            preact = normed * gain + shift
            sigmoid = jax.nn.sigmoid(preact)
            grad = act_grad[utt, start : start + 32, :] * sigmoid * (1.0 + preact * (1.0 - sigmoid))
            grad = masked_rows(grad, start, limit)
            normed = masked_rows(normed, start, limit)
            pre_out[utt, start : start + 32, :] = grad
            normed_out[utt, start : start + 32, :] = normed
            pre[utt, start : start + 32, :] = grad
            bias_sum = bias_sum + jnp.sum(grad, axis=0, keepdims=True)
            gain_sum = gain_sum + jnp.sum(grad * normed, axis=0, keepdims=True)
            if start == 0:
                ends_out[utt] = grad.astype(bf16)
                ends_out[utts + utt] = normed.astype(bf16)
    column = pl.program_id(0) // (pl.num_programs(0) // 4) >> 1
    near = (column - chip_of(place) & 3) >> 1

    def store(tap, value):
        sums[0, 0, near, tap : tap + 1, :] = value

    correlate(padded, pre, rows, store)
    ones = early[0:32, :]
    own_mean = stats[0, 0:1, :] / jnp.maximum(stats[0, 2:3, :], 1.0)
    sums[0, 0, near, 32:64, :] = ones
    sums[0, 0, near, 64:72, :] = jnp.zeros((8, LANES), f32) + bias_sum
    sums[0, 0, 1 - near, 0:32, :] = (early[32:64, :] + (own_mean - mean) * ones) * inverse
    sums[0, 0, 1 - near, 32:64, :] = jnp.zeros((32, LANES), f32)
    sums[0, 0, 1 - near, 64:72, :] = jnp.zeros((8, LANES), f32) + gain_sum


def late_sums(place, params, before, own, convolved, act_grad, stats, early):
    utts, rows, channels = own.shape
    block_tiles = channels // 4 // LANES

    def slot(j, s):
        column = j // block_tiles
        return ((column ^ s[9]) & 1, ((column >> 1) ^ (s[9] >> 1)) & 1, 0, 0, j % block_tiles)

    by_tile = lambda j, s: (0, 0, j)
    by_column = lambda j, s: (0, j)
    return pl.pallas_call(
        late_kernel,
        grid_spec=pltpu.PrefetchScalarGridSpec(
            num_scalar_prefetch=1,
            grid=(channels // LANES,),
            in_specs=[
                pl.BlockSpec((4, LANES), by_column),
                pl.BlockSpec((utts, HALO, LANES), by_tile),
                pl.BlockSpec((utts, rows, LANES), by_tile),
                pl.BlockSpec((utts, rows, LANES), by_tile),
                pl.BlockSpec((utts, rows, LANES), by_tile),
                pl.BlockSpec((1, 3, LANES), stats_place(block_tiles)),
                pl.BlockSpec((64, LANES), by_column),
            ],
            out_specs=[
                pl.BlockSpec((1, 1, 2, 72, LANES), slot),
                pl.BlockSpec((utts, rows, LANES), by_tile),
                pl.BlockSpec((utts, rows, LANES), by_tile),
                pl.BlockSpec((2 * utts, HALO, LANES), by_tile),
            ],
            scratch_shapes=[
                pltpu.VMEM((utts, HALO + rows, LANES), f32),
                pltpu.VMEM((utts, rows, LANES), f32),
            ],
        ),
        out_shape=[
            jax.ShapeDtypeStruct((2, 2, 2, 72, channels // 4), f32),
            jax.ShapeDtypeStruct((utts, rows, channels), f32),
            jax.ShapeDtypeStruct((utts, rows, channels), f32),
            jax.ShapeDtypeStruct((2 * utts, HALO, channels), bf16),
        ],
        compiler_params=pltpu.CompilerParams(vmem_limit_bytes=24 << 20),
        cost_estimate=pl.CostEstimate(flops=40_000_000, bytes_accessed=10_000_000, transcendentals=500_000),
    )(place, params, before, own, convolved, act_grad, stats, early)


def back_kernel(place, taps, params, pre, normed, ahead, out, grad):
    utts, rows = out.shape[0], out.shape[1]
    scale, bias_mean, gain_mean = (params[i : i + 1, :] for i in range(3))
    for utt in range(utts):
        limit = limit_of(place, utt, utts, rows)
        value = pre[utt] - bias_mean - normed[utt] * gain_mean
        grad[utt, 0:rows, :] = masked_rows(value * scale, 0, limit)
        value = ahead[utt].astype(f32) - bias_mean - ahead[utts + utt].astype(f32) * gain_mean
        grad[utt, rows:, :] = masked_rows(value * scale, rows, limit)
        for start in range(0, rows, 64):
            result = jnp.zeros((64, LANES), f32)
            for lead in range(HALO):
                tap = HALO - 1 - lead
                result = result + taps[tap : tap + 1, :] * grad[utt, start + lead : start + lead + 64, :]
            out[utt, start : start + 64, :] = masked_rows(result, start, limit).astype(bf16)


def frames_back(place, taps, params, pre, normed, ahead):
    utts, rows, channels = pre.shape
    by_tile = lambda j, s: (0, 0, j)
    return pl.pallas_call(
        back_kernel,
        grid_spec=pltpu.PrefetchScalarGridSpec(
            num_scalar_prefetch=1,
            grid=(channels // LANES,),
            in_specs=[
                pl.BlockSpec((HALO, LANES), lambda j, s: (0, j)),
                pl.BlockSpec((3, LANES), lambda j, s: (0, j)),
                pl.BlockSpec((utts, rows, LANES), by_tile),
                pl.BlockSpec((utts, rows, LANES), by_tile),
                pl.BlockSpec((2 * utts, HALO, LANES), by_tile),
            ],
            out_specs=pl.BlockSpec((utts, rows, LANES), by_tile),
            scratch_shapes=[pltpu.VMEM((utts, rows + HALO, LANES), f32)],
        ),
        out_shape=jax.ShapeDtypeStruct((utts, rows, channels), bf16),
        compiler_params=pltpu.CompilerParams(vmem_limit_bytes=24 << 20),
        cost_estimate=pl.CostEstimate(flops=30_000_000, bytes_accessed=5_000_000, transcendentals=0),
    )(place, taps, params, pre, normed, ahead)


def widen_kernel(place, value, *refs):
    refs[-1][0] = value[...].astype(f32)


def widened(place, value, other, whole):
    half, block = value.shape
    aliased = whole is not None
    return pl.pallas_call(
        widen_kernel,
        grid_spec=pltpu.PrefetchScalarGridSpec(
            num_scalar_prefetch=1,
            grid=(2,),
            in_specs=[pl.BlockSpec((half // 2, block), lambda i, s: (i, 0))]
            + [pl.BlockSpec(memory_space=pl.ANY)] * aliased,
            out_specs=pl.BlockSpec((1, half // 2, block), lambda i, s: ((s[8] & 1) ^ other, i, 0)),
        ),
        out_shape=jax.ShapeDtypeStruct((2, half, block), f32),
        input_output_aliases={2: 0} if aliased else {},
        compiler_params=pltpu.CompilerParams(vmem_limit_bytes=16 << 20),
        cost_estimate=pl.CostEstimate(flops=half * block, bytes_accessed=6 * half * block, transcendentals=0),
    )(place, value, *([whole] if aliased else []))


def moved(value, steps):
    count = lax.axis_size("tm")
    return lax.ppermute(value, "tm", [(i, i + steps) for i in range(count) if 0 <= i + steps < count])


def other_core(value):
    return lax.ppermute(value, "fsdp", [(0, 1), (1, 0), (2, 3), (3, 2)])


def other_chip(value):
    return lax.ppermute(value, "fsdp", [(0, 2), (2, 0), (1, 3), (3, 1)])


def across(value):
    return lax.ppermute(value, "tm", [(i, i ^ 1) for i in range(lax.axis_size("tm"))])


def along(value, steps):
    pairs = []
    for device in range(4 * lax.axis_size("tm")):
        plane, high, low, core = device // 8, device // 4 % 2, device // 2 % 2, device % 2
        place = (high * 2 + low + steps) % 4
        pairs.append((device, plane * 8 + place // 2 * 4 + place % 2 * 2 + core))
    return lax.ppermute(value, ("tm", "fsdp"), pairs)


def in_plane(value):
    count = lax.axis_size("tm")
    groups = [list(range(start, count, 2)) for start in range(2)]
    return lax.all_to_all(value, "tm", 0, 0, axis_index_groups=groups, tiled=True)


def from_all(value, chip, core):
    by_core = other_core(value)
    pair = jnp.where(core == 0, jnp.stack([value, by_core]), jnp.stack([by_core, value]))
    by_chip = other_chip(pair)
    return jnp.where(chip == 0, jnp.concatenate([pair, by_chip]), jnp.concatenate([by_chip, pair]))


def in_three(value):
    first = lax.reduce_precision(value, 8, 7)
    second = lax.reduce_precision(value - first, 8, 7)
    third = value - first - second
    return first.astype(bf16), second.astype(bf16), third.astype(bf16)


def on_device(frames_in, lengths, depth_kernel, norm_gain, norm_bias, out_weight, cotangent):
    utts, rows, channels = frames_in.shape
    tm, fsdp = lax.axis_index("tm"), lax.axis_index("fsdp")
    tm_count, fsdp_count = lax.axis_size("tm"), lax.axis_size("fsdp")
    block, half = channels // fsdp_count, channels // 2
    chip, core, high = fsdp // 2, fsdp % 2, tm % 2
    frames_valid = jnp.sum(lengths).astype(f32)
    table = [side for side, _ in QUARTERS] + [row for _, row in QUARTERS]
    scalars = jnp.concatenate(
        [lengths, jnp.stack([tm, fsdp]).astype(jnp.int32), jnp.array(table, jnp.int32)]
    )

    whole_weight = lax.all_gather(out_weight, "fsdp", axis=1, tiled=True)
    before = moved(frames_in[:, rows - HALO :, :], 1)
    convolved, stats = depthwise(scalars, depth_kernel, before, frames_in)

    plane = tm_count // 2
    chip_stats = in_vmem(pair_kernel, (3, half), stats, other_core(stats[1]))
    pieces = in_vmem(
        ring_kernel,
        (plane, 16, LANES),
        chip_stats,
        along(chip_stats, 1),
        along(chip_stats, -1),
        along(chip_stats, 2),
    )
    pieces, early_frames = lax.optimization_barrier((pieces, frames_in))
    pieces = in_plane(pieces)
    early = early_sums(scalars, before, early_frames, convolved, stats)
    pieces, early = lax.optimization_barrier((pieces, early))
    mine = in_vmem(moments_kernel, (2, half), lengths, pieces, scalars=1)
    params = in_vmem(
        params_kernel,
        (4, channels),
        scalars,
        mine,
        other_core(mine),
        norm_gain[None],
        norm_bias[None],
        scalars=1,
    )

    active, send_first, send_rest, keep_first, keep_rest = weight_terms(scalars, convolved, params, cotangent)
    got_first, got_rest = other_core(send_first), other_core(send_rest)
    upward = (keep_first[:2] + got_first[:2].astype(f32)).astype(bf16)
    downward = (keep_first[2:] + got_first[2:].astype(f32)).astype(bf16)
    upward, downward, out_grads = lax.optimization_barrier((upward, downward, cotangent))
    below, above = along(upward, 1), along(downward, -1)
    act_grad = lax.dot_general(
        out_grads.reshape(utts * rows, channels),
        whole_weight,
        (((1,), (1,)), ((), ())),
        preferred_element_type=f32,
    ).reshape(frames_in.shape)
    sums, pre, normed, first_rows = late_sums(
        scalars, params, before, frames_in, convolved, act_grad, stats, early
    )
    near_sums = sums[0] + other_core(sums[1])

    rest = keep_rest + got_rest.astype(f32)
    upward = (rest[0] + below[0].astype(f32)).astype(bf16)
    downward = (rest[1] + above[0].astype(f32)).astype(bf16)
    upward, downward, near_sums, first_rows = lax.optimization_barrier(
        (upward, downward, near_sums, first_rows)
    )
    base = jnp.concatenate([rest[2] + above[1].astype(f32), rest[3] + below[1].astype(f32)], 0)
    below, above = along(upward, 1), along(downward, -1)
    kept = (
        near_sums[0, 0]
        + along(near_sums[1, 0], 1)
        + along(near_sums[0, 1], 2)
        + along(near_sums[1, 1], -1)
    )

    outgoing = packed(base, below, above, kept, plane)
    incoming = in_plane(outgoing)
    summed = jnp.sum(incoming.astype(f32), axis=0)
    weight_rows = half // plane
    ride = summed[weight_rows : weight_rows + 3] + summed[weight_rows + 3 : weight_rows + 6]
    piece = summed[:weight_rows].astype(bf16)
    piece, ride, first_rows = lax.optimization_barrier((piece, ride, first_rows))
    ahead = moved(first_rows, -1)
    gathered = in_plane(jnp.broadcast_to(piece, (plane, *piece.shape)))

    far_ride = across(ride)
    by_high = jnp.where(high == 0, jnp.stack([ride, far_ride]), jnp.stack([far_ride, ride]))
    ends = by_high[:, 2] / frames_valid
    gain_scale = lax.dynamic_slice_in_dim(norm_gain * params[1], fsdp * block, block, 0)
    kernel_own = gain_scale * (by_high[0, 0] - ends[0] * by_high[0, 1] - ends[1] * by_high[1, 0])
    rows_own = jnp.concatenate([by_high[:, 2], kernel_own[None]], 0)
    whole_rows = from_all(rows_own, chip, core).transpose(1, 0, 2).reshape(3, channels)
    bias_grad, gain_grad = whole_rows[0], whole_rows[1]
    back_params = jnp.concatenate([(norm_gain * params[1])[None], whole_rows[:2] / frames_valid], 0)
    frames_grad = frames_back(scalars, depth_kernel, back_params, pre, normed, ahead)

    mine = gathered.reshape(half, block)
    mine, active, kernel_row = lax.optimization_barrier((mine, active, whole_rows[2:]))
    theirs = across(mine)
    kernel_row = kernel_row.reshape(channels // LANES, LANES)
    kernel_row = jnp.concatenate([kernel_row, kernel_row[: 16 - channels // LANES]], 0)
    kernel_rows = in_plane(jnp.broadcast_to(kernel_row, (plane, 16, LANES)))
    kernel_grad = kernel_rows[:, : channels // LANES].reshape(plane, channels)
    mixed = jnp.dot(active, whole_weight, preferred_element_type=f32).astype(bf16).reshape(frames_in.shape)
    weight_grad = widened(scalars, theirs, 1, widened(scalars, mine, 0, None)).reshape(channels, block)
    return (mixed, frames_grad, weight_grad, kernel_grad, gain_grad, bias_grad)


def solution(mesh):
    in_specs = (P("fsdp", "tm", None), P(), P(), P(), P(), P(None, "fsdp"), P("fsdp", "tm", None))
    out_specs = (P("fsdp", "tm", None), P("fsdp", "tm", None), P(None, "fsdp"), P(), P(), P())
    return jax.shard_map(
        on_device, mesh=mesh, in_specs=in_specs, out_specs=out_specs, check_vma=False
    )
```

time: 256 us -> 195 us (0.76)
  blocking collectives: 64.5 us -> 0 us
  starting transfers between devices: 28 us -> 60.5 us
  waiting for transfers between devices: 74.2 us -> 51.7 us
  Pallas kernels: 30.9 us -> 41.7 us
  local copies, waits for them, and re-layouts: 18.7 us -> 10.4 us
  other arithmetic: 12.2 us -> 6.62 us
    all_to_all x1 -> x0, blocking collectives: 48.1 us -> none  [on_device(): incoming = lax.all_to_all(outgoing, 'tm', 0, 0, tiled=True)]
    all_to_all x2 -> x4, waiting for transfers between devices: 45.5 us -> 23.7 us  [in_plane(): lax.all_to_all(value, 'tm', 0, 0, axis_index_groups=groups, tiled=True)]
    all_gather x3 -> x0, blocking collectives: 16.4 us -> none  [the longest x1 5.73 us: on_device(): final = lax.all_gather(final, 'fsdp', axis=1, tiled=True)]
    all_to_all x2 -> x4, starting transfers between devices: 16.7 us -> 31.8 us  [in_plane(): lax.all_to_all(value, 'tm', 0, 0, axis_index_groups=groups, tiled=True)]
    ppermute x0 -> x12, waiting for transfers between devices: none -> 14.6 us  [the longest x10 14.6 us: along(): return lax.ppermute(value, ('tm', 'fsdp'), pairs)]
    ppermute x0 -> x12, starting transfers between devices: none -> 14 us  [the longest x10 10.8 us: along(): return lax.ppermute(value, ('tm', 'fsdp'), pairs)]
    pallas_call x2 -> x11, Pallas kernels: 18.6 us -> 29.5 us  [the longest x1 8.11 us: late_sums(): pl.pallas_call(late_kernel, grid_spec=pltpu.PrefetchScalarGridSpec(num_sc...]
    ppermute x2 -> x1, waiting for transfers between devices: 8.4 us -> 0.01 us  [other_chip(): return lax.ppermute(value, 'fsdp', [(0, 2), (2, 0), (1, 3), (3, 1)])]
  transfers between devices with their start and end apart: 9 -> 26, of which waited for: 6 -> 12; matrix products, arithmetic and copies ran while one was open for 8% -> 11% of each run, Pallas kernels for 9% -> 20%
where the time goes in v2:
time: 195 us
  starting transfers between devices  60.5 us (31%)
  waiting for transfers between devices  51.7 us (27%)
  Pallas kernels  41.7 us (21%)
  between operations  15.3 us (8%)
  local copies, waits for them, and re-layouts  10.4 us (5%)
  matrix products  8.39 us (4%)
  other arithmetic  6.62 us (3%)
    all_to_all x4, starting transfers between devices, in_plane(): lax.all_to_all(value, 'tm', 0, 0, axis_index_groups=groups, tiled=True)  31.8 us
    all_to_all x4, waiting for transfers between devices, in_plane(): lax.all_to_all(value, 'tm', 0, 0, axis_index_groups=groups, tiled=True)  23.7 us
    ppermute x10, waiting for transfers between devices, along(): return lax.ppermute(value, ('tm', 'fsdp'), pairs)  14.6 us
    ppermute x2, starting transfers between devices, moved(): lax.ppermute(value, 'tm', [(i, i + steps) for i in range(count) if 0 <= i...  11.3 us
    ppermute x10, starting transfers between devices, along(): return lax.ppermute(value, ('tm', 'fsdp'), pairs)  10.8 us
    ppermute x2, waiting for transfers between devices, moved(): lax.ppermute(value, 'tm', [(i, i + steps) for i in range(count) if 0 <= i...  9.96 us
    pallas_call x1, Pallas kernels, late_sums(): pl.pallas_call(late_kernel, grid_spec=pltpu.PrefetchScalarGridSpec(num_sc...  8.11 us
    pallas_call x1, Pallas kernels, early_sums(): pl.pallas_call(early_kernel, grid_spec=pltpu.PrefetchScalarGridSpec(num_s...  7.19 us
  transfers between devices with their start and end apart: 26, of which 12 were waited for; matrix products, arithmetic and copies ran while one was open for 11% of the time, Pallas kernels for 20%

profile of v2, /device:TPU:8, one launch (start us, length us, event | category | flops | bytes accessed | tf_op | source)
XLA Modules:
  0.0 194.5 jit_solution(6230992254822980931)
XLA Ops:
  8.9 4.9 %collective-permute-start = (bf16[2,32,1536]{2,1,0:T(8,128)(2,1)S(1)}, bf16[2,32,1536]{2,1,0:T(8,128)(2,1)S(1)}, u32[]{:S(2)}, u32[]{:S(2)}) collective-permute-start(bf16[2,32,1536]{2,1,0:T(8,128)(2,1)S(1)} %slice.120), channel_id=1, source_target_pairs={{0,4},{4,8},{8,12},{12,16},{16,20},{20,24},{24,28},{28,32},{32,36}... | collective-permute-start | bytes 589832 | tf_op jit(solution)/shard_map/ppermute | solution.py:541
  13.9 10.0 %collective-permute-done.before = bf16[2,32,1536]{2,1,0:T(8,128)(2,1)S(1)} collective-permute-done((bf16[2,32,1536]{2,1,0:T(8,128)(2,1)S(1)}, bf16[2,32,1536]{2,1,0:T(8,128)(2,1)S(1)}, u32[]{:S(2)}, u32[]{:S(2)}) %collective-permute-start) | collective-permute-done | bytes 196640 | tf_op jit(solution)/shard_map/ppermute | solution.py:541
  23.9 5.2 %shard_map.127 = (f32[2,128,1536]{2,1,0:T(8,128)S(1)}, f32[2,3,768]{2,1,0:T(4,128)S(1)}) custom-call(s32[26]{0:T(128)S(1)} %pad_add_fusion.place, f32[32,1536]{1,0:T(8,128)S(1)} %copy-done.10, bf16[2,32,1536]{2,1,0:T(8,128)(2,1)S(1)} %collective-permute-done.before, bf16[2,128,1536]{2,1,0:T(8,128)(2,1)S(1)} %copy-done.1), custom_call_target="tpu_custom_call" | custom-call | flops 30000000 | bytes 3000000 | tf_op jit(solution)/shard_map/pallas_call | solution.py:131
  31.1 2.6 %collective-permute-start.3 = (f32[3,768]{1,0:T(4,128)S(1)}, f32[3,768]{1,0:T(4,128)S(1)}, u32[]{:S(2)}, u32[]{:S(2)}) collective-permute-start(f32[3,768]{1,0:T(4,128)S(1)} %shard_map.128.own), channel_id=1, source_target_pairs={{0,6},{1,7},{2,0},{3,1},{4,2},{5,3},{6,4},{7,5},{8,14},{9,15},{10,... | collective-permute-start | bytes 27656 | tf_op jit(solution)/shard_map/ppermute | solution.py:562
  33.8 1.7 collective-permute-done.2.first
  35.4 3.8 %collective-permute-done.4.third = f32[3,768]{1,0:T(4,128)S(1)} collective-permute-done((f32[3,768]{1,0:T(4,128)S(1)}, f32[3,768]{1,0:T(4,128)S(1)}, u32[]{:S(2)}, u32[]{:S(2)}) %collective-permute-start.4) | collective-permute-done | bytes 9248 | tf_op jit(solution)/shard_map/ppermute | solution.py:562
  39.9 8.9 %all-to-all-start = ((f32[32,16,128]{2,1,0:T(8,128)}), f32[32,16,128]{2,1,0:T(8,128)}, u32[]{:S(2)}, u32[]{:S(2)}) async-start(f32[32,16,128]{2,1,0:T(8,128)} %shard_map.129), calls=%async_computation | async-start | bytes 524288 | tf_op jit(solution)/shard_map/all_to_all | solution.py:568
  49.6 7.2 %shard_map.130.early = f32[64,1536]{1,0:T(8,128)S(1)} custom-call(s32[26]{0:T(128)S(1)} %pad_add_fusion.place, bf16[2,32,1536]{2,1,0:T(8,128)(2,1)S(1)} %collective-permute-done.before, bf16[2,128,1536]{2,1,0:T(8,128)(2,1)S(1)} %copy-done.1, f32[2,128,1536]{2,1,0:T(8,128)S(1)} %get-tuple-element.34.convolved, f32[2,3,768]{2,1,0:T(4,128)S(1)} %copy-done.14), custom_call_target="tpu_custom_call" | custom-call | flops 30000000 | bytes 4000000 | tf_op jit(solution)/shard_map/pallas_call | solution.py:365
  57.6 1.6 all-to-all-done.pieces
  62.0 4.1 %shard_map.133 = (bf16[256,1536]{1,0:T(8,128)(2,1)S(1)}, bf16[4,384,384]{2,1,0:T(8,128)(2,1)S(1)}, bf16[4,384,384]{2,1,0:T(8,128)(2,1)}) custom-call(s32[26]{0:T(128)S(1)} %pad_add_fusion.place, f32[2,128,1536]{2,1,0:T(8,128)S(1)} %get-tuple-element.34.convolved, f32[4,1536]{1,0:T(4,128)S(1)} %shard_map.132.params, bf16[2,128,1536]{2,1,0:T(8,128)(2,1)S(1)} %copy-done, ...), custom_call_target="tpu_custom_call" | custom-call | flops 603979776 | bytes 6000000 | tf_op jit(solution)/shard_map/pallas_call | solution.py:229
  66.7 2.8 %shard_map.134 = (f32[4,384,384]{2,1,0:T(8,128)S(1)}, f32[4,384,384]{2,1,0:T(8,128)S(1)}) custom-call(s32[26]{0:T(128)S(1)} %pad_add_fusion.place, bf16[256,1536]{1,0:T(8,128)(2,1)S(1)} %get-tuple-element.56.active, bf16[2,128,1536]{2,1,0:T(8,128)(2,1)S(1)} %copy-done, bf16[2,128,1536]{2,1,0:T(8,128)(2,1)S(1)} %copy-done), custom_call_target="tpu_custom_call" | custom-call | flops 603979776 | bytes 6000000 | tf_op jit(solution)/shard_map/pallas_call | solution.py:257
  71.3 2.0 %collective-permute-start.9 = (bf16[2,384,384]{2,1,0:T(8,128)(2,1)}, bf16[2,384,384]{2,1,0:T(8,128)(2,1)}, u32[]{:S(2)}, u32[]{:S(2)}) collective-permute-start(bf16[2,384,384]{2,1,0:T(8,128)(2,1)} %get-tuple-element.45), channel_id=1, source_target_pairs={{0,2},{1,3},{2,4},{3,5},{4,6},{5,7},{6,0},{7,1},{8,10},{9,11},{10,... | collective-permute-start | bytes 1769480 | tf_op jit(solution)/shard_map/ppermute | solution.py:562
  73.3 3.8 %fusion.act_grad = f32[2,128,1536]{2,1,0:T(8,128)S(1)} fusion(bf16[2,128,1536]{2,1,0:T(8,128)(2,1)S(1)} %copy-done, bf16[1536,1536]{1,0:T(8,128)(2,1)} %all-gather.2.cloned.1.call-done), kind=kOutput, calls=%fused_computation | convolution fusion | flops 1207959552 | bytes 7077888 | tf_op jit(solution)/shard_map/dot_general | solution.py:633
  77.1 8.1 %shard_map.135 = (f32[2,2,2,72,384]{4,3,2,1,0:T(8,128)S(1)}, f32[2,128,1536]{2,1,0:T(8,128)S(1)}, f32[2,128,1536]{2,1,0:T(8,128)S(1)}, bf16[4,32,1536]{2,1,0:T(8,128)(2,1)}) custom-call(s32[26]{0:T(128)S(1)} %pad_add_fusion.place, f32[4,1536]{1,0:T(4,128)S(1)} %copy-done.17, bf16[2,32,1536]{2,1,0:T(8,128)(2,1)S(1)} %collective-permute-done.before, ...), custom_call_target="tpu_custom_call" | custom-call | flops 40000000 | bytes 10000000 | tf_op jit(solution)/shard_map/pallas_call | solution.py:439
  85.6 2.3 %convert_add_fusion = f32[4,384,384]{2,1,0:T(8,128)S(1)} fusion(f32[4,384,384]{2,1,0:T(8,128)S(1)} %copy-done.3, bf16[4,384,384]{2,1,0:T(8,128)(2,1)} %collective-permute-done.6), kind=kLoop, calls=%fused_computation.3 | loop fusion | flops 1179648 | bytes 5898240 | tf_op jit(solution)/shard_map/add | solution.py:644
  88.2 1.5 fusion.7
  90.4 2.7 %collective-permute-start.12 = (bf16[384,384]{1,0:T(8,128)(2,1)S(1)}, bf16[384,384]{1,0:T(8,128)(2,1)S(1)}, u32[]{:S(2)}, u32[]{:S(2)}) collective-permute-start(bf16[384,384]{1,0:T(8,128)(2,1)S(1)} %get-tuple-element.51), channel_id=1, source_target_pairs={{0,6},{1,7},{2,0},{3,1},{4,2},{5,3},{6,4},{7,5},{8,14},{9,15},{10,... | collective-permute-start | bytes 884744 | tf_op jit(solution)/shard_map/ppermute | solution.py:562
  95.3 8.2 %collective-permute-done.15 = f32[72,384]{1,0:T(8,128)S(1)} collective-permute-done((f32[72,384]{1,0:T(8,128)S(1)}, f32[72,384]{1,0:T(8,128)S(1)}, u32[]{:S(2)}, u32[]{:S(2)}) %collective-permute-start.15) | collective-permute-done | bytes 110624 | tf_op jit(solution)/shard_map/ppermute | solution.py:562
  104.3 1.7 shard_map.136
  106.0 8.2 %all-to-all-start.1 = ((bf16[32,32,384]{2,1,0:T(8,128)(2,1)}), bf16[32,32,384]{2,1,0:T(8,128)(2,1)S(1)}, u32[]{:S(2)}, u32[]{:S(2)}) async-start(bf16[32,32,384]{2,1,0:T(8,128)(2,1)} %shard_map.136), calls=%async_computation.1 | async-start | bytes 1572864 | tf_op jit(solution)/shard_map/all_to_all | solution.py:568
  115.5 17.9 %all-to-all-done.1 = bf16[32,32,384]{2,1,0:T(8,128)(2,1)S(1)} async-done(((bf16[32,32,384]{2,1,0:T(8,128)(2,1)}), bf16[32,32,384]{2,1,0:T(8,128)(2,1)S(1)}, u32[]{:S(2)}, u32[]{:S(2)}) %all-to-all-start.1) | async-done | bytes 786464 | tf_op jit(solution)/shard_map/all_to_all | solution.py:568
  135.4 7.6 %all-to-all-start.2 = ((bf16[32,24,384]{2,1,0:T(8,128)(2,1)}), bf16[32,24,384]{2,1,0:T(8,128)(2,1)S(1)}, u32[]{:S(2)}, u32[]{:S(2)}) async-start(bf16[32,24,384]{2,1,0:T(8,128)(2,1)} %broadcast_in_dim.20), calls=%async_computation.2 | async-start | bytes 1179648 | tf_op jit(solution)/shard_map/all_to_all | solution.py:568
  144.5 2.3 %collective-permute-start.18 = (f32[2,3,384]{2,0,1:T(2,128)S(1)}, f32[2,3,384]{2,0,1:T(2,128)S(1)}, u32[]{:S(2)}, u32[]{:S(2)}) collective-permute-start(f32[2,3,384]{2,0,1:T(2,128)S(1)} %maximum_select_fusion.2), channel_id=1, source_target_pairs={{0,2},{2,0},{1,3},{3,1},{4,6},{6,4},{5,7},{7,5},{8,10},{10,8},{9,1... | collective-permute-start | bytes 27656 | tf_op jit(solution)/shard_map/ppermute | solution.py:549
  146.9 6.4 %collective-permute-start.19 = (bf16[4,32,1536]{2,1,0:T(8,128)(2,1)}, bf16[4,32,1536]{2,1,0:T(8,128)(2,1)S(1)}, u32[]{:S(2)}, u32[]{:S(2)}) collective-permute-start(bf16[4,32,1536]{2,1,0:T(8,128)(2,1)} %get-tuple-element.59), channel_id=1, source_target_pairs={{4,0},{8,4},{12,8},{16,12},{20,16},{24,20},{28,24},{32,28},{36,32}... | collective-permute-start | bytes 1179656 | tf_op jit(solution)/shard_map/ppermute | solution.py:541
  153.3 4.3 %all-to-all-done.2 = bf16[32,24,384]{2,1,0:T(8,128)(2,1)S(1)} async-done(((bf16[32,24,384]{2,1,0:T(8,128)(2,1)}), bf16[32,24,384]{2,1,0:T(8,128)(2,1)S(1)}, u32[]{:S(2)}, u32[]{:S(2)}) %all-to-all-start.2) | async-done | bytes 589856 | tf_op jit(solution)/shard_map/all_to_all | solution.py:568
  157.6 3.1 %collective-permute-start.20 = (bf16[768,384]{1,0:T(8,128)(2,1)S(1)}, bf16[768,384]{1,0:T(8,128)(2,1)S(1)}, u32[]{:S(2)}, u32[]{:S(2)}) collective-permute-start(bf16[768,384]{1,0:T(8,128)(2,1)S(1)} %bitcast.56), channel_id=1, source_target_pairs={{0,4},{4,0},{8,12},{12,8},{16,20},{20,16},{24,28},{28,24},{32,36},... | collective-permute-start | bytes 1769480 | tf_op jit(solution)/shard_map/ppermute | solution.py:553
  161.5 7.0 %all-to-all-start.3 = ((f32[32,16,128]{2,1,0:T(8,128)}), f32[32,16,128]{2,1,0:T(8,128)}, u32[]{:S(2)}, u32[]{:S(2)}) async-start(f32[32,16,128]{2,1,0:T(8,128)} %broadcast_in_dim.23), calls=%async_computation.3 | async-start | bytes 524288 | tf_op jit(solution)/shard_map/all_to_all | solution.py:568
  171.2 7.0 %shard_map.137 = bf16[2,128,1536]{2,1,0:T(8,128)(2,1)} custom-call(s32[26]{0:T(128)S(1)} %pad_add_fusion.place, f32[32,1536]{1,0:T(8,128)S(1)} %copy-done.10, f32[3,1536]{1,0:T(4,128)S(1)} %pad_maximum_fusion.1.params, f32[2,128,1536]{2,1,0:T(8,128)S(1)} %copy-done.7, f32[2,128,1536]{2,1,0:T(8,128)S(1)} %copy-done.9, ...), custom_call_target="tpu_custom_call" | custom-call | flops 30000000 | bytes 5000000 | tf_op jit(solution)/shard_map/pallas_call | solution.py:495
  178.1 1.6 shard_map.138.refs_0_
  179.8 4.6 %convolution_convert_fusion = bf16[256,1536]{1,0:T(8,128)(2,1)} fusion(bf16[256,1536]{1,0:T(8,128)(2,1)S(1)} %copy-done.12, bf16[1536,1536]{1,0:T(8,128)(2,1)} %all-gather.2.cloned.1.call-done), kind=kOutput, calls=%fused_computation.2 | convolution fusion | flops 1208352768 | bytes 6291456 | tf_op jit(solution)/shard_map/dot_general | solution.py:687
  184.4 1.7 copy.19
  186.1 1.6 shard_map.139
  (125 shorter events, 22.8 us)
Async XLA Ops:
  7.2 16.7 %copy-start.1 = (bf16[2,128,1536]{2,1,0:T(8,128)(2,1)S(1)}, bf16[2,128,1536]{2,1,0:T(8,128)(2,1)}, u32[]{:S(2)}) copy-start(bf16[2,128,1536]{2,1,0:T(8,128)(2,1)} %own.4) | copy-start | bytes 2359300
  7.2 16.7 %copy-start.10 = (f32[32,1536]{1,0:T(8,128)S(1)}, f32[32,1536]{1,0:T(8,128)}, u32[]{:S(2)}) copy-start(f32[32,1536]{1,0:T(8,128)} %taps.3) | copy-start | bytes 589828
  7.2 66.1 %all-gather.2.cloned.1.call-start = ((), (), s32[]{:S(2)}) async-start(), calls=%async_computation.4 | async-start | bytes 5898240 | tf_op jit(solution)/shard_map/all_gather | solution.py:597
  8.9 15.0 %collective-permute-start = (bf16[2,32,1536]{2,1,0:T(8,128)(2,1)S(1)}, bf16[2,32,1536]{2,1,0:T(8,128)(2,1)S(1)}, u32[]{:S(2)}, u32[]{:S(2)}) collective-permute-start(bf16[2,32,1536]{2,1,0:T(8,128)(2,1)S(1)} %slice.120), channel_id=1, source_target_pairs={{0,4},{4,8},{8,12},{12,16},{16,20},{20,24},{24,28},{28,32},{32,36}... | collective-permute-start | bytes 589832 | tf_op jit(solution)/shard_map/ppermute | solution.py:541
  29.1 19.7 %copy-start.13 = (f32[2,3,768]{2,1,0:T(4,128)}, f32[2,3,768]{2,1,0:T(4,128)S(1)}, u32[]{:S(2)}) copy-start(f32[2,3,768]{2,1,0:T(4,128)S(1)} %get-tuple-element.35.own.stats) | copy-start | bytes 55300
  29.2 1.3 collective-permute-start.1
  30.4 5.0 %collective-permute-start.2 = (f32[3,768]{1,0:T(4,128)S(1)}, f32[3,768]{1,0:T(4,128)S(1)}, u32[]{:S(2)}, u32[]{:S(2)}) collective-permute-start(f32[3,768]{1,0:T(4,128)S(1)} %shard_map.128.own), channel_id=1, source_target_pairs={{0,2},{1,3},{2,4},{3,5},{4,6},{5,7},{6,0},{7,1},{8,10},{9,11},{10,... | collective-permute-start | bytes 27656 | tf_op jit(solution)/shard_map/ppermute | solution.py:562
  31.1 4.3 %collective-permute-start.3 = (f32[3,768]{1,0:T(4,128)S(1)}, f32[3,768]{1,0:T(4,128)S(1)}, u32[]{:S(2)}, u32[]{:S(2)}) collective-permute-start(f32[3,768]{1,0:T(4,128)S(1)} %shard_map.128.own), channel_id=1, source_target_pairs={{0,6},{1,7},{2,0},{3,1},{4,2},{5,3},{6,4},{7,5},{8,14},{9,15},{10,... | collective-permute-start | bytes 27656 | tf_op jit(solution)/shard_map/ppermute | solution.py:562
  33.8 5.4 %collective-permute-start.4 = (f32[3,768]{1,0:T(4,128)S(1)}, f32[3,768]{1,0:T(4,128)S(1)}, u32[]{:S(2)}, u32[]{:S(2)}) collective-permute-start(f32[3,768]{1,0:T(4,128)S(1)} %shard_map.128.own), channel_id=1, source_target_pairs={{0,4},{1,5},{2,6},{3,7},{4,0},{5,1},{6,2},{7,3},{8,12},{9,13},{10,... | collective-permute-start | bytes 27656 | tf_op jit(solution)/shard_map/ppermute | solution.py:562
  39.9 19.2 %all-to-all-start = ((f32[32,16,128]{2,1,0:T(8,128)}), f32[32,16,128]{2,1,0:T(8,128)}, u32[]{:S(2)}, u32[]{:S(2)}) async-start(f32[32,16,128]{2,1,0:T(8,128)} %shard_map.129), calls=%async_computation | async-start | bytes 524288 | tf_op jit(solution)/shard_map/all_to_all | solution.py:568
  49.6 10.7 %copy-start.19 = (f32[1536]{0:T(1024)S(1)}, f32[1536]{0:T(1024)}, u32[]{:S(2)}) copy-start(f32[1536]{0:T(1024)} %param.11) | copy-start | bytes 18436
  49.6 12.4 %copy-start = (bf16[2,128,1536]{2,1,0:T(8,128)(2,1)S(1)}, bf16[2,128,1536]{2,1,0:T(8,128)(2,1)}, u32[]{:S(2)}) copy-start(bf16[2,128,1536]{2,1,0:T(8,128)(2,1)} %grads_odd.3) | copy-start | bytes 2359300
  60.2 1.3 collective-permute-start.5
  66.2 3.3 %collective-permute-start.7 = (bf16[4,384,384]{2,1,0:T(8,128)(2,1)S(1)}, bf16[4,384,384]{2,1,0:T(8,128)(2,1)S(1)}, u32[]{:S(2)}, u32[]{:S(2)}) collective-permute-start(bf16[4,384,384]{2,1,0:T(8,128)(2,1)S(1)} %get-tuple-element.43), channel_id=1, source_target_pairs={{0,1},{1,0},{2,3},{3,2},{4,5},{5,4},{6,7},{7,6},{8,9},{9,8},{10,11... | collective-permute-start | bytes 3538952 | tf_op jit(solution)/shard_map/ppermute | solution.py:545
  66.3 19.3 %collective-permute-start.6 = (bf16[4,384,384]{2,1,0:T(8,128)(2,1)}, bf16[4,384,384]{2,1,0:T(8,128)(2,1)}, u32[]{:S(2)}, u32[]{:S(2)}) collective-permute-start(bf16[4,384,384]{2,1,0:T(8,128)(2,1)} %get-tuple-element.41), channel_id=1, source_target_pairs={{0,1},{1,0},{2,3},{3,2},{4,5},{5,4},{6,7},{7,6},{8,9},{9,8},{10,11... | collective-permute-start | bytes 3538952 | tf_op jit(solution)/shard_map/ppermute | solution.py:545
  71.3 16.7 %collective-permute-start.8 = (bf16[2,384,384]{2,1,0:T(8,128)(2,1)}, bf16[2,384,384]{2,1,0:T(8,128)(2,1)}, u32[]{:S(2)}, u32[]{:S(2)}) collective-permute-start(bf16[2,384,384]{2,1,0:T(8,128)(2,1)} %get-tuple-element.44), channel_id=1, source_target_pairs={{0,6},{1,7},{2,0},{3,1},{4,2},{5,3},{6,4},{7,5},{8,14},{9,15},{10,... | collective-permute-start | bytes 1769480 | tf_op jit(solution)/shard_map/ppermute | solution.py:562
  71.3 16.9 %collective-permute-start.9 = (bf16[2,384,384]{2,1,0:T(8,128)(2,1)}, bf16[2,384,384]{2,1,0:T(8,128)(2,1)}, u32[]{:S(2)}, u32[]{:S(2)}) collective-permute-start(bf16[2,384,384]{2,1,0:T(8,128)(2,1)} %get-tuple-element.45), channel_id=1, source_target_pairs={{0,2},{1,3},{2,4},{3,5},{4,6},{5,7},{6,0},{7,1},{8,10},{9,11},{10,... | collective-permute-start | bytes 1769480 | tf_op jit(solution)/shard_map/ppermute | solution.py:562
  85.3 4.4 %collective-permute-start.10 = (f32[2,2,72,384]{3,2,1,0:T(8,128)S(1)}, f32[2,2,72,384]{3,2,1,0:T(8,128)S(1)}, u32[]{:S(2)}, u32[]{:S(2)}) collective-permute-start(f32[2,2,72,384]{3,2,1,0:T(8,128)S(1)} %slice_bitcast_fusion), channel_id=1, source_target_pairs={{0,1},{1,0},{2,3},{3,2},{4,5},{5,4},{6,7},{7,6},{8,9},{9,8},{10,11... | collective-permute-start | bytes 1327112 | tf_op jit(solution)/shard_map/ppermute | solution.py:545
  89.8 14.5 %collective-permute-start.11 = (bf16[384,384]{1,0:T(8,128)(2,1)S(1)}, bf16[384,384]{1,0:T(8,128)(2,1)S(1)}, u32[]{:S(2)}, u32[]{:S(2)}) collective-permute-start(bf16[384,384]{1,0:T(8,128)(2,1)S(1)} %get-tuple-element.50), channel_id=1, source_target_pairs={{0,2},{1,3},{2,4},{3,5},{4,6},{5,7},{6,0},{7,1},{8,10},{9,11},{10,... | collective-permute-start | bytes 884744 | tf_op jit(solution)/shard_map/ppermute | solution.py:562
  90.4 13.9 %collective-permute-start.12 = (bf16[384,384]{1,0:T(8,128)(2,1)S(1)}, bf16[384,384]{1,0:T(8,128)(2,1)S(1)}, u32[]{:S(2)}, u32[]{:S(2)}) collective-permute-start(bf16[384,384]{1,0:T(8,128)(2,1)S(1)} %get-tuple-element.51), channel_id=1, source_target_pairs={{0,6},{1,7},{2,0},{3,1},{4,2},{5,3},{6,4},{7,5},{8,14},{9,15},{10,... | collective-permute-start | bytes 884744 | tf_op jit(solution)/shard_map/ppermute | solution.py:562
  93.1 10.4 %collective-permute-start.15 = (f32[72,384]{1,0:T(8,128)S(1)}, f32[72,384]{1,0:T(8,128)S(1)}, u32[]{:S(2)}, u32[]{:S(2)}) collective-permute-start(f32[72,384]{1,0:T(8,128)S(1)} %get-tuple-element.76), channel_id=1, source_target_pairs={{0,6},{1,7},{2,0},{3,1},{4,2},{5,3},{6,4},{7,5},{8,14},{9,15},{10,... | collective-permute-start | bytes 331784 | tf_op jit(solution)/shard_map/ppermute | solution.py:562
  93.2 10.3 %collective-permute-start.14 = (f32[72,384]{1,0:T(8,128)S(1)}, f32[72,384]{1,0:T(8,128)S(1)}, u32[]{:S(2)}, u32[]{:S(2)}) collective-permute-start(f32[72,384]{1,0:T(8,128)S(1)} %get-tuple-element.77), channel_id=1, source_target_pairs={{0,4},{1,5},{2,6},{3,7},{4,0},{5,1},{6,2},{7,3},{8,12},{9,13},{10,... | collective-permute-start | bytes 331784 | tf_op jit(solution)/shard_map/ppermute | solution.py:562
  94.6 9.6 %collective-permute-start.13 = (f32[72,384]{1,0:T(8,128)S(1)}, f32[72,384]{1,0:T(8,128)S(1)}, u32[]{:S(2)}, u32[]{:S(2)}) collective-permute-start(f32[72,384]{1,0:T(8,128)S(1)} %get-tuple-element.75), channel_id=1, source_target_pairs={{0,2},{1,3},{2,4},{3,5},{4,6},{5,7},{6,0},{7,1},{8,10},{9,11},{10,... | collective-permute-start | bytes 331784 | tf_op jit(solution)/shard_map/ppermute | solution.py:562
  106.0 27.4 %all-to-all-start.1 = ((bf16[32,32,384]{2,1,0:T(8,128)(2,1)}), bf16[32,32,384]{2,1,0:T(8,128)(2,1)S(1)}, u32[]{:S(2)}, u32[]{:S(2)}) async-start(bf16[32,32,384]{2,1,0:T(8,128)(2,1)} %shard_map.136), calls=%async_computation.1 | async-start | bytes 1572864 | tf_op jit(solution)/shard_map/all_to_all | solution.py:568
  133.5 36.3 %copy-start.7 = (f32[2,128,1536]{2,1,0:T(8,128)S(1)}, f32[2,128,1536]{2,1,0:T(8,128)}, u32[]{:S(2)}) copy-start(f32[2,128,1536]{2,1,0:T(8,128)} %copy-done.6) | copy-start | bytes 4718596
  133.5 9.5 %collective-permute-start.16 = (f32[3,384]{1,0:T(4,128)S(1)}, f32[3,384]{1,0:T(4,128)S(1)}, u32[]{:S(2)}, u32[]{:S(2)}) collective-permute-start(f32[3,384]{1,0:T(4,128)S(1)} %slice_add_fusion.4), channel_id=1, source_target_pairs={{0,4},{4,0},{8,12},{12,8},{16,20},{20,16},{24,28},{28,24},{32,36},... | collective-permute-start | bytes 13832 | tf_op jit(solution)/shard_map/ppermute | solution.py:553
  135.4 22.2 %all-to-all-start.2 = ((bf16[32,24,384]{2,1,0:T(8,128)(2,1)}), bf16[32,24,384]{2,1,0:T(8,128)(2,1)S(1)}, u32[]{:S(2)}, u32[]{:S(2)}) async-start(bf16[32,24,384]{2,1,0:T(8,128)(2,1)} %broadcast_in_dim.20), calls=%async_computation.2 | async-start | bytes 1179648 | tf_op jit(solution)/shard_map/all_to_all | solution.py:568
  143.2 1.3 collective-permute-start.17
  144.5 8.7 %collective-permute-start.18 = (f32[2,3,384]{2,0,1:T(2,128)S(1)}, f32[2,3,384]{2,0,1:T(2,128)S(1)}, u32[]{:S(2)}, u32[]{:S(2)}) collective-permute-start(f32[2,3,384]{2,0,1:T(2,128)S(1)} %maximum_select_fusion.2), channel_id=1, source_target_pairs={{0,2},{2,0},{1,3},{3,1},{4,6},{6,4},{5,7},{7,5},{8,10},{10,8},{9,1... | collective-permute-start | bytes 27656 | tf_op jit(solution)/shard_map/ppermute | solution.py:549
  146.9 22.9 %collective-permute-start.19 = (bf16[4,32,1536]{2,1,0:T(8,128)(2,1)}, bf16[4,32,1536]{2,1,0:T(8,128)(2,1)S(1)}, u32[]{:S(2)}, u32[]{:S(2)}) collective-permute-start(bf16[4,32,1536]{2,1,0:T(8,128)(2,1)} %get-tuple-element.59), channel_id=1, source_target_pairs={{4,0},{8,4},{12,8},{16,12},{20,16},{24,20},{28,24},{32,28},{36,32}... | collective-permute-start | bytes 1179656 | tf_op jit(solution)/shard_map/ppermute | solution.py:541
  157.6 28.5 %collective-permute-start.20 = (bf16[768,384]{1,0:T(8,128)(2,1)S(1)}, bf16[768,384]{1,0:T(8,128)(2,1)S(1)}, u32[]{:S(2)}, u32[]{:S(2)}) collective-permute-start(bf16[768,384]{1,0:T(8,128)(2,1)S(1)} %bitcast.56), channel_id=1, source_target_pairs={{0,4},{4,0},{8,12},{12,8},{16,20},{20,16},{24,28},{28,24},{32,36},... | collective-permute-start | bytes 1769480 | tf_op jit(solution)/shard_map/ppermute | solution.py:553
  161.5 22.9 %all-to-all-start.3 = ((f32[32,16,128]{2,1,0:T(8,128)}), f32[32,16,128]{2,1,0:T(8,128)}, u32[]{:S(2)}, u32[]{:S(2)}) async-start(f32[32,16,128]{2,1,0:T(8,128)} %broadcast_in_dim.23), calls=%async_computation.3 | async-start | bytes 524288 | tf_op jit(solution)/shard_map/all_to_all | solution.py:568
  (15 other events, 54.0 us)
Sparse Core Ops, SparseCore 0:
  9.9 56.2 all-gather.1

commit v3 on v2

--- a/solution.py
+++ b/solution.py
@@ -513,6 +513,65 @@
     )(place, taps, params, pre, normed, ahead)
 
 
+def column_starts(place, block):
+    chip, core = place[9] >> 1, place[9] & 1
+    owners = (chip * 2 + core, (1 - chip) * 2 + core, chip * 2 + 1 - core, (1 - chip) * 2 + 1 - core)
+    return [pl.multiple_of(owner * block, LANES) for owner in owners]
+
+
+def act_kernel(place, grads, *refs):
+    weights, out = refs[:-1], refs[-1]
+    size, block = weights[1].shape
+    utts, rows = grads.shape[0], grads.shape[1]
+    columns = [
+        jnp.concatenate([grads[utt, :, pl.ds(first, block)] for utt in range(utts)], 0)
+        for first in column_starts(place, block)
+    ]
+    for half in range(2):
+        for start in range(0, size, 384):
+            part = slice(start, start + 384)
+            whole = slice(half * size + start, half * size + start + 384)
+            tiles = (weights[0][whole, :], weights[1 + half][part, :], weights[3][whole, :], weights[4 + half][part, :])
+            total = jnp.zeros((utts * rows, 384), f32)
+            for column, tile in zip(columns, tiles):
+                total = total + lax.dot_general(
+                    column, tile, (((1,), (1,)), ((), ())), preferred_element_type=f32
+                )
+            for utt in range(utts):
+                out[utt, :, whole] = total[utt * rows : (utt + 1) * rows]
+
+
+def mixed_kernel(place, active, *refs):
+    weights, out = refs[:-1], refs[-1]
+    size, block = weights[1].shape
+    utts, rows = out.shape[0], out.shape[1]
+    first, second = active[:, :size], active[:, size:]
+    tiles = (
+        (weights[0][:size, :], weights[0][size:, :]),
+        (weights[1][...], weights[2][...]),
+        (weights[3][:size, :], weights[3][size:, :]),
+        (weights[4][...], weights[5][...]),
+    )
+    for column, (top, bottom) in zip(column_starts(place, block), tiles):
+        total = jnp.dot(first, top, preferred_element_type=f32)
+        total = total + jnp.dot(second, bottom, preferred_element_type=f32)
+        total = total.astype(bf16)
+        for utt in range(utts):
+            out[utt, :, pl.ds(column, block)] = total[utt * rows : (utt + 1) * rows]
+
+
+def with_weights(kernel, place, value, weights, shape, dtype):
+    smem, vmem = pl.BlockSpec(memory_space=pltpu.SMEM), pl.BlockSpec(memory_space=pltpu.VMEM)
+    return pl.pallas_call(
+        kernel,
+        in_specs=[smem] + [vmem] * (1 + len(weights)),
+        out_specs=vmem,
+        out_shape=jax.ShapeDtypeStruct(shape, dtype),
+        compiler_params=pltpu.CompilerParams(vmem_limit_bytes=28 << 20),
+        cost_estimate=pl.CostEstimate(flops=100_000_000, bytes_accessed=2_000_000, transcendentals=0),
+    )(place, value, *weights)
+
+
 def widen_kernel(place, value, *refs):
     refs[-1][0] = value[...].astype(f32)
 
@@ -594,7 +653,6 @@
         [lengths, jnp.stack([tm, fsdp]).astype(jnp.int32), jnp.array(table, jnp.int32)]
     )
 
-    whole_weight = lax.all_gather(out_weight, "fsdp", axis=1, tiled=True)
     before = moved(frames_in[:, rows - HALO :, :], 1)
     convolved, stats = depthwise(scalars, depth_kernel, before, frames_in)
 
@@ -608,10 +666,15 @@
         along(chip_stats, -1),
         along(chip_stats, 2),
     )
-    pieces, early_frames = lax.optimization_barrier((pieces, frames_in))
+    pieces, early_frames, columns, core_columns = lax.optimization_barrier(
+        (pieces, frames_in, out_weight, other_core(out_weight))
+    )
     pieces = in_plane(pieces)
+    low_rows = along(columns[:half], 1)
+    high_rows = along(columns[half:], -1)
     early = early_sums(scalars, before, early_frames, convolved, stats)
-    pieces, early = lax.optimization_barrier((pieces, early))
+    pieces, early, low_rows, high_rows = lax.optimization_barrier((pieces, early, low_rows, high_rows))
+    core_low, core_high = other_core(low_rows), other_core(high_rows)
     mine = in_vmem(moments_kernel, (2, half), lengths, pieces, scalars=1)
     params = in_vmem(
         params_kernel,
@@ -625,28 +688,22 @@
     )
 
     active, send_first, send_rest, keep_first, keep_rest = weight_terms(scalars, convolved, params, cotangent)
+    send_first, core_low, core_high = lax.optimization_barrier((send_first, core_low, core_high))
+    weights = (columns, low_rows, high_rows, core_columns, core_low, core_high)
     got_first, got_rest = other_core(send_first), other_core(send_rest)
     upward = (keep_first[:2] + got_first[:2].astype(f32)).astype(bf16)
     downward = (keep_first[2:] + got_first[2:].astype(f32)).astype(bf16)
     upward, downward, out_grads = lax.optimization_barrier((upward, downward, cotangent))
     below, above = along(upward, 1), along(downward, -1)
-    act_grad = lax.dot_general(
-        out_grads.reshape(utts * rows, channels),
-        whole_weight,
-        (((1,), (1,)), ((), ())),
-        preferred_element_type=f32,
-    ).reshape(frames_in.shape)
+    act_grad = with_weights(act_kernel, scalars, out_grads, weights, frames_in.shape, f32)
     sums, pre, normed, first_rows = late_sums(
         scalars, params, before, frames_in, convolved, act_grad, stats, early
     )
-    near_sums = sums[0] + other_core(sums[1])
-
     rest = keep_rest + got_rest.astype(f32)
     upward = (rest[0] + below[0].astype(f32)).astype(bf16)
     downward = (rest[1] + above[0].astype(f32)).astype(bf16)
-    upward, downward, near_sums, first_rows = lax.optimization_barrier(
-        (upward, downward, near_sums, first_rows)
-    )
+    upward, downward, sums = lax.optimization_barrier((upward, downward, sums))
+    near_sums = sums[0] + other_core(sums[1])
     base = jnp.concatenate([rest[2] + above[1].astype(f32), rest[3] + below[1].astype(f32)], 0)
     below, above = along(upward, 1), along(downward, -1)
     kept = (
@@ -657,7 +714,10 @@
     )
 
     outgoing = packed(base, below, above, kept, plane)
+    outgoing, active = lax.optimization_barrier((outgoing, active))
     incoming = in_plane(outgoing)
+    mixed = with_weights(mixed_kernel, scalars, active, weights, frames_in.shape, bf16)
+    incoming, mixed = lax.optimization_barrier((incoming, mixed))
     summed = jnp.sum(incoming.astype(f32), axis=0)
     weight_rows = half // plane
     ride = summed[weight_rows : weight_rows + 3] + summed[weight_rows + 3 : weight_rows + 6]
@@ -678,13 +738,12 @@
     frames_grad = frames_back(scalars, depth_kernel, back_params, pre, normed, ahead)
 
     mine = gathered.reshape(half, block)
-    mine, active, kernel_row = lax.optimization_barrier((mine, active, whole_rows[2:]))
+    mine, kernel_row = lax.optimization_barrier((mine, whole_rows[2:]))
     theirs = across(mine)
     kernel_row = kernel_row.reshape(channels // LANES, LANES)
     kernel_row = jnp.concatenate([kernel_row, kernel_row[: 16 - channels // LANES]], 0)
     kernel_rows = in_plane(jnp.broadcast_to(kernel_row, (plane, 16, LANES)))
     kernel_grad = kernel_rows[:, : channels // LANES].reshape(plane, channels)
-    mixed = jnp.dot(active, whole_weight, preferred_element_type=f32).astype(bf16).reshape(frames_in.shape)
     weight_grad = widened(scalars, theirs, 1, widened(scalars, mine, 0, None)).reshape(channels, block)
     return (mixed, frames_grad, weight_grad, kernel_grad, gain_grad, bias_grad)
 

time: 195 us -> 202 us (1.036); the launches traced: 195 us -> 199 us
  between operations: 15.3 us -> 1.98 us
  waiting for transfers between devices: 51.7 us -> 64 us
  matrix products: 8.39 us -> 0 us
  Pallas kernels: 41.7 us -> 48.5 us
  starting transfers between devices: 60.5 us -> 65.8 us
  local copies, waits for them, and re-layouts: 10.4 us -> 15.4 us
  other arithmetic: 6.62 us -> 3.73 us
    dot_general x2 -> x0, matrix products: 8.39 us -> none  [the longest x1 4.6 us: on_device(): jnp.dot(active, whole_weight, preferred_element_type=f32).astype(bf16)]
    pallas_call x0 -> x2, Pallas kernels: none -> 8.28 us  [with_weights(): pl.pallas_call(kernel, in_specs=[smem] + [vmem] * (1 + len(weights)), out...]
    ppermute x2, waiting for transfers between devices: 9.96 us -> 17.5 us  [moved(): lax.ppermute(value, 'tm', [(i, i + steps) for i in range(count) if 0 <= i...]
    unnamed x45 -> x61, local copies, waits for them, and re-layouts: 4.95 us -> 8.81 us
    ppermute x10 -> x12, waiting for transfers between devices: 14.6 us -> 18 us  [along(): return lax.ppermute(value, ('tm', 'fsdp'), pairs)]
    ppermute x10 -> x12, starting transfers between devices: 10.8 us -> 14.1 us  [along(): return lax.ppermute(value, ('tm', 'fsdp'), pairs)]
    add x1, other arithmetic: 2.34 us -> 0.2 us  [on_device(): rest = keep_rest + got_rest.astype(f32)]
    ppermute x2, starting transfers between devices: 11.3 us -> 9.24 us  [moved(): lax.ppermute(value, 'tm', [(i, i + steps) for i in range(count) if 0 <= i...]
  transfers between devices with their start and end apart: 26 -> 30, of which waited for: 12 -> 14; matrix products, arithmetic and copies ran while one was open for 11% -> 5% of each run, Pallas kernels for 20% -> 23%
where the time goes in v3:
time: 202 us; the launch traced here: 199 us
  starting transfers between devices  65.8 us (33%)
  waiting for transfers between devices  64 us (32%)
  Pallas kernels  48.5 us (24%)
  local copies, waits for them, and re-layouts  15.4 us (8%)
  other arithmetic  3.73 us (2%)
    all_to_all x4, starting transfers between devices, in_plane(): lax.all_to_all(value, 'tm', 0, 0, axis_index_groups=groups, tiled=True)  33.6 us
    all_to_all x4, waiting for transfers between devices, in_plane(): lax.all_to_all(value, 'tm', 0, 0, axis_index_groups=groups, tiled=True)  24.2 us
    ppermute x12, waiting for transfers between devices, along(): return lax.ppermute(value, ('tm', 'fsdp'), pairs)  18 us
    ppermute x2, waiting for transfers between devices, moved(): lax.ppermute(value, 'tm', [(i, i + steps) for i in range(count) if 0 <= i...  17.5 us
    ppermute x12, starting transfers between devices, along(): return lax.ppermute(value, ('tm', 'fsdp'), pairs)  14.1 us
    ppermute x2, starting transfers between devices, moved(): lax.ppermute(value, 'tm', [(i, i + steps) for i in range(count) if 0 <= i...  9.24 us
    unnamed x61, local copies, waits for them, and re-layouts  8.81 us
    pallas_call x2, Pallas kernels, with_weights(): pl.pallas_call(kernel, in_specs=[smem] + [vmem] * (1 + len(weights)), out...  8.28 us
  transfers between devices with their start and end apart: 30, of which 14 were waited for; matrix products, arithmetic and copies ran while one was open for 5% of the time, Pallas kernels for 23%

profile of v3, /device:TPU:8, one launch (start us, length us, event | category | flops | bytes accessed | tf_op | source)
XLA Modules:
  0.0 199.3 jit_solution(1622320249213375487)
XLA Ops:
  1.8 4.9 %collective-permute-start = (bf16[2,32,1536]{2,1,0:T(8,128)(2,1)S(1)}, bf16[2,32,1536]{2,1,0:T(8,128)(2,1)S(1)}, u32[]{:S(2)}, u32[]{:S(2)}) collective-permute-start(bf16[2,32,1536]{2,1,0:T(8,128)(2,1)S(1)} %slice.126), channel_id=1, source_target_pairs={{0,4},{4,8},{8,12},{12,16},{16,20},{20,24},{24,28},{28,32},{32,36}... | collective-permute-start | bytes 589832 | tf_op jit(solution)/shard_map/ppermute | solution.py:600
  7.5 9.9 %collective-permute-done.before = bf16[2,32,1536]{2,1,0:T(8,128)(2,1)S(1)} collective-permute-done((bf16[2,32,1536]{2,1,0:T(8,128)(2,1)S(1)}, bf16[2,32,1536]{2,1,0:T(8,128)(2,1)S(1)}, u32[]{:S(2)}, u32[]{:S(2)}) %collective-permute-start) | collective-permute-done | bytes 196640 | tf_op jit(solution)/shard_map/ppermute | solution.py:600
  19.4 5.2 %shard_map.127 = (f32[2,128,1536]{2,1,0:T(8,128)S(1)}, f32[2,3,768]{2,1,0:T(4,128)S(1)}) custom-call(s32[26]{0:T(128)S(1)} %pad_add_fusion.place, f32[32,1536]{1,0:T(8,128)S(1)} %copy-done.20, bf16[2,32,1536]{2,1,0:T(8,128)(2,1)S(1)} %collective-permute-done.before, bf16[2,128,1536]{2,1,0:T(8,128)(2,1)S(1)} %copy-done.2), custom_call_target="tpu_custom_call" | custom-call | flops 30000000 | bytes 3000000 | tf_op jit(solution)/shard_map/pallas_call | solution.py:131
  26.6 2.6 %collective-permute-start.3 = (f32[3,768]{1,0:T(4,128)S(1)}, f32[3,768]{1,0:T(4,128)S(1)}, u32[]{:S(2)}, u32[]{:S(2)}) collective-permute-start(f32[3,768]{1,0:T(4,128)S(1)} %shard_map.128.own), channel_id=1, source_target_pairs={{0,6},{1,7},{2,0},{3,1},{4,2},{5,3},{6,4},{7,5},{8,14},{9,15},{10,... | collective-permute-start | bytes 27656 | tf_op jit(solution)/shard_map/ppermute | solution.py:621
  29.3 1.7 collective-permute-done.2.first
  30.9 3.5 %collective-permute-done.4.third = f32[3,768]{1,0:T(4,128)S(1)} collective-permute-done((f32[3,768]{1,0:T(4,128)S(1)}, f32[3,768]{1,0:T(4,128)S(1)}, u32[]{:S(2)}, u32[]{:S(2)}) %collective-permute-start.4) | collective-permute-done | bytes 9248 | tf_op jit(solution)/shard_map/ppermute | solution.py:621
  36.4 3.2 %collective-permute-start.7 = (bf16[768,384]{1,0:T(8,128)(2,1)}, bf16[768,384]{1,0:T(8,128)(2,1)}, u32[]{:S(2)}, u32[]{:S(2)}) collective-permute-start(bf16[768,384]{1,0:T(8,128)(2,1)} %get-tuple-element.93), channel_id=1, source_target_pairs={{0,6},{1,7},{2,0},{3,1},{4,2},{5,3},{6,4},{7,5},{8,14},{9,15},{10,... | collective-permute-start | bytes 1769480 | tf_op jit(solution)/shard_map/ppermute | solution.py:621
  39.6 8.9 %all-to-all-start = ((f32[32,16,128]{2,1,0:T(8,128)}), f32[32,16,128]{2,1,0:T(8,128)}, u32[]{:S(2)}, u32[]{:S(2)}) async-start(f32[32,16,128]{2,1,0:T(8,128)} %shard_map.129), calls=%async_computation | async-start | bytes 524288 | tf_op jit(solution)/shard_map/all_to_all | solution.py:627
  51.3 7.2 %shard_map.130.early = f32[64,1536]{1,0:T(8,128)S(1)} custom-call(s32[26]{0:T(128)S(1)} %pad_add_fusion.place, bf16[2,32,1536]{2,1,0:T(8,128)(2,1)S(1)} %copy-done.12, bf16[2,128,1536]{2,1,0:T(8,128)(2,1)S(1)} %copy-done.3, f32[2,128,1536]{2,1,0:T(8,128)S(1)} %get-tuple-element.43.convolved, f32[2,3,768]{2,1,0:T(4,128)S(1)} %copy-done.23), custom_call_target="tpu_custom_call" | custom-call | flops 30000000 | bytes 4000000 | tf_op jit(solution)/shard_map/pallas_call | solution.py:365
  62.8 3.2 %shard_map.133 = (bf16[256,1536]{1,0:T(8,128)(2,1)S(1)}, bf16[4,384,384]{2,1,0:T(8,128)(2,1)S(1)}, bf16[4,384,384]{2,1,0:T(8,128)(2,1)S(1)}) custom-call(s32[26]{0:T(128)S(1)} %pad_add_fusion.place, f32[2,128,1536]{2,1,0:T(8,128)S(1)} %get-tuple-element.43.convolved, f32[4,1536]{1,0:T(4,128)S(1)} %shard_map.132.params, bf16[2,128,1536]{2,1,0:T(8,128)(2,1)S(1)} %copy-done, ...), custom_call_target="tpu_custom_call" | custom-call | flops 603979776 | bytes 6000000 | tf_op jit(solution)/shard_map/pallas_call | solution.py:229
  66.7 2.8 %shard_map.134 = (f32[4,384,384]{2,1,0:T(8,128)S(1)}, f32[4,384,384]{2,1,0:T(8,128)S(1)}) custom-call(s32[26]{0:T(128)S(1)} %pad_add_fusion.place, bf16[256,1536]{1,0:T(8,128)(2,1)S(1)} %get-tuple-element.69.active, bf16[2,128,1536]{2,1,0:T(8,128)(2,1)S(1)} %copy-done, bf16[2,128,1536]{2,1,0:T(8,128)(2,1)S(1)} %copy-done), custom_call_target="tpu_custom_call" | custom-call | flops 603979776 | bytes 6000000 | tf_op jit(solution)/shard_map/pallas_call | solution.py:257
  69.9 2.0 %collective-permute-start.14 = (bf16[2,384,384]{2,1,0:T(8,128)(2,1)S(1)}, bf16[2,384,384]{2,1,0:T(8,128)(2,1)S(1)}, u32[]{:S(2)}, u32[]{:S(2)}) collective-permute-start(bf16[2,384,384]{2,1,0:T(8,128)(2,1)S(1)} %get-tuple-element.58), channel_id=1, source_target_pairs={{0,2},{1,3},{2,4},{3,5},{4,6},{5,7},{6,0},{7,1},{8,10},{9,11},{10,... | collective-permute-start | bytes 1769480 | tf_op jit(solution)/shard_map/ppermute | solution.py:621
  72.2 4.0 %shard_map.135.act_grad = f32[2,128,1536]{2,1,0:T(8,128)S(1)} custom-call(s32[26]{0:T(128)S(1)} %pad_add_fusion.place, bf16[2,128,1536]{2,1,0:T(8,128)(2,1)S(1)} %copy-done, bf16[1536,384]{1,0:T(8,128)(2,1)S(1)} %copy-done.1, bf16[768,384]{1,0:T(8,128)(2,1)} %collective-permute-done.6.refs_1_, bf16[768,384]{1,0:T(8,128)(2,1)} %collective-permute-done.7.refs_2_, ...), custom_call_target="tpu_custom_call" | custom-call | flops 100000000 | bytes 2000000 | tf_op jit(solution)/shard_map/pallas_call | solution.py:565
  76.2 7.5 %shard_map.136 = (f32[2,2,2,72,384]{4,3,2,1,0:T(8,128)S(1)}, f32[2,128,1536]{2,1,0:T(8,128)S(1)}, f32[2,128,1536]{2,1,0:T(8,128)S(1)}, bf16[4,32,1536]{2,1,0:T(8,128)(2,1)S(1)}) custom-call(s32[26]{0:T(128)S(1)} %pad_add_fusion.place, f32[4,1536]{1,0:T(4,128)S(1)} %shard_map.132.params, bf16[2,32,1536]{2,1,0:T(8,128)(2,1)S(1)} %copy-done.13, ...), custom_call_target="tpu_custom_call" | custom-call | flops 40000000 | bytes 10000000 | tf_op jit(solution)/shard_map/pallas_call | solution.py:439
  87.5 3.0 %collective-permute-start.16 = (bf16[384,384]{1,0:T(8,128)(2,1)S(1)}, bf16[384,384]{1,0:T(8,128)(2,1)S(1)}, u32[]{:S(2)}, u32[]{:S(2)}) collective-permute-start(bf16[384,384]{1,0:T(8,128)(2,1)S(1)} %get-tuple-element.66), channel_id=1, source_target_pairs={{0,6},{1,7},{2,0},{3,1},{4,2},{5,3},{6,4},{7,5},{8,14},{9,15},{10,... | collective-permute-start | bytes 884744 | tf_op jit(solution)/shard_map/ppermute | solution.py:621
  92.8 9.1 %collective-permute-done.20 = f32[72,384]{1,0:T(8,128)S(1)} collective-permute-done((f32[72,384]{1,0:T(8,128)S(1)}, f32[72,384]{1,0:T(8,128)S(1)}, u32[]{:S(2)}, u32[]{:S(2)}) %collective-permute-start.20) | collective-permute-done | bytes 110624 | tf_op jit(solution)/shard_map/ppermute | solution.py:621
  102.6 1.7 shard_map.137
  104.3 10.0 %all-to-all-start.1 = ((bf16[32,32,384]{2,1,0:T(8,128)(2,1)}), bf16[32,32,384]{2,1,0:T(8,128)(2,1)}, u32[]{:S(2)}, u32[]{:S(2)}) async-start(bf16[32,32,384]{2,1,0:T(8,128)(2,1)} %shard_map.137), calls=%async_computation.1 | async-start | bytes 1572864 | tf_op jit(solution)/shard_map/all_to_all | solution.py:627
  115.6 4.3 %shard_map.138 = bf16[2,128,1536]{2,1,0:T(8,128)(2,1)} custom-call(s32[26]{0:T(128)S(1)} %pad_add_fusion.place, bf16[256,1536]{1,0:T(8,128)(2,1)S(1)} %copy-done.6, bf16[1536,384]{1,0:T(8,128)(2,1)S(1)} %copy-done.1, bf16[768,384]{1,0:T(8,128)(2,1)} %collective-permute-done.6.refs_1_, bf16[768,384]{1,0:T(8,128)(2,1)} %collective-permute-done.7.refs_2_, ...), custom_call_target="tpu_custom_call" | custom-call | flops 100000000 | bytes 2000000 | tf_op jit(solution)/shard_map/pallas_call | solution.py:565
  119.9 15.1 %all-to-all-done.1 = bf16[32,32,384]{2,1,0:T(8,128)(2,1)} async-done(((bf16[32,32,384]{2,1,0:T(8,128)(2,1)}), bf16[32,32,384]{2,1,0:T(8,128)(2,1)}, u32[]{:S(2)}, u32[]{:S(2)}) %all-to-all-start.1) | async-done | bytes 786464 | tf_op jit(solution)/shard_map/all_to_all | solution.py:627
  138.0 7.4 %all-to-all-start.2 = ((bf16[32,24,384]{2,1,0:T(8,128)(2,1)}), bf16[32,24,384]{2,1,0:T(8,128)(2,1)S(1)}, u32[]{:S(2)}, u32[]{:S(2)}) async-start(bf16[32,24,384]{2,1,0:T(8,128)(2,1)} %broadcast_in_dim.22), calls=%async_computation.2 | async-start | bytes 1179648 | tf_op jit(solution)/shard_map/all_to_all | solution.py:627
  147.1 3.6 %collective-permute-start.23 = (f32[2,3,384]{2,0,1:T(2,128)S(1)}, f32[2,3,384]{2,0,1:T(2,128)S(1)}, u32[]{:S(2)}, u32[]{:S(2)}) collective-permute-start(f32[2,3,384]{2,0,1:T(2,128)S(1)} %maximum_select_fusion.2), channel_id=1, source_target_pairs={{0,2},{2,0},{1,3},{3,1},{4,6},{6,4},{5,7},{7,5},{8,10},{10,8},{9,1... | collective-permute-start | bytes 27656 | tf_op jit(solution)/shard_map/ppermute | solution.py:608
  150.7 1.6 collective-permute-done.23
  152.4 9.1 %all-to-all-done.2 = bf16[32,24,384]{2,1,0:T(8,128)(2,1)S(1)} async-done(((bf16[32,24,384]{2,1,0:T(8,128)(2,1)}), bf16[32,24,384]{2,1,0:T(8,128)(2,1)S(1)}, u32[]{:S(2)}, u32[]{:S(2)}) %all-to-all-start.2) | async-done | bytes 589856 | tf_op jit(solution)/shard_map/all_to_all | solution.py:627
  161.5 3.2 %collective-permute-start.25 = (bf16[768,384]{1,0:T(8,128)(2,1)S(1)}, bf16[768,384]{1,0:T(8,128)(2,1)S(1)}, u32[]{:S(2)}, u32[]{:S(2)}) collective-permute-start(bf16[768,384]{1,0:T(8,128)(2,1)S(1)} %bitcast.51), channel_id=1, source_target_pairs={{0,4},{4,0},{8,12},{12,8},{16,20},{20,16},{24,28},{28,24},{32,36},... | collective-permute-start | bytes 1769480 | tf_op jit(solution)/shard_map/ppermute | solution.py:612
  165.5 7.3 %all-to-all-start.3 = ((f32[32,16,128]{2,1,0:T(8,128)}), f32[32,16,128]{2,1,0:T(8,128)}, u32[]{:S(2)}, u32[]{:S(2)}) async-start(f32[32,16,128]{2,1,0:T(8,128)} %broadcast_in_dim.23), calls=%async_computation.3 | async-start | bytes 524288 | tf_op jit(solution)/shard_map/all_to_all | solution.py:627
  172.8 4.3 %collective-permute-start.24 = (bf16[4,32,1536]{2,1,0:T(8,128)(2,1)}, bf16[4,32,1536]{2,1,0:T(8,128)(2,1)S(1)}, u32[]{:S(2)}, u32[]{:S(2)}) collective-permute-start(bf16[4,32,1536]{2,1,0:T(8,128)(2,1)} %copy-done.27), channel_id=1, source_target_pairs={{4,0},{8,4},{12,8},{16,12},{20,16},{24,20},{28,24},{32,28},{36,32}... | collective-permute-start | bytes 1179656 | tf_op jit(solution)/shard_map/ppermute | solution.py:600
  178.4 7.6 %collective-permute-done.24.ahead = bf16[4,32,1536]{2,1,0:T(8,128)(2,1)S(1)} collective-permute-done((bf16[4,32,1536]{2,1,0:T(8,128)(2,1)}, bf16[4,32,1536]{2,1,0:T(8,128)(2,1)S(1)}, u32[]{:S(2)}, u32[]{:S(2)}) %collective-permute-start.24) | collective-permute-done | bytes 393248 | tf_op jit(solution)/shard_map/ppermute | solution.py:600
  187.4 7.0 %shard_map.139 = bf16[2,128,1536]{2,1,0:T(8,128)(2,1)} custom-call(s32[26]{0:T(128)S(1)} %pad_add_fusion.place, f32[32,1536]{1,0:T(8,128)S(1)} %copy-done.21, f32[3,1536]{1,0:T(4,128)S(1)} %pad_maximum_fusion.1.params, f32[2,128,1536]{2,1,0:T(8,128)S(1)} %copy-done.17, f32[2,128,1536]{2,1,0:T(8,128)S(1)} %copy-done.19, ...), custom_call_target="tpu_custom_call" | custom-call | flops 30000000 | bytes 5000000 | tf_op jit(solution)/shard_map/pallas_call | solution.py:495
  194.4 1.6 shard_map.140.refs_0_
  196.0 1.7 copy.19
  197.7 1.6 shard_map.141
  (149 shorter events, 31.5 us)
Async XLA Ops:
  0.6 34.6 %collective-permute-start.5 = (bf16[1536,384]{1,0:T(8,128)(2,1)}, bf16[1536,384]{1,0:T(8,128)(2,1)}, u32[]{:S(2)}, u32[]{:S(2)}) collective-permute-start(bf16[1536,384]{1,0:T(8,128)(2,1)} %refs_0_.1), channel_id=1, source_target_pairs={{0,1},{1,0},{2,3},{3,2},{4,5},{5,4},{6,7},{7,6},{8,9},{9,8},{10,11... | collective-permute-start | bytes 3538952 | tf_op jit(solution)/shard_map/ppermute | solution.py:604
  1.8 15.6 %collective-permute-start = (bf16[2,32,1536]{2,1,0:T(8,128)(2,1)S(1)}, bf16[2,32,1536]{2,1,0:T(8,128)(2,1)S(1)}, u32[]{:S(2)}, u32[]{:S(2)}) collective-permute-start(bf16[2,32,1536]{2,1,0:T(8,128)(2,1)S(1)} %slice.126), channel_id=1, source_target_pairs={{0,4},{4,8},{8,12},{12,16},{16,20},{20,24},{24,28},{28,32},{32,36}... | collective-permute-start | bytes 589832 | tf_op jit(solution)/shard_map/ppermute | solution.py:600
  24.7 1.3 collective-permute-start.1
  26.0 5.0 %collective-permute-start.2 = (f32[3,768]{1,0:T(4,128)S(1)}, f32[3,768]{1,0:T(4,128)S(1)}, u32[]{:S(2)}, u32[]{:S(2)}) collective-permute-start(f32[3,768]{1,0:T(4,128)S(1)} %shard_map.128.own), channel_id=1, source_target_pairs={{0,2},{1,3},{2,4},{3,5},{4,6},{5,7},{6,0},{7,1},{8,10},{9,11},{10,... | collective-permute-start | bytes 27656 | tf_op jit(solution)/shard_map/ppermute | solution.py:621
  26.6 4.3 %collective-permute-start.3 = (f32[3,768]{1,0:T(4,128)S(1)}, f32[3,768]{1,0:T(4,128)S(1)}, u32[]{:S(2)}, u32[]{:S(2)}) collective-permute-start(f32[3,768]{1,0:T(4,128)S(1)} %shard_map.128.own), channel_id=1, source_target_pairs={{0,6},{1,7},{2,0},{3,1},{4,2},{5,3},{6,4},{7,5},{8,14},{9,15},{10,... | collective-permute-start | bytes 27656 | tf_op jit(solution)/shard_map/ppermute | solution.py:621
  29.3 5.2 %collective-permute-start.4 = (f32[3,768]{1,0:T(4,128)S(1)}, f32[3,768]{1,0:T(4,128)S(1)}, u32[]{:S(2)}, u32[]{:S(2)}) collective-permute-start(f32[3,768]{1,0:T(4,128)S(1)} %shard_map.128.own), channel_id=1, source_target_pairs={{0,4},{1,5},{2,6},{3,7},{4,0},{5,1},{6,2},{7,3},{8,12},{9,13},{10,... | collective-permute-start | bytes 27656 | tf_op jit(solution)/shard_map/ppermute | solution.py:621
  36.4 22.9 %collective-permute-start.6 = (bf16[768,384]{1,0:T(8,128)(2,1)}, bf16[768,384]{1,0:T(8,128)(2,1)}, u32[]{:S(2)}, u32[]{:S(2)}) collective-permute-start(bf16[768,384]{1,0:T(8,128)(2,1)} %get-tuple-element.94), channel_id=1, source_target_pairs={{0,2},{1,3},{2,4},{3,5},{4,6},{5,7},{6,0},{7,1},{8,10},{9,11},{10,... | collective-permute-start | bytes 1769480 | tf_op jit(solution)/shard_map/ppermute | solution.py:621
  36.4 22.9 %collective-permute-start.7 = (bf16[768,384]{1,0:T(8,128)(2,1)}, bf16[768,384]{1,0:T(8,128)(2,1)}, u32[]{:S(2)}, u32[]{:S(2)}) collective-permute-start(bf16[768,384]{1,0:T(8,128)(2,1)} %get-tuple-element.93), channel_id=1, source_target_pairs={{0,6},{1,7},{2,0},{3,1},{4,2},{5,3},{6,4},{7,5},{8,14},{9,15},{10,... | collective-permute-start | bytes 1769480 | tf_op jit(solution)/shard_map/ppermute | solution.py:621
  39.6 19.7 %all-to-all-start = ((f32[32,16,128]{2,1,0:T(8,128)}), f32[32,16,128]{2,1,0:T(8,128)}, u32[]{:S(2)}, u32[]{:S(2)}) async-start(f32[32,16,128]{2,1,0:T(8,128)} %shard_map.129), calls=%async_computation | async-start | bytes 524288 | tf_op jit(solution)/shard_map/all_to_all | solution.py:627
  59.3 6.8 %collective-permute-start.10 = (bf16[768,384]{1,0:T(8,128)(2,1)}, bf16[768,384]{1,0:T(8,128)(2,1)S(1)}, u32[]{:S(2)}, u32[]{:S(2)}) collective-permute-start(bf16[768,384]{1,0:T(8,128)(2,1)} %collective-permute-done.6.refs_1_), channel_id=1, source_target_pairs={{0,1},{1,0},{2,3},{3,2},{4,5},{5,4},{6,7},{7,6},{8,9},{9,8},{10,11... | collective-permute-start | bytes 1769480 | tf_op jit(solution)/shard_map/ppermute | solution.py:604
  59.4 6.7 %collective-permute-start.11 = (bf16[768,384]{1,0:T(8,128)(2,1)}, bf16[768,384]{1,0:T(8,128)(2,1)S(1)}, u32[]{:S(2)}, u32[]{:S(2)}) collective-permute-start(bf16[768,384]{1,0:T(8,128)(2,1)} %collective-permute-done.7.refs_2_), channel_id=1, source_target_pairs={{0,1},{1,0},{2,3},{3,2},{4,5},{5,4},{6,7},{7,6},{8,9},{9,8},{10,11... | collective-permute-start | bytes 1769480 | tf_op jit(solution)/shard_map/ppermute | solution.py:604
  60.9 1.3 collective-permute-start.8
  66.1 3.4 %collective-permute-start.12 = (bf16[4,384,384]{2,1,0:T(8,128)(2,1)S(1)}, bf16[4,384,384]{2,1,0:T(8,128)(2,1)S(1)}, u32[]{:S(2)}, u32[]{:S(2)}) collective-permute-start(bf16[4,384,384]{2,1,0:T(8,128)(2,1)S(1)} %get-tuple-element.56), channel_id=1, source_target_pairs={{0,1},{1,0},{2,3},{3,2},{4,5},{5,4},{6,7},{7,6},{8,9},{9,8},{10,11... | collective-permute-start | bytes 3538952 | tf_op jit(solution)/shard_map/ppermute | solution.py:604
  66.4 5.6 %collective-permute-start.9 = (bf16[4,384,384]{2,1,0:T(8,128)(2,1)S(1)}, bf16[4,384,384]{2,1,0:T(8,128)(2,1)S(1)}, u32[]{:S(2)}, u32[]{:S(2)}) collective-permute-start(bf16[4,384,384]{2,1,0:T(8,128)(2,1)S(1)} %get-tuple-element.51), channel_id=1, source_target_pairs={{0,1},{1,0},{2,3},{3,2},{4,5},{5,4},{6,7},{7,6},{8,9},{9,8},{10,11... | collective-permute-start | bytes 3538952 | tf_op jit(solution)/shard_map/ppermute | solution.py:604
  69.8 15.5 %collective-permute-start.13 = (bf16[2,384,384]{2,1,0:T(8,128)(2,1)S(1)}, bf16[2,384,384]{2,1,0:T(8,128)(2,1)S(1)}, u32[]{:S(2)}, u32[]{:S(2)}) collective-permute-start(bf16[2,384,384]{2,1,0:T(8,128)(2,1)S(1)} %get-tuple-element.57), channel_id=1, source_target_pairs={{0,6},{1,7},{2,0},{3,1},{4,2},{5,3},{6,4},{7,5},{8,14},{9,15},{10,... | collective-permute-start | bytes 1769480 | tf_op jit(solution)/shard_map/ppermute | solution.py:621
  69.9 16.9 %collective-permute-start.14 = (bf16[2,384,384]{2,1,0:T(8,128)(2,1)S(1)}, bf16[2,384,384]{2,1,0:T(8,128)(2,1)S(1)}, u32[]{:S(2)}, u32[]{:S(2)}) collective-permute-start(bf16[2,384,384]{2,1,0:T(8,128)(2,1)S(1)} %get-tuple-element.58), channel_id=1, source_target_pairs={{0,2},{1,3},{2,4},{3,5},{4,6},{5,7},{6,0},{7,1},{8,10},{9,11},{10,... | collective-permute-start | bytes 1769480 | tf_op jit(solution)/shard_map/ppermute | solution.py:621
  87.1 3.4 %collective-permute-start.17 = (f32[2,2,72,384]{3,2,1,0:T(8,128)S(1)}, f32[2,2,72,384]{3,2,1,0:T(8,128)S(1)}, u32[]{:S(2)}, u32[]{:S(2)}) collective-permute-start(f32[2,2,72,384]{3,2,1,0:T(8,128)S(1)} %slice_bitcast_fusion), channel_id=1, source_target_pairs={{0,1},{1,0},{2,3},{3,2},{4,5},{5,4},{6,7},{7,6},{8,9},{9,8},{10,11... | collective-permute-start | bytes 1327112 | tf_op jit(solution)/shard_map/ppermute | solution.py:604
  87.2 15.4 %collective-permute-start.15 = (bf16[384,384]{1,0:T(8,128)(2,1)S(1)}, bf16[384,384]{1,0:T(8,128)(2,1)S(1)}, u32[]{:S(2)}, u32[]{:S(2)}) collective-permute-start(bf16[384,384]{1,0:T(8,128)(2,1)S(1)} %get-tuple-element.65), channel_id=1, source_target_pairs={{0,2},{1,3},{2,4},{3,5},{4,6},{5,7},{6,0},{7,1},{8,10},{9,11},{10,... | collective-permute-start | bytes 884744 | tf_op jit(solution)/shard_map/ppermute | solution.py:621
  87.5 15.1 %collective-permute-start.16 = (bf16[384,384]{1,0:T(8,128)(2,1)S(1)}, bf16[384,384]{1,0:T(8,128)(2,1)S(1)}, u32[]{:S(2)}, u32[]{:S(2)}) collective-permute-start(bf16[384,384]{1,0:T(8,128)(2,1)S(1)} %get-tuple-element.66), channel_id=1, source_target_pairs={{0,6},{1,7},{2,0},{3,1},{4,2},{5,3},{6,4},{7,5},{8,14},{9,15},{10,... | collective-permute-start | bytes 884744 | tf_op jit(solution)/shard_map/ppermute | solution.py:621
  90.6 11.2 %collective-permute-start.20 = (f32[72,384]{1,0:T(8,128)S(1)}, f32[72,384]{1,0:T(8,128)S(1)}, u32[]{:S(2)}, u32[]{:S(2)}) collective-permute-start(f32[72,384]{1,0:T(8,128)S(1)} %get-tuple-element.96), channel_id=1, source_target_pairs={{0,6},{1,7},{2,0},{3,1},{4,2},{5,3},{6,4},{7,5},{8,14},{9,15},{10,... | collective-permute-start | bytes 331784 | tf_op jit(solution)/shard_map/ppermute | solution.py:621
  90.7 11.2 %collective-permute-start.19 = (f32[72,384]{1,0:T(8,128)S(1)}, f32[72,384]{1,0:T(8,128)S(1)}, u32[]{:S(2)}, u32[]{:S(2)}) collective-permute-start(f32[72,384]{1,0:T(8,128)S(1)} %get-tuple-element.97), channel_id=1, source_target_pairs={{0,4},{1,5},{2,6},{3,7},{4,0},{5,1},{6,2},{7,3},{8,12},{9,13},{10,... | collective-permute-start | bytes 331784 | tf_op jit(solution)/shard_map/ppermute | solution.py:621
  91.8 10.8 %collective-permute-start.18 = (f32[72,384]{1,0:T(8,128)S(1)}, f32[72,384]{1,0:T(8,128)S(1)}, u32[]{:S(2)}, u32[]{:S(2)}) collective-permute-start(f32[72,384]{1,0:T(8,128)S(1)} %get-tuple-element.95), channel_id=1, source_target_pairs={{0,2},{1,3},{2,4},{3,5},{4,6},{5,7},{6,0},{7,1},{8,10},{9,11},{10,... | collective-permute-start | bytes 331784 | tf_op jit(solution)/shard_map/ppermute | solution.py:621
  104.3 30.7 %all-to-all-start.1 = ((bf16[32,32,384]{2,1,0:T(8,128)(2,1)}), bf16[32,32,384]{2,1,0:T(8,128)(2,1)}, u32[]{:S(2)}, u32[]{:S(2)}) async-start(bf16[32,32,384]{2,1,0:T(8,128)(2,1)} %shard_map.137), calls=%async_computation.1 | async-start | bytes 1572864 | tf_op jit(solution)/shard_map/all_to_all | solution.py:627
  136.2 9.2 %collective-permute-start.21 = (f32[3,384]{1,0:T(4,128)S(1)}, f32[3,384]{1,0:T(4,128)S(1)}, u32[]{:S(2)}, u32[]{:S(2)}) collective-permute-start(f32[3,384]{1,0:T(4,128)S(1)} %slice_add_fusion.4), channel_id=1, source_target_pairs={{0,4},{4,0},{8,12},{12,8},{16,20},{20,16},{24,28},{28,24},{32,36},... | collective-permute-start | bytes 13832 | tf_op jit(solution)/shard_map/ppermute | solution.py:612
  138.0 48.0 %copy-start.17 = (f32[2,128,1536]{2,1,0:T(8,128)S(1)}, f32[2,128,1536]{2,1,0:T(8,128)}, u32[]{:S(2)}) copy-start(f32[2,128,1536]{2,1,0:T(8,128)} %copy-done.16) | copy-start | bytes 4718596
  138.0 48.0 %copy-start.21 = (f32[32,1536]{1,0:T(8,128)S(1)}, f32[32,1536]{1,0:T(8,128)}, u32[]{:S(2)}) copy-start(f32[32,1536]{1,0:T(8,128)} %taps.3) | copy-start | bytes 589828
  138.0 23.5 %all-to-all-start.2 = ((bf16[32,24,384]{2,1,0:T(8,128)(2,1)}), bf16[32,24,384]{2,1,0:T(8,128)(2,1)S(1)}, u32[]{:S(2)}, u32[]{:S(2)}) async-start(bf16[32,24,384]{2,1,0:T(8,128)(2,1)} %broadcast_in_dim.22), calls=%async_computation.2 | async-start | bytes 1179648 | tf_op jit(solution)/shard_map/all_to_all | solution.py:627
  145.6 1.5 collective-permute-start.22
  147.1 5.2 %collective-permute-start.23 = (f32[2,3,384]{2,0,1:T(2,128)S(1)}, f32[2,3,384]{2,0,1:T(2,128)S(1)}, u32[]{:S(2)}, u32[]{:S(2)}) collective-permute-start(f32[2,3,384]{2,0,1:T(2,128)S(1)} %maximum_select_fusion.2), channel_id=1, source_target_pairs={{0,2},{2,0},{1,3},{3,1},{4,6},{6,4},{5,7},{7,5},{8,10},{10,8},{9,1... | collective-permute-start | bytes 27656 | tf_op jit(solution)/shard_map/ppermute | solution.py:608
  161.5 36.2 %collective-permute-start.25 = (bf16[768,384]{1,0:T(8,128)(2,1)S(1)}, bf16[768,384]{1,0:T(8,128)(2,1)S(1)}, u32[]{:S(2)}, u32[]{:S(2)}) collective-permute-start(bf16[768,384]{1,0:T(8,128)(2,1)S(1)} %bitcast.51), channel_id=1, source_target_pairs={{0,4},{4,0},{8,12},{12,8},{16,20},{20,16},{24,28},{28,24},{32,36},... | collective-permute-start | bytes 1769480 | tf_op jit(solution)/shard_map/ppermute | solution.py:612
  165.5 30.5 %all-to-all-start.3 = ((f32[32,16,128]{2,1,0:T(8,128)}), f32[32,16,128]{2,1,0:T(8,128)}, u32[]{:S(2)}, u32[]{:S(2)}) async-start(f32[32,16,128]{2,1,0:T(8,128)} %broadcast_in_dim.23), calls=%async_computation.3 | async-start | bytes 524288 | tf_op jit(solution)/shard_map/all_to_all | solution.py:627
  172.8 13.2 %collective-permute-start.24 = (bf16[4,32,1536]{2,1,0:T(8,128)(2,1)}, bf16[4,32,1536]{2,1,0:T(8,128)(2,1)S(1)}, u32[]{:S(2)}, u32[]{:S(2)}) collective-permute-start(bf16[4,32,1536]{2,1,0:T(8,128)(2,1)} %copy-done.27), channel_id=1, source_target_pairs={{4,0},{8,4},{12,8},{16,12},{20,16},{24,20},{28,24},{32,28},{36,32}... | collective-permute-start | bytes 1179656 | tf_op jit(solution)/shard_map/ppermute | solution.py:600
  (27 other events, 190.4 us)

commit v4 on v3

--- a/solution.py
+++ b/solution.py
@@ -714,17 +714,16 @@
     )
 
     outgoing = packed(base, below, above, kept, plane)
-    outgoing, active = lax.optimization_barrier((outgoing, active))
     incoming = in_plane(outgoing)
-    mixed = with_weights(mixed_kernel, scalars, active, weights, frames_in.shape, bf16)
-    incoming, mixed = lax.optimization_barrier((incoming, mixed))
     summed = jnp.sum(incoming.astype(f32), axis=0)
     weight_rows = half // plane
     ride = summed[weight_rows : weight_rows + 3] + summed[weight_rows + 3 : weight_rows + 6]
     piece = summed[:weight_rows].astype(bf16)
-    piece, ride, first_rows = lax.optimization_barrier((piece, ride, first_rows))
+    piece, ride, first_rows, active = lax.optimization_barrier((piece, ride, first_rows, active))
     ahead = moved(first_rows, -1)
     gathered = in_plane(jnp.broadcast_to(piece, (plane, *piece.shape)))
+    mixed = with_weights(mixed_kernel, scalars, active, weights, frames_in.shape, bf16)
+    gathered, ahead, mixed = lax.optimization_barrier((gathered, ahead, mixed))
 
     far_ride = across(ride)
     by_high = jnp.where(high == 0, jnp.stack([ride, far_ride]), jnp.stack([far_ride, ride]))

time: 202 us -> 198 us (0.980)
  waiting for transfers between devices: 64 us -> 52.3 us
  starting transfers between devices: 65.8 us -> 69.2 us
    all_to_all x4, waiting for transfers between devices: 24.2 us -> 19.4 us  [in_plane(): lax.all_to_all(value, 'tm', 0, 0, axis_index_groups=groups, tiled=True)]
    ppermute x2, waiting for transfers between devices: 17.5 us -> 13.4 us  [moved(): lax.ppermute(value, 'tm', [(i, i + steps) for i in range(count) if 0 <= i...]
    ppermute x2, starting transfers between devices: 9.24 us -> 12.5 us  [moved(): lax.ppermute(value, 'tm', [(i, i + steps) for i in range(count) if 0 <= i...]
    ppermute x1, starting transfers between devices: 3.58 us -> 1.17 us  [other_chip(): return lax.ppermute(value, 'fsdp', [(0, 2), (2, 0), (1, 3), (3, 1)])]
    unnamed x61 -> x63, local copies, waits for them, and re-layouts: 8.81 us -> 7.23 us
  transfers between devices with their start and end apart: 30 -> 30, of which waited for: 14 -> 11; matrix products, arithmetic and copies ran while one was open for 5% -> 7% of each run, Pallas kernels for 23% -> 24%
where the time goes in v4:
time: 198 us; the launch traced here: 195 us
  starting transfers between devices  69.2 us (35%)
  waiting for transfers between devices  52.3 us (26%)
  Pallas kernels  49.4 us (25%)
  local copies, waits for them, and re-layouts  17.2 us (9%)
  other arithmetic  5.25 us (3%)
    all_to_all x4, starting transfers between devices, in_plane(): lax.all_to_all(value, 'tm', 0, 0, axis_index_groups=groups, tiled=True)  35 us
    all_to_all x4, waiting for transfers between devices, in_plane(): lax.all_to_all(value, 'tm', 0, 0, axis_index_groups=groups, tiled=True)  19.4 us
    ppermute x12, waiting for transfers between devices, along(): return lax.ppermute(value, ('tm', 'fsdp'), pairs)  18 us
    ppermute x12, starting transfers between devices, along(): return lax.ppermute(value, ('tm', 'fsdp'), pairs)  14.1 us
    ppermute x2, waiting for transfers between devices, moved(): lax.ppermute(value, 'tm', [(i, i + steps) for i in range(count) if 0 <= i...  13.4 us
    ppermute x2, starting transfers between devices, moved(): lax.ppermute(value, 'tm', [(i, i + steps) for i in range(count) if 0 <= i...  12.5 us
    pallas_call x2, Pallas kernels, with_weights(): pl.pallas_call(kernel, in_specs=[smem] + [vmem] * (1 + len(weights)), out...  8.31 us
    pallas_call x1, Pallas kernels, late_sums(): pl.pallas_call(late_kernel, grid_spec=pltpu.PrefetchScalarGridSpec(num_sc...  7.5 us
  transfers between devices with their start and end apart: 30, of which 11 were waited for; matrix products, arithmetic and copies ran while one was open for 7% of the time, Pallas kernels for 24%

profile of v4, /device:TPU:8, one launch (start us, length us, event | category | flops | bytes accessed | tf_op | source)
XLA Modules:
  0.0 195.3 jit_solution(17949000339577588403)
XLA Ops:
  1.8 4.9 %collective-permute-start = (bf16[2,32,1536]{2,1,0:T(8,128)(2,1)S(1)}, bf16[2,32,1536]{2,1,0:T(8,128)(2,1)S(1)}, u32[]{:S(2)}, u32[]{:S(2)}) collective-permute-start(bf16[2,32,1536]{2,1,0:T(8,128)(2,1)S(1)} %slice.126), channel_id=1, source_target_pairs={{0,4},{4,8},{8,12},{12,16},{16,20},{20,24},{24,28},{28,32},{32,36}... | collective-permute-start | bytes 589832 | tf_op jit(solution)/shard_map/ppermute | solution.py:600
  7.5 9.9 %collective-permute-done.before = bf16[2,32,1536]{2,1,0:T(8,128)(2,1)S(1)} collective-permute-done((bf16[2,32,1536]{2,1,0:T(8,128)(2,1)S(1)}, bf16[2,32,1536]{2,1,0:T(8,128)(2,1)S(1)}, u32[]{:S(2)}, u32[]{:S(2)}) %collective-permute-start) | collective-permute-done | bytes 196640 | tf_op jit(solution)/shard_map/ppermute | solution.py:600
  19.4 5.2 %shard_map.127 = (f32[2,128,1536]{2,1,0:T(8,128)S(1)}, f32[2,3,768]{2,1,0:T(4,128)S(1)}) custom-call(s32[26]{0:T(128)S(1)} %pad_add_fusion.place, f32[32,1536]{1,0:T(8,128)S(1)} %copy-done.20, bf16[2,32,1536]{2,1,0:T(8,128)(2,1)S(1)} %collective-permute-done.before, bf16[2,128,1536]{2,1,0:T(8,128)(2,1)S(1)} %copy-done.2), custom_call_target="tpu_custom_call" | custom-call | flops 30000000 | bytes 3000000 | tf_op jit(solution)/shard_map/pallas_call | solution.py:131
  26.6 2.6 %collective-permute-start.3 = (f32[3,768]{1,0:T(4,128)S(1)}, f32[3,768]{1,0:T(4,128)S(1)}, u32[]{:S(2)}, u32[]{:S(2)}) collective-permute-start(f32[3,768]{1,0:T(4,128)S(1)} %shard_map.128.own), channel_id=1, source_target_pairs={{0,6},{1,7},{2,0},{3,1},{4,2},{5,3},{6,4},{7,5},{8,14},{9,15},{10,... | collective-permute-start | bytes 27656 | tf_op jit(solution)/shard_map/ppermute | solution.py:621
  29.3 1.7 collective-permute-done.2.first
  30.9 3.5 %collective-permute-done.4.third = f32[3,768]{1,0:T(4,128)S(1)} collective-permute-done((f32[3,768]{1,0:T(4,128)S(1)}, f32[3,768]{1,0:T(4,128)S(1)}, u32[]{:S(2)}, u32[]{:S(2)}) %collective-permute-start.4) | collective-permute-done | bytes 9248 | tf_op jit(solution)/shard_map/ppermute | solution.py:621
  36.4 3.2 %collective-permute-start.7 = (bf16[768,384]{1,0:T(8,128)(2,1)}, bf16[768,384]{1,0:T(8,128)(2,1)}, u32[]{:S(2)}, u32[]{:S(2)}) collective-permute-start(bf16[768,384]{1,0:T(8,128)(2,1)} %get-tuple-element.93), channel_id=1, source_target_pairs={{0,6},{1,7},{2,0},{3,1},{4,2},{5,3},{6,4},{7,5},{8,14},{9,15},{10,... | collective-permute-start | bytes 1769480 | tf_op jit(solution)/shard_map/ppermute | solution.py:621
  39.6 8.9 %all-to-all-start = ((f32[32,16,128]{2,1,0:T(8,128)}), f32[32,16,128]{2,1,0:T(8,128)}, u32[]{:S(2)}, u32[]{:S(2)}) async-start(f32[32,16,128]{2,1,0:T(8,128)} %shard_map.129), calls=%async_computation | async-start | bytes 524288 | tf_op jit(solution)/shard_map/all_to_all | solution.py:627
  51.3 7.2 %shard_map.130.early = f32[64,1536]{1,0:T(8,128)S(1)} custom-call(s32[26]{0:T(128)S(1)} %pad_add_fusion.place, bf16[2,32,1536]{2,1,0:T(8,128)(2,1)S(1)} %copy-done.12, bf16[2,128,1536]{2,1,0:T(8,128)(2,1)S(1)} %copy-done.3, f32[2,128,1536]{2,1,0:T(8,128)S(1)} %get-tuple-element.43.convolved, f32[2,3,768]{2,1,0:T(4,128)S(1)} %copy-done.25), custom_call_target="tpu_custom_call" | custom-call | flops 30000000 | bytes 4000000 | tf_op jit(solution)/shard_map/pallas_call | solution.py:365
  62.8 3.3 %shard_map.133 = (bf16[256,1536]{1,0:T(8,128)(2,1)S(1)}, bf16[4,384,384]{2,1,0:T(8,128)(2,1)S(1)}, bf16[4,384,384]{2,1,0:T(8,128)(2,1)S(1)}) custom-call(s32[26]{0:T(128)S(1)} %pad_add_fusion.place, f32[2,128,1536]{2,1,0:T(8,128)S(1)} %get-tuple-element.43.convolved, f32[4,1536]{1,0:T(4,128)S(1)} %shard_map.132.params, bf16[2,128,1536]{2,1,0:T(8,128)(2,1)S(1)} %copy-done, ...), custom_call_target="tpu_custom_call" | custom-call | flops 603979776 | bytes 6000000 | tf_op jit(solution)/shard_map/pallas_call | solution.py:229
  66.7 2.8 %shard_map.134 = (f32[4,384,384]{2,1,0:T(8,128)S(1)}, f32[4,384,384]{2,1,0:T(8,128)S(1)}) custom-call(s32[26]{0:T(128)S(1)} %pad_add_fusion.place, bf16[256,1536]{1,0:T(8,128)(2,1)S(1)} %get-tuple-element.71.active, bf16[2,128,1536]{2,1,0:T(8,128)(2,1)S(1)} %copy-done, bf16[2,128,1536]{2,1,0:T(8,128)(2,1)S(1)} %copy-done), custom_call_target="tpu_custom_call" | custom-call | flops 603979776 | bytes 6000000 | tf_op jit(solution)/shard_map/pallas_call | solution.py:257
  69.9 2.0 %collective-permute-start.14 = (bf16[2,384,384]{2,1,0:T(8,128)(2,1)S(1)}, bf16[2,384,384]{2,1,0:T(8,128)(2,1)S(1)}, u32[]{:S(2)}, u32[]{:S(2)}) collective-permute-start(bf16[2,384,384]{2,1,0:T(8,128)(2,1)S(1)} %get-tuple-element.58), channel_id=1, source_target_pairs={{0,2},{1,3},{2,4},{3,5},{4,6},{5,7},{6,0},{7,1},{8,10},{9,11},{10,... | collective-permute-start | bytes 1769480 | tf_op jit(solution)/shard_map/ppermute | solution.py:621
  72.2 4.0 %shard_map.135.act_grad = f32[2,128,1536]{2,1,0:T(8,128)S(1)} custom-call(s32[26]{0:T(128)S(1)} %pad_add_fusion.place, bf16[2,128,1536]{2,1,0:T(8,128)(2,1)S(1)} %copy-done, bf16[1536,384]{1,0:T(8,128)(2,1)S(1)} %copy-done.1, bf16[768,384]{1,0:T(8,128)(2,1)} %collective-permute-done.6.refs_1_, bf16[768,384]{1,0:T(8,128)(2,1)} %collective-permute-done.7.refs_2_, ...), custom_call_target="tpu_custom_call" | custom-call | flops 100000000 | bytes 2000000 | tf_op jit(solution)/shard_map/pallas_call | solution.py:565
  76.2 7.5 %shard_map.136 = (f32[2,2,2,72,384]{4,3,2,1,0:T(8,128)S(1)}, f32[2,128,1536]{2,1,0:T(8,128)S(1)}, f32[2,128,1536]{2,1,0:T(8,128)S(1)}, bf16[4,32,1536]{2,1,0:T(8,128)(2,1)S(1)}) custom-call(s32[26]{0:T(128)S(1)} %pad_add_fusion.place, f32[4,1536]{1,0:T(4,128)S(1)} %shard_map.132.params, bf16[2,32,1536]{2,1,0:T(8,128)(2,1)S(1)} %copy-done.13, ...), custom_call_target="tpu_custom_call" | custom-call | flops 40000000 | bytes 10000000 | tf_op jit(solution)/shard_map/pallas_call | solution.py:439
  83.8 1.5 collective-permute-done.13
  85.3 1.5 collective-permute-done.14
  87.5 3.0 %collective-permute-start.16 = (bf16[384,384]{1,0:T(8,128)(2,1)S(1)}, bf16[384,384]{1,0:T(8,128)(2,1)S(1)}, u32[]{:S(2)}, u32[]{:S(2)}) collective-permute-start(bf16[384,384]{1,0:T(8,128)(2,1)S(1)} %get-tuple-element.66), channel_id=1, source_target_pairs={{0,6},{1,7},{2,0},{3,1},{4,2},{5,3},{6,4},{7,5},{8,14},{9,15},{10,... | collective-permute-start | bytes 884744 | tf_op jit(solution)/shard_map/ppermute | solution.py:621
  92.8 9.0 %collective-permute-done.20 = f32[72,384]{1,0:T(8,128)S(1)} collective-permute-done((f32[72,384]{1,0:T(8,128)S(1)}, f32[72,384]{1,0:T(8,128)S(1)}, u32[]{:S(2)}, u32[]{:S(2)}) %collective-permute-start.20) | collective-permute-done | bytes 110624 | tf_op jit(solution)/shard_map/ppermute | solution.py:621
  102.6 1.7 shard_map.137
  104.3 9.8 %all-to-all-start.1 = ((bf16[32,32,384]{2,1,0:T(8,128)(2,1)}), bf16[32,32,384]{2,1,0:T(8,128)(2,1)S(1)}, u32[]{:S(2)}, u32[]{:S(2)}) async-start(bf16[32,32,384]{2,1,0:T(8,128)(2,1)} %shard_map.137), calls=%async_computation.1 | async-start | bytes 1572864 | tf_op jit(solution)/shard_map/all_to_all | solution.py:627
  115.3 19.4 %all-to-all-done.1 = bf16[32,32,384]{2,1,0:T(8,128)(2,1)S(1)} async-done(((bf16[32,32,384]{2,1,0:T(8,128)(2,1)}), bf16[32,32,384]{2,1,0:T(8,128)(2,1)S(1)}, u32[]{:S(2)}, u32[]{:S(2)}) %all-to-all-start.1) | async-done | bytes 786464 | tf_op jit(solution)/shard_map/all_to_all | solution.py:627
  136.9 1.3 stack.36
  139.1 7.3 %all-to-all-start.2 = ((bf16[32,24,384]{2,1,0:T(8,128)(2,1)}), bf16[32,24,384]{2,1,0:T(8,128)(2,1)}, u32[]{:S(2)}, u32[]{:S(2)}) async-start(bf16[32,24,384]{2,1,0:T(8,128)(2,1)} %broadcast_in_dim.20), calls=%async_computation.2 | async-start | bytes 1179648 | tf_op jit(solution)/shard_map/all_to_all | solution.py:627
  148.6 7.5 %collective-permute-start.21 = (bf16[4,32,1536]{2,1,0:T(8,128)(2,1)S(1)}, bf16[4,32,1536]{2,1,0:T(8,128)(2,1)S(1)}, u32[]{:S(2)}, u32[]{:S(2)}) collective-permute-start(bf16[4,32,1536]{2,1,0:T(8,128)(2,1)S(1)} %get-tuple-element.70), channel_id=1, source_target_pairs={{4,0},{8,4},{12,8},{16,12},{20,16},{24,20},{28,24},{32,28},{36,32}... | collective-permute-start | bytes 1179656 | tf_op jit(solution)/shard_map/ppermute | solution.py:600
  157.6 1.2 collective-permute-start.24
  158.8 4.4 %shard_map.138 = bf16[2,128,1536]{2,1,0:T(8,128)(2,1)} custom-call(s32[26]{0:T(128)S(1)} %pad_add_fusion.place, bf16[256,1536]{1,0:T(8,128)(2,1)S(1)} %copy-done.6, bf16[1536,384]{1,0:T(8,128)(2,1)S(1)} %copy-done.1, bf16[768,384]{1,0:T(8,128)(2,1)} %collective-permute-done.6.refs_1_, bf16[768,384]{1,0:T(8,128)(2,1)} %collective-permute-done.7.refs_2_, ...), custom_call_target="tpu_custom_call" | custom-call | flops 100000000 | bytes 2000000 | tf_op jit(solution)/shard_map/pallas_call | solution.py:565
  163.2 3.5 %collective-permute-done.21.ahead = bf16[4,32,1536]{2,1,0:T(8,128)(2,1)S(1)} collective-permute-done((bf16[4,32,1536]{2,1,0:T(8,128)(2,1)S(1)}, bf16[4,32,1536]{2,1,0:T(8,128)(2,1)S(1)}, u32[]{:S(2)}, u32[]{:S(2)}) %collective-permute-start.21) | collective-permute-done | bytes 393248 | tf_op jit(solution)/shard_map/ppermute | solution.py:600
  167.4 4.9 %collective-permute-start.25 = (bf16[768,384]{1,0:T(8,128)(2,1)}, bf16[768,384]{1,0:T(8,128)(2,1)S(1)}, u32[]{:S(2)}, u32[]{:S(2)}) collective-permute-start(bf16[768,384]{1,0:T(8,128)(2,1)} %bitcast.15.value), channel_id=1, source_target_pairs={{0,4},{4,0},{8,12},{12,8},{16,20},{20,16},{24,28},{28,24},{32,36},... | collective-permute-start | bytes 1769480 | tf_op jit(solution)/shard_map/ppermute | solution.py:612
  173.1 9.0 %all-to-all-start.3 = ((f32[32,16,128]{2,1,0:T(8,128)}), f32[32,16,128]{2,1,0:T(8,128)S(1)}, u32[]{:S(2)}, u32[]{:S(2)}) async-start(f32[32,16,128]{2,1,0:T(8,128)} %broadcast_in_dim.23), calls=%async_computation.3 | async-start | bytes 524288 | tf_op jit(solution)/shard_map/all_to_all | solution.py:627
  183.4 2.6 %shard_map.140.refs_0_ = f32[2,768,384]{2,1,0:T(8,128)} custom-call(s32[26]{0:T(128)S(1)} %pad_add_fusion.place, bf16[768,384]{1,0:T(8,128)(2,1)} %bitcast.15.value), custom_call_target="tpu_custom_call" | custom-call | flops 294912 | bytes 1769472 | tf_op jit(solution)/shard_map/pallas_call | solution.py:582
  186.0 7.0 %shard_map.139 = bf16[2,128,1536]{2,1,0:T(8,128)(2,1)} custom-call(s32[26]{0:T(128)S(1)} %pad_add_fusion.place, f32[32,1536]{1,0:T(8,128)S(1)} %copy-done.21, f32[3,1536]{1,0:T(4,128)S(1)} %pad_maximum_fusion.1.params, f32[2,128,1536]{2,1,0:T(8,128)S(1)} %copy-done.17, f32[2,128,1536]{2,1,0:T(8,128)S(1)} %copy-done.19, bf16[4,32,1536]{2,1,0:T(8,128)(2,1)S(1)} %copy-done.23), custom_call_target="tpu_custom_call" | custom-call | flops 30000000 | bytes 5000000 | tf_op jit(solution)/shard_map/pallas_call | solution.py:495
  193.7 1.6 shard_map.141
  (151 shorter events, 30.7 us)
Async XLA Ops:
  0.6 34.6 %copy-start.1 = (bf16[1536,384]{1,0:T(8,128)(2,1)S(1)}, bf16[1536,384]{1,0:T(8,128)(2,1)}, u32[]{:S(2)}) copy-start(bf16[1536,384]{1,0:T(8,128)(2,1)} %refs_0_.1) | copy-start | bytes 3538948
  0.6 34.6 %collective-permute-start.5 = (bf16[1536,384]{1,0:T(8,128)(2,1)}, bf16[1536,384]{1,0:T(8,128)(2,1)}, u32[]{:S(2)}, u32[]{:S(2)}) collective-permute-start(bf16[1536,384]{1,0:T(8,128)(2,1)} %refs_0_.1), channel_id=1, source_target_pairs={{0,1},{1,0},{2,3},{3,2},{4,5},{5,4},{6,7},{7,6},{8,9},{9,8},{10,11... | collective-permute-start | bytes 3538952 | tf_op jit(solution)/shard_map/ppermute | solution.py:604
  1.8 15.6 %collective-permute-start = (bf16[2,32,1536]{2,1,0:T(8,128)(2,1)S(1)}, bf16[2,32,1536]{2,1,0:T(8,128)(2,1)S(1)}, u32[]{:S(2)}, u32[]{:S(2)}) collective-permute-start(bf16[2,32,1536]{2,1,0:T(8,128)(2,1)S(1)} %slice.126), channel_id=1, source_target_pairs={{0,4},{4,8},{8,12},{12,16},{16,20},{20,24},{24,28},{28,32},{32,36}... | collective-permute-start | bytes 589832 | tf_op jit(solution)/shard_map/ppermute | solution.py:600
  24.7 1.3 collective-permute-start.1
  26.0 5.0 %collective-permute-start.2 = (f32[3,768]{1,0:T(4,128)S(1)}, f32[3,768]{1,0:T(4,128)S(1)}, u32[]{:S(2)}, u32[]{:S(2)}) collective-permute-start(f32[3,768]{1,0:T(4,128)S(1)} %shard_map.128.own), channel_id=1, source_target_pairs={{0,2},{1,3},{2,4},{3,5},{4,6},{5,7},{6,0},{7,1},{8,10},{9,11},{10,... | collective-permute-start | bytes 27656 | tf_op jit(solution)/shard_map/ppermute | solution.py:621
  26.6 4.3 %collective-permute-start.3 = (f32[3,768]{1,0:T(4,128)S(1)}, f32[3,768]{1,0:T(4,128)S(1)}, u32[]{:S(2)}, u32[]{:S(2)}) collective-permute-start(f32[3,768]{1,0:T(4,128)S(1)} %shard_map.128.own), channel_id=1, source_target_pairs={{0,6},{1,7},{2,0},{3,1},{4,2},{5,3},{6,4},{7,5},{8,14},{9,15},{10,... | collective-permute-start | bytes 27656 | tf_op jit(solution)/shard_map/ppermute | solution.py:621
  29.3 5.2 %collective-permute-start.4 = (f32[3,768]{1,0:T(4,128)S(1)}, f32[3,768]{1,0:T(4,128)S(1)}, u32[]{:S(2)}, u32[]{:S(2)}) collective-permute-start(f32[3,768]{1,0:T(4,128)S(1)} %shard_map.128.own), channel_id=1, source_target_pairs={{0,4},{1,5},{2,6},{3,7},{4,0},{5,1},{6,2},{7,3},{8,12},{9,13},{10,... | collective-permute-start | bytes 27656 | tf_op jit(solution)/shard_map/ppermute | solution.py:621
  36.4 22.9 %collective-permute-start.6 = (bf16[768,384]{1,0:T(8,128)(2,1)}, bf16[768,384]{1,0:T(8,128)(2,1)}, u32[]{:S(2)}, u32[]{:S(2)}) collective-permute-start(bf16[768,384]{1,0:T(8,128)(2,1)} %get-tuple-element.94), channel_id=1, source_target_pairs={{0,2},{1,3},{2,4},{3,5},{4,6},{5,7},{6,0},{7,1},{8,10},{9,11},{10,... | collective-permute-start | bytes 1769480 | tf_op jit(solution)/shard_map/ppermute | solution.py:621
  36.4 22.9 %collective-permute-start.7 = (bf16[768,384]{1,0:T(8,128)(2,1)}, bf16[768,384]{1,0:T(8,128)(2,1)}, u32[]{:S(2)}, u32[]{:S(2)}) collective-permute-start(bf16[768,384]{1,0:T(8,128)(2,1)} %get-tuple-element.93), channel_id=1, source_target_pairs={{0,6},{1,7},{2,0},{3,1},{4,2},{5,3},{6,4},{7,5},{8,14},{9,15},{10,... | collective-permute-start | bytes 1769480 | tf_op jit(solution)/shard_map/ppermute | solution.py:621
  39.6 19.7 %all-to-all-start = ((f32[32,16,128]{2,1,0:T(8,128)}), f32[32,16,128]{2,1,0:T(8,128)}, u32[]{:S(2)}, u32[]{:S(2)}) async-start(f32[32,16,128]{2,1,0:T(8,128)} %shard_map.129), calls=%async_computation | async-start | bytes 524288 | tf_op jit(solution)/shard_map/all_to_all | solution.py:627
  59.3 6.8 %collective-permute-start.10 = (bf16[768,384]{1,0:T(8,128)(2,1)}, bf16[768,384]{1,0:T(8,128)(2,1)S(1)}, u32[]{:S(2)}, u32[]{:S(2)}) collective-permute-start(bf16[768,384]{1,0:T(8,128)(2,1)} %collective-permute-done.6.refs_1_), channel_id=1, source_target_pairs={{0,1},{1,0},{2,3},{3,2},{4,5},{5,4},{6,7},{7,6},{8,9},{9,8},{10,11... | collective-permute-start | bytes 1769480 | tf_op jit(solution)/shard_map/ppermute | solution.py:604
  59.4 6.7 %collective-permute-start.11 = (bf16[768,384]{1,0:T(8,128)(2,1)}, bf16[768,384]{1,0:T(8,128)(2,1)S(1)}, u32[]{:S(2)}, u32[]{:S(2)}) collective-permute-start(bf16[768,384]{1,0:T(8,128)(2,1)} %collective-permute-done.7.refs_2_), channel_id=1, source_target_pairs={{0,1},{1,0},{2,3},{3,2},{4,5},{5,4},{6,7},{7,6},{8,9},{9,8},{10,11... | collective-permute-start | bytes 1769480 | tf_op jit(solution)/shard_map/ppermute | solution.py:604
  61.0 1.3 collective-permute-start.8
  66.1 3.4 %collective-permute-start.12 = (bf16[4,384,384]{2,1,0:T(8,128)(2,1)S(1)}, bf16[4,384,384]{2,1,0:T(8,128)(2,1)S(1)}, u32[]{:S(2)}, u32[]{:S(2)}) collective-permute-start(bf16[4,384,384]{2,1,0:T(8,128)(2,1)S(1)} %get-tuple-element.56), channel_id=1, source_target_pairs={{0,1},{1,0},{2,3},{3,2},{4,5},{5,4},{6,7},{7,6},{8,9},{9,8},{10,11... | collective-permute-start | bytes 3538952 | tf_op jit(solution)/shard_map/ppermute | solution.py:604
  66.4 5.6 %collective-permute-start.9 = (bf16[4,384,384]{2,1,0:T(8,128)(2,1)S(1)}, bf16[4,384,384]{2,1,0:T(8,128)(2,1)S(1)}, u32[]{:S(2)}, u32[]{:S(2)}) collective-permute-start(bf16[4,384,384]{2,1,0:T(8,128)(2,1)S(1)} %get-tuple-element.51), channel_id=1, source_target_pairs={{0,1},{1,0},{2,3},{3,2},{4,5},{5,4},{6,7},{7,6},{8,9},{9,8},{10,11... | collective-permute-start | bytes 3538952 | tf_op jit(solution)/shard_map/ppermute | solution.py:604
  69.8 15.4 %collective-permute-start.13 = (bf16[2,384,384]{2,1,0:T(8,128)(2,1)S(1)}, bf16[2,384,384]{2,1,0:T(8,128)(2,1)S(1)}, u32[]{:S(2)}, u32[]{:S(2)}) collective-permute-start(bf16[2,384,384]{2,1,0:T(8,128)(2,1)S(1)} %get-tuple-element.57), channel_id=1, source_target_pairs={{0,6},{1,7},{2,0},{3,1},{4,2},{5,3},{6,4},{7,5},{8,14},{9,15},{10,... | collective-permute-start | bytes 1769480 | tf_op jit(solution)/shard_map/ppermute | solution.py:621
  69.9 16.8 %collective-permute-start.14 = (bf16[2,384,384]{2,1,0:T(8,128)(2,1)S(1)}, bf16[2,384,384]{2,1,0:T(8,128)(2,1)S(1)}, u32[]{:S(2)}, u32[]{:S(2)}) collective-permute-start(bf16[2,384,384]{2,1,0:T(8,128)(2,1)S(1)} %get-tuple-element.58), channel_id=1, source_target_pairs={{0,2},{1,3},{2,4},{3,5},{4,6},{5,7},{6,0},{7,1},{8,10},{9,11},{10,... | collective-permute-start | bytes 1769480 | tf_op jit(solution)/shard_map/ppermute | solution.py:621
  87.1 3.4 %collective-permute-start.17 = (f32[2,2,72,384]{3,2,1,0:T(8,128)S(1)}, f32[2,2,72,384]{3,2,1,0:T(8,128)S(1)}, u32[]{:S(2)}, u32[]{:S(2)}) collective-permute-start(f32[2,2,72,384]{3,2,1,0:T(8,128)S(1)} %slice_bitcast_fusion), channel_id=1, source_target_pairs={{0,1},{1,0},{2,3},{3,2},{4,5},{5,4},{6,7},{7,6},{8,9},{9,8},{10,11... | collective-permute-start | bytes 1327112 | tf_op jit(solution)/shard_map/ppermute | solution.py:604
  87.2 15.4 %collective-permute-start.15 = (bf16[384,384]{1,0:T(8,128)(2,1)S(1)}, bf16[384,384]{1,0:T(8,128)(2,1)S(1)}, u32[]{:S(2)}, u32[]{:S(2)}) collective-permute-start(bf16[384,384]{1,0:T(8,128)(2,1)S(1)} %get-tuple-element.65), channel_id=1, source_target_pairs={{0,2},{1,3},{2,4},{3,5},{4,6},{5,7},{6,0},{7,1},{8,10},{9,11},{10,... | collective-permute-start | bytes 884744 | tf_op jit(solution)/shard_map/ppermute | solution.py:621
  87.5 15.1 %collective-permute-start.16 = (bf16[384,384]{1,0:T(8,128)(2,1)S(1)}, bf16[384,384]{1,0:T(8,128)(2,1)S(1)}, u32[]{:S(2)}, u32[]{:S(2)}) collective-permute-start(bf16[384,384]{1,0:T(8,128)(2,1)S(1)} %get-tuple-element.66), channel_id=1, source_target_pairs={{0,6},{1,7},{2,0},{3,1},{4,2},{5,3},{6,4},{7,5},{8,14},{9,15},{10,... | collective-permute-start | bytes 884744 | tf_op jit(solution)/shard_map/ppermute | solution.py:621
  90.6 11.2 %collective-permute-start.20 = (f32[72,384]{1,0:T(8,128)S(1)}, f32[72,384]{1,0:T(8,128)S(1)}, u32[]{:S(2)}, u32[]{:S(2)}) collective-permute-start(f32[72,384]{1,0:T(8,128)S(1)} %get-tuple-element.96), channel_id=1, source_target_pairs={{0,6},{1,7},{2,0},{3,1},{4,2},{5,3},{6,4},{7,5},{8,14},{9,15},{10,... | collective-permute-start | bytes 331784 | tf_op jit(solution)/shard_map/ppermute | solution.py:621
  90.7 11.1 %collective-permute-start.19 = (f32[72,384]{1,0:T(8,128)S(1)}, f32[72,384]{1,0:T(8,128)S(1)}, u32[]{:S(2)}, u32[]{:S(2)}) collective-permute-start(f32[72,384]{1,0:T(8,128)S(1)} %get-tuple-element.97), channel_id=1, source_target_pairs={{0,4},{1,5},{2,6},{3,7},{4,0},{5,1},{6,2},{7,3},{8,12},{9,13},{10,... | collective-permute-start | bytes 331784 | tf_op jit(solution)/shard_map/ppermute | solution.py:621
  91.8 10.8 %collective-permute-start.18 = (f32[72,384]{1,0:T(8,128)S(1)}, f32[72,384]{1,0:T(8,128)S(1)}, u32[]{:S(2)}, u32[]{:S(2)}) collective-permute-start(f32[72,384]{1,0:T(8,128)S(1)} %get-tuple-element.95), channel_id=1, source_target_pairs={{0,2},{1,3},{2,4},{3,5},{4,6},{5,7},{6,0},{7,1},{8,10},{9,11},{10,... | collective-permute-start | bytes 331784 | tf_op jit(solution)/shard_map/ppermute | solution.py:621
  104.3 30.4 %all-to-all-start.1 = ((bf16[32,32,384]{2,1,0:T(8,128)(2,1)}), bf16[32,32,384]{2,1,0:T(8,128)(2,1)S(1)}, u32[]{:S(2)}, u32[]{:S(2)}) async-start(bf16[32,32,384]{2,1,0:T(8,128)(2,1)} %shard_map.137), calls=%async_computation.1 | async-start | bytes 1572864 | tf_op jit(solution)/shard_map/all_to_all | solution.py:627
  134.8 24.0 %copy-start.6 = (bf16[256,1536]{1,0:T(8,128)(2,1)S(1)}, bf16[256,1536]{1,0:T(8,128)(2,1)}, u32[]{:S(2)}) copy-start(bf16[256,1536]{1,0:T(8,128)(2,1)} %copy-done.5) | copy-start | bytes 2359300
  135.4 10.9 %collective-permute-start.22 = (f32[3,384]{1,0:T(4,128)}, f32[3,384]{1,0:T(4,128)}, u32[]{:S(2)}, u32[]{:S(2)}) collective-permute-start(f32[3,384]{1,0:T(4,128)} %slice_add_fusion.4), channel_id=1, source_target_pairs={{0,4},{4,0},{8,12},{12,8},{16,20},{20,16},{24,28},{28,24},{32,36},... | collective-permute-start | bytes 13832 | tf_op jit(solution)/shard_map/ppermute | solution.py:612
  139.1 28.3 %all-to-all-start.2 = ((bf16[32,24,384]{2,1,0:T(8,128)(2,1)}), bf16[32,24,384]{2,1,0:T(8,128)(2,1)}, u32[]{:S(2)}, u32[]{:S(2)}) async-start(bf16[32,24,384]{2,1,0:T(8,128)(2,1)} %broadcast_in_dim.20), calls=%async_computation.2 | async-start | bytes 1179648 | tf_op jit(solution)/shard_map/all_to_all | solution.py:627
  148.6 8.2 %collective-permute-start.23 = (f32[3,384]{1,0:T(4,128)}, f32[3,384]{1,0:T(4,128)}, u32[]{:S(2)}, u32[]{:S(2)}) collective-permute-start(f32[3,384]{1,0:T(4,128)} %pad_maximum_fusion.3), channel_id=1, source_target_pairs={{0,1},{1,0},{2,3},{3,2},{4,5},{5,4},{6,7},{7,6},{8,9},{9,8},{10,11... | collective-permute-start | bytes 13832 | tf_op jit(solution)/shard_map/ppermute | solution.py:604
  148.6 18.0 %collective-permute-start.21 = (bf16[4,32,1536]{2,1,0:T(8,128)(2,1)S(1)}, bf16[4,32,1536]{2,1,0:T(8,128)(2,1)S(1)}, u32[]{:S(2)}, u32[]{:S(2)}) collective-permute-start(bf16[4,32,1536]{2,1,0:T(8,128)(2,1)S(1)} %get-tuple-element.70), channel_id=1, source_target_pairs={{4,0},{8,4},{12,8},{16,12},{20,16},{24,20},{28,24},{32,28},{36,32}... | collective-permute-start | bytes 1179656 | tf_op jit(solution)/shard_map/ppermute | solution.py:600
  157.6 5.5 %collective-permute-start.24 = (f32[2,3,384]{2,0,1:T(2,128)S(1)}, f32[2,3,384]{2,0,1:T(2,128)S(1)}, u32[]{:S(2)}, u32[]{:S(2)}) collective-permute-start(f32[2,3,384]{2,0,1:T(2,128)S(1)} %maximum_select_fusion.2), channel_id=1, source_target_pairs={{0,2},{2,0},{1,3},{3,1},{4,6},{6,4},{5,7},{7,5},{8,10},{10,8},{9,1... | collective-permute-start | bytes 27656 | tf_op jit(solution)/shard_map/ppermute | solution.py:608
  167.4 26.3 %collective-permute-start.25 = (bf16[768,384]{1,0:T(8,128)(2,1)}, bf16[768,384]{1,0:T(8,128)(2,1)S(1)}, u32[]{:S(2)}, u32[]{:S(2)}) collective-permute-start(bf16[768,384]{1,0:T(8,128)(2,1)} %bitcast.15.value), channel_id=1, source_target_pairs={{0,4},{4,0},{8,12},{12,8},{16,20},{20,16},{24,28},{28,24},{32,36},... | collective-permute-start | bytes 1769480 | tf_op jit(solution)/shard_map/ppermute | solution.py:612
  173.1 19.8 %all-to-all-start.3 = ((f32[32,16,128]{2,1,0:T(8,128)}), f32[32,16,128]{2,1,0:T(8,128)S(1)}, u32[]{:S(2)}, u32[]{:S(2)}) async-start(f32[32,16,128]{2,1,0:T(8,128)} %broadcast_in_dim.23), calls=%async_computation.3 | async-start | bytes 524288 | tf_op jit(solution)/shard_map/all_to_all | solution.py:627
  (28 other events, 196.0 us)
